TPU v7x, 32 devices: a whole 2x2x4 slice. The times are simulated.
32 devices in a mesh: seq: 16 (over z, y, x), head: 2 (over core).
Axes of the slice: x: 2, y: 2, z: 4, core: 2. Of those that a mesh axis runs over, the one named last changes fastest.
Arguments:
- ssm_input: bfloat16 [4096, 2048], P('seq', 'head'), may hold values from -6 to 6
- bc_input: bfloat16 [4096, 512], P('seq', 'head'), may hold values from -4 to 4
- conv_taps: float32 [4, 2048], P(None, 'head'), may hold values from -3 to 3
- conv_bias: float32 [2048], P('head'), may hold values from -1 to 0
- bc_taps: float32 [4, 512], P(None, 'head'), may hold values from -3 to 3
- bc_bias: float32 [512], P('head'), may hold values from -0.6 to 0.35
- step_input: float32 [32, 4096], P('head', 'seq'), may hold values from -4 to 4
- step_bias: float32 [32], P('head'), may hold values from -8 to -2
- decay_log: float32 [32], P('head'), may hold values from -8 to -1
- skip_gain: float32 [32], P('head'), may hold values from 0.5 to 2
- request_offset: int32 [4096], P('seq'), may hold values from 0 to 2047, as said below
Outputs:
- ssm_output: bfloat16 [4096, 2048], P('seq', 'head')
Inputs may be any that keep to these rules, and one draw needn't show every extreme that they name: request_offset counts the earlier tokens of the token's request: 0 at the first token and wherever a request starts, else one more than at the token before; one request has exactly 2048 tokens and none has more.
All inputs are finite; a program needn't handle non-finite values.
Results may differ from a plain program's by a relative error of at most 0.0095.
Values may be sent and summed in bfloat16 or wider, within the bound.
No kernel may reach another device: no remote copies, remote signals or barrier semaphores. Data moves between devices by JAX's collectives and lax.ppermute only.
A program may use at most 192 MiB of HBM per device.

v0:
```python
import jax
import jax.numpy as jnp
from jax import lax
from jax.sharding import PartitionSpec as P

HEADDIM = 64
BLOCK = 256


def passed_along(block, axis, distance):
    devices = range(lax.axis_size(axis))
    route = [(i - distance, i) for i in devices if i - distance in devices]
    return lax.ppermute(block, axis, route)


def from_partner(array, axis, stride):
    return lax.ppermute(array, axis, [(i, i ^ 1 << stride) for i in range(lax.axis_size(axis))])


def prefix(value, axis, join, neutral):
    count, mine = (lax.axis_size(axis), lax.axis_index(axis))
    pieces = jax.tree.map(lambda part: lax.all_gather(part, axis), value)
    total = jax.tree.map(
        lambda part, zero: jnp.full_like(part, 0) + jnp.asarray(zero, part.dtype), value, neutral
    )

    def hop(position, total):
        longer = join(total, jax.tree.map(lambda part: part[position], pieces))
        return jax.tree.map(lambda new, old: jnp.where(position < mine, new, old), longer, total)

    return lax.fori_loop(0, count - 1, hop, total)


def conv_silu(source, earlier, tap_weights, tap_bias, offset):
    tok_rows = source.shape[0]
    tap_count = tap_weights.shape[0]
    extended = jnp.concatenate([earlier, source], axis=0)
    summed = jnp.zeros(source.shape, jnp.float32) + tap_bias[None, :]
    for lag_steps in range(tap_count):
        first_row = tap_count - 1 - lag_steps
        shifted = extended[first_row : first_row + tok_rows].astype(jnp.float32)
        in_request = (offset >= lag_steps).astype(jnp.float32)[:, None]
        summed = summed + tap_weights[tap_count - 1 - lag_steps][None, :] * shifted * in_request
    return jax.nn.silu(summed).astype(jnp.bfloat16)


def block_terms(x_block, b_block, c_block, step_block, decay_block, offset_block):
    block_len = offset_block.shape[0]
    rate_sum = jnp.cumsum(decay_block, axis=1)
    positions = lax.iota(jnp.int32, block_len)
    linked = (positions[None, :] <= positions[:, None]) & (
        offset_block[:, None] >= positions[:, None] - positions[None, :]
    )
    scores = jnp.einsum("in,jn->ij", c_block, b_block, preferred_element_type=jnp.float32)
    rate_gap = jnp.where(linked[None], rate_sum[:, :, None] - rate_sum[:, None, :], -1e30)
    weights = (scores[None] * jnp.exp(rate_gap) * step_block[:, None, :]).astype(jnp.bfloat16)
    intra_part = jnp.einsum("hij,jhp->ihp", weights, x_block, preferred_element_type=jnp.float32)
    tail_gap = jnp.where(
        offset_block[-1] >= block_len - 1 - positions[None, :], rate_sum[:, -1:] - rate_sum, -1e30
    )
    weighted_b = (
        b_block[None].astype(jnp.float32) * (jnp.exp(tail_gap) * step_block)[:, :, None]
    ).astype(jnp.bfloat16)
    block_state = jnp.einsum(
        "hjn,jhp->hnp", weighted_b, x_block, preferred_element_type=jnp.float32
    )
    carry_scale = jnp.exp(rate_sum) * (offset_block >= positions + 1).astype(jnp.float32)[None, :]
    passing = jnp.exp(rate_sum[:, -1]) * (offset_block[-1] >= block_len).astype(jnp.float32)
    return (intra_part, block_state, carry_scale, passing)


def state_read(c_float, state_value):
    return jnp.einsum("in,hnp->ihp", c_float, state_value, precision=lax.Precision.HIGHEST)


def combine(earlier, latter):
    return (earlier[0] * latter[0], latter[0][:, None, None] * earlier[1] + latter[1])


def on_device(
    ssm_input,
    bc_input,
    conv_taps,
    conv_bias,
    bc_taps,
    bc_bias,
    step_input,
    step_bias,
    decay_log,
    skip_gain,
    request_offset,
):
    tok_rows = ssm_input.shape[0]
    tap_count = conv_taps.shape[0]
    head_count = step_input.shape[0]
    state_size = bc_input.shape[1]
    earlier_x, earlier_bc = passed_along(
        (ssm_input[tok_rows - tap_count + 1 :], bc_input[tok_rows - tap_count + 1 :]), "seq", 1
    )
    x_conv = conv_silu(ssm_input, earlier_x, conv_taps, conv_bias, request_offset)
    own_half = conv_silu(bc_input, earlier_bc, bc_taps, bc_bias, request_offset)
    partner = from_partner(own_half, "head", 0)
    is_even = lax.axis_index("head") % 2 == 0
    b_rows = jnp.where(is_even, own_half, partner)
    c_rows = jnp.where(is_even, partner, own_half)
    time_step = jax.nn.softplus(step_input + step_bias[:, None])
    log_decay = -jnp.exp(decay_log)[:, None] * time_step
    block_count = tok_rows // BLOCK
    x_blocks = x_conv.reshape(block_count, BLOCK, head_count, HEADDIM)
    block_number = 0
    pieces = [
        block_terms(x_blocks[block_number], b_rows, c_rows, time_step, log_decay, request_offset)
    ]
    run_state = jnp.zeros((head_count, state_size, HEADDIM), jnp.float32)
    decay_prefix = jnp.ones((head_count,), jnp.float32)
    intra_part, block_state, carry_scale, passing = pieces[0]
    entering = [run_state]
    before = [decay_prefix]
    run_state = passing[:, None, None] * run_state + block_state
    decay_prefix = decay_prefix * passing
    identity = (jnp.ones_like(decay_prefix), jnp.zeros_like(run_state))
    totals, carry_in = prefix((decay_prefix, run_state), "seq", combine, identity)
    block_number = 0
    intra_part, block_state, carry_scale, passing = pieces[block_number]
    c_float = c_rows.astype(jnp.float32)
    x_float = x_blocks[block_number].astype(jnp.float32)
    incoming = before[block_number][:, None, None] * carry_in
    inter_part = state_read(c_float, entering[block_number] + incoming)
    block_out = (
        intra_part + inter_part * carry_scale.T[:, :, None] + skip_gain[None, :, None] * x_float
    )
    outputs = block_out.reshape(BLOCK, head_count * HEADDIM).astype(jnp.bfloat16)
    return outputs


def solution(mesh):
    return jax.shard_map(
        on_device,
        mesh=mesh,
        in_specs=(
            P("seq", "head"),
            P("seq", "head"),
            P(None, "head"),
            P("head"),
            P(None, "head"),
            P("head"),
            P("head", "seq"),
            P("head"),
            P("head"),
            P("head"),
            P("seq"),
        ),
        out_specs=P("seq", "head"),
        check_vma=False,
    )
```

profile of v0, /device:TPU:24, one launch (start us, length us, event | category | flops | bytes accessed | tf_op | source)
XLA Modules:
  0.0 309.2 jit_solution(7965363464001770051)
XLA Ops:
  7.2 3.4 %collective-permute-start.1 = (bf16[3,256]{1,0:T(4,128)(2,1)S(1)}, bf16[3,256]{1,0:T(4,128)(2,1)S(1)}, u32[]{:S(2)}, u32[]{:S(2)}) collective-permute-start(bf16[3,256]{1,0:T(4,128)(2,1)S(1)} %slice.72), channel_id=1, source_target_pairs={{0,2},{2,4},{4,6},{6,8},{8,10},{10,12},{12,14},{14,16},{16,18},{18... | collective-permute-start | bytes 4616 | tf_op jit(solution)/shard_map/ppermute | solution.py:13
  11.4 3.4 %collective-permute-start = (bf16[3,1024]{1,0:T(4,128)(2,1)S(1)}, bf16[3,1024]{1,0:T(4,128)(2,1)S(1)}, u32[]{:S(2)}, u32[]{:S(2)}) collective-permute-start(bf16[3,1024]{1,0:T(4,128)(2,1)S(1)} %slice.64), channel_id=1, source_target_pairs={{0,2},{2,4},{4,6},{6,8},{8,10},{10,12},{12,14},{14,16},{16,18},{18... | collective-permute-start | bytes 18440 | tf_op jit(solution)/shard_map/ppermute | solution.py:13
  22.4 1.5 multiply_convert_fusion.9
  24.0 3.0 multiply_convert_fusion.8
  27.3 1.9 fusion.11
  30.7 33.2 %all-reduce = f32[256]{0:T(256)S(1)} all-reduce(f32[256]{0:T(256)S(1)} %dynamic-update-slice), channel_id=2, replica_groups=mesh['seq'=16,'head'=2] {'seq'}, use_global_device_ids=true, to_apply=%add | all-reduce | flops 256 | bytes 2048
  65.0 154.7 %all-gather.4.cloned.1.call-done = f32[256,256,64]{1,2,0:T(8,128)} async-done(((f32[16,256,64]{1,2,0:T(8,128)}), f32[256,256,64]{1,2,0:T(8,128)}) %all-gather.4.cloned.1.call-update) | async-done | bytes 16777232 | tf_op jit(solution)/shard_map/all_gather | solution.py:22
  219.7 77.2 %while.14 = (s32[]{:T(128)}, f32[16,256,64]{2,1,0:T(8,128)}, s32[]{:T(128)}, f32[16,16]{1,0:T(8,128)S(1)}, f32[16,16,256,64]{2,3,1,0:T(8,128)}, /*index=5*/s32[]{:T(128)}, s32[]{:T(128)}) while((s32[]{:T(128)}, f32[16,256,64]{2,1,0:T(8,128)}, s32[]{:T(128)}, f32[16,16]{1,0:T(8,128)S(1)}, f32[16,16,256,64]{2,3,1,0:T(8,128)}, ...), condition=%wide.region_3.4_spmd.clone, body=%wide.region_2.3_spmd.clone.sunk | while | flops 1048580 | bytes 7340329 | solution.py:31
  219.7 1.3 constant_dynamic-slice_fusion.2
  221.6 1.7 fusion.28
  223.3 1.3 constant_dynamic-slice_fusion.2
  225.3 3.3 %fusion.28 = f32[16,256,64]{2,1,0:T(8,128)} fusion(f32[1,16,256,64]{3,2,1,0:T(8,128)S(1)} %copy.40, f32[16,256,64]{2,1,0:T(8,128)} %get-tuple-element.201, f32[16]{0:T(128)S(1)} %dynamic-slice_bitcast_fusion.2, pred[]{:T(512)S(6)} %compare.4, pred[]{:T(512)S(6)} %lt.29), kind=kLoop, calls=%fused_computation.1.clone.1 | loop fusion | flops 1048576 | bytes 3145794 | tf_op jit(solution)/shard_map/while/body/eval_jaxpr/jit(_where)/select_n | solution.py:29
  228.6 1.3 constant_dynamic-slice_fusion.2
  230.6 3.3 %fusion.28 = f32[16,256,64]{2,1,0:T(8,128)} fusion(f32[1,16,256,64]{3,2,1,0:T(8,128)S(1)} %copy.40, f32[16,256,64]{2,1,0:T(8,128)} %get-tuple-element.201, f32[16]{0:T(128)S(1)} %dynamic-slice_bitcast_fusion.2, pred[]{:T(512)S(6)} %compare.4, pred[]{:T(512)S(6)} %lt.29), kind=kLoop, calls=%fused_computation.1.clone.1 | loop fusion | flops 1048576 | bytes 3145794 | tf_op jit(solution)/shard_map/while/body/eval_jaxpr/jit(_where)/select_n | solution.py:29
  233.9 1.3 constant_dynamic-slice_fusion.2
  235.8 3.3 %fusion.28 = f32[16,256,64]{2,1,0:T(8,128)} fusion(f32[1,16,256,64]{3,2,1,0:T(8,128)S(1)} %copy.40, f32[16,256,64]{2,1,0:T(8,128)} %get-tuple-element.201, f32[16]{0:T(128)S(1)} %dynamic-slice_bitcast_fusion.2, pred[]{:T(512)S(6)} %compare.4, pred[]{:T(512)S(6)} %lt.29), kind=kLoop, calls=%fused_computation.1.clone.1 | loop fusion | flops 1048576 | bytes 3145794 | tf_op jit(solution)/shard_map/while/body/eval_jaxpr/jit(_where)/select_n | solution.py:29
  241.1 3.3 %fusion.28 = f32[16,256,64]{2,1,0:T(8,128)} fusion(f32[1,16,256,64]{3,2,1,0:T(8,128)S(1)} %copy.40, f32[16,256,64]{2,1,0:T(8,128)} %get-tuple-element.201, f32[16]{0:T(128)S(1)} %dynamic-slice_bitcast_fusion.2, pred[]{:T(512)S(6)} %compare.4, pred[]{:T(512)S(6)} %lt.29), kind=kLoop, calls=%fused_computation.1.clone.1 | loop fusion | flops 1048576 | bytes 3145794 | tf_op jit(solution)/shard_map/while/body/eval_jaxpr/jit(_where)/select_n | solution.py:29
  244.4 1.3 constant_dynamic-slice_fusion.2
  246.3 3.3 %fusion.28 = f32[16,256,64]{2,1,0:T(8,128)} fusion(f32[1,16,256,64]{3,2,1,0:T(8,128)S(1)} %copy.40, f32[16,256,64]{2,1,0:T(8,128)} %get-tuple-element.201, f32[16]{0:T(128)S(1)} %dynamic-slice_bitcast_fusion.2, pred[]{:T(512)S(6)} %compare.4, pred[]{:T(512)S(6)} %lt.29), kind=kLoop, calls=%fused_computation.1.clone.1 | loop fusion | flops 1048576 | bytes 3145794 | tf_op jit(solution)/shard_map/while/body/eval_jaxpr/jit(_where)/select_n | solution.py:29
  249.6 1.3 constant_dynamic-slice_fusion.2
  251.6 3.3 %fusion.28 = f32[16,256,64]{2,1,0:T(8,128)} fusion(f32[1,16,256,64]{3,2,1,0:T(8,128)S(1)} %copy.40, f32[16,256,64]{2,1,0:T(8,128)} %get-tuple-element.201, f32[16]{0:T(128)S(1)} %dynamic-slice_bitcast_fusion.2, pred[]{:T(512)S(6)} %compare.4, pred[]{:T(512)S(6)} %lt.29), kind=kLoop, calls=%fused_computation.1.clone.1 | loop fusion | flops 1048576 | bytes 3145794 | tf_op jit(solution)/shard_map/while/body/eval_jaxpr/jit(_where)/select_n | solution.py:29
  254.9 1.3 constant_dynamic-slice_fusion.2
  256.8 3.3 %fusion.28 = f32[16,256,64]{2,1,0:T(8,128)} fusion(f32[1,16,256,64]{3,2,1,0:T(8,128)S(1)} %copy.40, f32[16,256,64]{2,1,0:T(8,128)} %get-tuple-element.201, f32[16]{0:T(128)S(1)} %dynamic-slice_bitcast_fusion.2, pred[]{:T(512)S(6)} %compare.4, pred[]{:T(512)S(6)} %lt.29), kind=kLoop, calls=%fused_computation.1.clone.1 | loop fusion | flops 1048576 | bytes 3145794 | tf_op jit(solution)/shard_map/while/body/eval_jaxpr/jit(_where)/select_n | solution.py:29
  262.1 3.3 %fusion.28 = f32[16,256,64]{2,1,0:T(8,128)} fusion(f32[1,16,256,64]{3,2,1,0:T(8,128)S(1)} %copy.40, f32[16,256,64]{2,1,0:T(8,128)} %get-tuple-element.201, f32[16]{0:T(128)S(1)} %dynamic-slice_bitcast_fusion.2, pred[]{:T(512)S(6)} %compare.4, pred[]{:T(512)S(6)} %lt.29), kind=kLoop, calls=%fused_computation.1.clone.1 | loop fusion | flops 1048576 | bytes 3145794 | tf_op jit(solution)/shard_map/while/body/eval_jaxpr/jit(_where)/select_n | solution.py:29
  267.3 3.3 %fusion.28 = f32[16,256,64]{2,1,0:T(8,128)} fusion(f32[1,16,256,64]{3,2,1,0:T(8,128)S(1)} %copy.40, f32[16,256,64]{2,1,0:T(8,128)} %get-tuple-element.201, f32[16]{0:T(128)S(1)} %dynamic-slice_bitcast_fusion.2, pred[]{:T(512)S(6)} %compare.4, pred[]{:T(512)S(6)} %lt.29), kind=kLoop, calls=%fused_computation.1.clone.1 | loop fusion | flops 1048576 | bytes 3145794 | tf_op jit(solution)/shard_map/while/body/eval_jaxpr/jit(_where)/select_n | solution.py:29
  272.6 3.3 %fusion.28 = f32[16,256,64]{2,1,0:T(8,128)} fusion(f32[1,16,256,64]{3,2,1,0:T(8,128)S(1)} %copy.40, f32[16,256,64]{2,1,0:T(8,128)} %get-tuple-element.201, f32[16]{0:T(128)S(1)} %dynamic-slice_bitcast_fusion.2, pred[]{:T(512)S(6)} %compare.4, pred[]{:T(512)S(6)} %lt.29), kind=kLoop, calls=%fused_computation.1.clone.1 | loop fusion | flops 1048576 | bytes 3145794 | tf_op jit(solution)/shard_map/while/body/eval_jaxpr/jit(_where)/select_n | solution.py:29
  277.8 3.3 %fusion.28 = f32[16,256,64]{2,1,0:T(8,128)} fusion(f32[1,16,256,64]{3,2,1,0:T(8,128)S(1)} %copy.40, f32[16,256,64]{2,1,0:T(8,128)} %get-tuple-element.201, f32[16]{0:T(128)S(1)} %dynamic-slice_bitcast_fusion.2, pred[]{:T(512)S(6)} %compare.4, pred[]{:T(512)S(6)} %lt.29), kind=kLoop, calls=%fused_computation.1.clone.1 | loop fusion | flops 1048576 | bytes 3145794 | tf_op jit(solution)/shard_map/while/body/eval_jaxpr/jit(_where)/select_n | solution.py:29
  283.1 3.3 %fusion.28 = f32[16,256,64]{2,1,0:T(8,128)} fusion(f32[1,16,256,64]{3,2,1,0:T(8,128)S(1)} %copy.40, f32[16,256,64]{2,1,0:T(8,128)} %get-tuple-element.201, f32[16]{0:T(128)S(1)} %dynamic-slice_bitcast_fusion.2, pred[]{:T(512)S(6)} %compare.4, pred[]{:T(512)S(6)} %lt.29), kind=kLoop, calls=%fused_computation.1.clone.1 | loop fusion | flops 1048576 | bytes 3145794 | tf_op jit(solution)/shard_map/while/body/eval_jaxpr/jit(_where)/select_n | solution.py:29
  288.3 3.3 %fusion.28 = f32[16,256,64]{2,1,0:T(8,128)} fusion(f32[1,16,256,64]{3,2,1,0:T(8,128)S(1)} %copy.40, f32[16,256,64]{2,1,0:T(8,128)} %get-tuple-element.201, f32[16]{0:T(128)S(1)} %dynamic-slice_bitcast_fusion.2, pred[]{:T(512)S(6)} %compare.4, pred[]{:T(512)S(6)} %lt.29), kind=kLoop, calls=%fused_computation.1.clone.1 | loop fusion | flops 1048576 | bytes 3145794 | tf_op jit(solution)/shard_map/while/body/eval_jaxpr/jit(_where)/select_n | solution.py:29
  293.6 3.3 %fusion.28 = f32[16,256,64]{2,1,0:T(8,128)} fusion(f32[1,16,256,64]{3,2,1,0:T(8,128)S(1)} %copy.40, f32[16,256,64]{2,1,0:T(8,128)} %get-tuple-element.201, f32[16]{0:T(128)S(1)} %dynamic-slice_bitcast_fusion.2, pred[]{:T(512)S(6)} %compare.4, pred[]{:T(512)S(6)} %lt.29), kind=kLoop, calls=%fused_computation.1.clone.1 | loop fusion | flops 1048576 | bytes 3145794 | tf_op jit(solution)/shard_map/while/body/eval_jaxpr/jit(_where)/select_n | solution.py:29
  296.9 2.2 copy.27
  299.8 1.6 add_convert_fusion
  (85 shorter events, 32.0 us)
Async XLA Ops:
  6.5 213.1 %all-gather.4.cloned.1.call-start = ((), (), s32[]{:S(2)}) async-start(), calls=%async_computation | async-start | bytes 17825792 | tf_op jit(solution)/shard_map/all_gather | solution.py:22
  7.2 15.2 %collective-permute-start.1 = (bf16[3,256]{1,0:T(4,128)(2,1)S(1)}, bf16[3,256]{1,0:T(4,128)(2,1)S(1)}, u32[]{:S(2)}, u32[]{:S(2)}) collective-permute-start(bf16[3,256]{1,0:T(4,128)(2,1)S(1)} %slice.72), channel_id=1, source_target_pairs={{0,2},{2,4},{4,6},{6,8},{8,10},{10,12},{12,14},{14,16},{16,18},{18... | collective-permute-start | bytes 4616 | tf_op jit(solution)/shard_map/ppermute | solution.py:13
  11.4 12.6 %collective-permute-start = (bf16[3,1024]{1,0:T(4,128)(2,1)S(1)}, bf16[3,1024]{1,0:T(4,128)(2,1)S(1)}, u32[]{:S(2)}, u32[]{:S(2)}) collective-permute-start(bf16[3,1024]{1,0:T(4,128)(2,1)S(1)} %slice.64), channel_id=1, source_target_pairs={{0,2},{2,4},{4,6},{6,8},{8,10},{10,12},{12,14},{14,16},{16,18},{18... | collective-permute-start | bytes 18440 | tf_op jit(solution)/shard_map/ppermute | solution.py:13
  23.9 3.4 %collective-permute-start.2 = (bf16[256,256]{1,0:T(8,128)(2,1)S(1)}, bf16[256,256]{1,0:T(8,128)(2,1)S(1)}, u32[]{:S(2)}, u32[]{:S(2)}) collective-permute-start(bf16[256,256]{1,0:T(8,128)(2,1)S(1)} %multiply_convert_fusion.9), channel_id=1, source_target_pairs={{0,1},{1,0},{2,3},{3,2},{4,5},{5,4},{6,7},{7,6},{8,9},{9,8},{10,11... | collective-permute-start | bytes 393224 | tf_op jit(solution)/shard_map/ppermute | solution.py:17
  27.2 37.7 %copy-start = (bf16[256,1024]{0,1:T(8,128)(2,1)}, bf16[256,1024]{0,1:T(8,128)(2,1)S(1)}, u32[]{:S(2)}) copy-start(bf16[256,1024]{0,1:T(8,128)(2,1)S(1)} %copy.23) | copy-start | bytes 1572868
  27.3 2.0 copy-start.5
  27.3 36.7 %copy-start.3 = (s32[256]{0:T(256)S(1)}, s32[256]{0:T(256)}, u32[]{:S(2)}) copy-start(s32[256]{0:T(256)} %param.23) | copy-start | bytes 3076
  296.9 2.9 copy-start.1
  296.9 2.9 copy-start.2
  296.9 2.9 copy-start.4
Sparse Core Ops, SparseCore 0:
  29.3 190.2 all-gather.3
where the time goes:
time: 315 us; the launch traced here: 309 us
  waiting for transfers between devices  155 us (49%)
  other arithmetic  56.3 us (18%)
  local copies, waits for them, and re-layouts  37.9 us (12%)
  blocking collectives  33.2 us (11%)
  between operations  14.9 us (5%)
  starting transfers between devices  6.85 us (2%)
  matrix products  5 us (2%)
    all_gather x1, waiting for transfers between devices, prefix(): pieces = jax.tree.map(lambda part: lax.all_gather(part, axis), value)  155 us
    select_n x15, other arithmetic, hop(): jnp.where(position < mine, new, old)  47.8 us
    unnamed x1, blocking collectives  33.2 us
    dynamic_slice x30, local copies, waits for them, and re-layouts, hop(): longer = join(total, jax.tree.map(lambda part: part[position], pieces))  28.8 us
    ppermute x2, starting transfers between devices, passed_along(): return lax.ppermute(block, axis, route)  6.77 us
  transfers between devices with their start and end apart: 4, of which 1 were waited for; matrix products, arithmetic and copies ran while one was open for 5% of the time, Pallas kernels for 0%

commit v1 on v0

v1 whole, which is shorter than its diff:
```python
import functools

import jax
import jax.numpy as jnp
from jax import lax
from jax.experimental import pallas as pl
from jax.experimental.pallas import tpu as pltpu
from jax.sharding import PartitionSpec as P

HEADDIM = 64
BLOCK = 256
GROUP = 4
PAD = 16
HALO = 16
LANES = 128
NEG = -1e30
F32 = jnp.float32
BF16 = jnp.bfloat16
SMALL = pltpu.CompilerParams(vmem_limit_bytes=24 * 1024 * 1024)


def dot(a, b, dims=((1,), (0,))):
    return lax.dot_general(a, b, (dims, ((), ())), preferred_element_type=F32)


def exact_dot(a, b, dims=((1,), (0,))):
    return lax.dot_general(
        a, b, (dims, ((), ())), preferred_element_type=F32, precision=lax.Precision.HIGHEST
    )


def two_parts(value):
    high = value.astype(BF16)
    return high, (value - high.astype(F32)).astype(BF16)


def silu(v):
    return 0.5 * v * (1.0 + jnp.tanh(0.5 * v))


def spread(per_head, first_channel, width):
    heads = per_head.shape[1]
    head = lax.broadcasted_iota(jnp.int32, (heads, width), 0)
    channel = lax.broadcasted_iota(jnp.int32, (heads, width), 1) + first_channel
    member = (channel // HEADDIM == head).astype(BF16)
    high, low = two_parts(per_head)
    return dot(high, member) + dot(low, member)


def rates(step, step_bias, decay_log):
    block = step.shape[1]
    time_step = jax.nn.softplus(step + step_bias)
    log_decay = -jnp.exp(decay_log) * time_step
    row = lax.broadcasted_iota(jnp.int32, (block, block), 0)
    column = lax.broadcasted_iota(jnp.int32, (block, block), 1)
    return time_step, exact_dot(log_decay, (row <= column).astype(F32))


def offset_columns(offset_row):
    wide = jnp.broadcast_to(offset_row.astype(F32), (LANES, offset_row.shape[1]))
    return wide.T


def convolve(ext, source, halo, taps, bias, masks, store):
    rows, width = source.shape
    count = taps.shape[0]
    ext[0:8, 0:width] = halo[HALO - 8 : HALO, :].astype(F32)
    ext[8 : 8 + rows, 0:width] = source[...].astype(F32)
    step = 64
    for lane in range(0, width, LANES):
        cols = slice(lane, lane + LANES)
        tap_rows = [taps[k : k + 1, cols] for k in range(count)]
        for top in range(0, rows, step):
            total = tap_rows[count - 1] * ext[8 + top : 8 + top + step, cols] + bias[:, cols]
            for lag in range(1, count):
                shifted = ext[8 - lag + top : 8 - lag + top + step, cols]
                total = total + tap_rows[count - 1 - lag] * shifted * masks[lag - 1, top : top + step, :]
            store(top, step, cols, silu(total))


def front_kernel(
    place, x, own, other, halo_x, halo_own, halo_other, taps, bias, own_taps, other_taps,
    step, step_bias, decay_log, offset, x_out, b_out, c_out, s0, s1, s2, s3, ext, masks, gates,
):
    member = place[0]
    first = place[1] == 0
    block = x.shape[0]
    offset_col = offset_columns(offset[...])
    for lag in range(1, taps.shape[0]):
        masks[lag - 1] = (offset_col >= lag).astype(F32)
    count = taps.shape[0]

    def to_b(top, size, cols, value):
        b_out[top : top + size, cols] = value.astype(BF16)

    def to_c(top, size, cols, value):
        c_out[top : top + size, cols] = value.astype(BF16)

    def pick(a, b, shape):
        return jnp.where(first, a[...], b[...]) if shape is None else jnp.where(first, a, b)

    own_t, other_t = own_taps[...], other_taps[...]
    b_t, c_t = jnp.where(first, own_t, other_t), jnp.where(first, other_t, own_t)
    own_v, other_v = own[...].astype(F32), other[...].astype(F32)
    own_h, other_h = halo_own[...].astype(F32), halo_other[...].astype(F32)
    convolve(
        ext, jnp.where(first, own_v, other_v), jnp.where(first, own_h, other_h),
        b_t[0:count], b_t[count : count + 1], masks, to_b,
    )
    convolve(
        ext, jnp.where(first, other_v, own_v), jnp.where(first, other_h, own_h),
        c_t[0:count], c_t[count : count + 1], masks, to_c,
    )
    time_step, rate_sum = rates(step[...], step_bias[...], decay_log[...])
    last_offset = offset[0, block - 1]
    behind = block - 1 - lax.broadcasted_iota(jnp.int32, rate_sum.shape, 1)
    last = rate_sum[:, block - 1 : block]
    gate = jnp.exp(jnp.where(last_offset >= behind, last - rate_sum, NEG)) * time_step
    gates[...] = gate.T
    passing = jnp.exp(last) * (last_offset >= block).astype(F32)
    passing_rows = jnp.broadcast_to(passing, (passing.shape[0], LANES)).T[0:8, :]

    def to_x(top, size, cols, value):
        x_out[top : top + size, cols] = value.astype(BF16)

    convolve(ext, x, halo_x, taps, bias, masks, to_x)
    slices = (s0, s1, s2, s3)
    width = x.shape[1] // len(slices)
    b_rows = b_out[...]
    for k, out in enumerate(slices):
        channel = pl.multiple_of((member ^ k) * width, width)
        scale = spread(gates[...], channel, width)
        scaled = (x_out[:, pl.ds(channel, width)].astype(F32) * scale).astype(BF16)
        state = dot(b_rows, scaled, ((0,), (0,)))
        out[0 : b_rows.shape[1], :] = state.astype(BF16)
        high, low = two_parts(spread(passing_rows, channel, width)[0:1, :])
        line = lax.broadcasted_iota(jnp.int32, (PAD, width), 0)
        tail = jnp.where(line == 0, high.astype(F32), jnp.where(line == 1, low.astype(F32), 0.0))
        out[b_rows.shape[1] :, :] = tail.astype(BF16)


def decay_of(state):
    rows = state.shape[0] - PAD
    tail = state[rows : rows + PAD, :].astype(F32)
    return tail[0:1, :] + tail[1:2, :]


def over(condition, decay):
    return jnp.where(condition, decay, jnp.ones_like(decay))


def group_kernel(place, r0, r1, r2, r3, total):
    member = place[0]
    states = (r0, r1, r2, r3)
    rows = r0.shape[0] - PAD
    decays = [decay_of(state) for state in states]
    factors = []
    for k in range(len(states)):
        factor = jnp.ones_like(decays[0])
        for other in range(len(states)):
            if other != k:
                factor = factor * over((member ^ other) > (member ^ k), decays[other])
        factors.append(factor)
    step = 64
    for top in range(0, rows, step):
        value = factors[0] * r0[top : top + step, :].astype(F32)
        for k in range(1, len(states)):
            value = value + factors[k] * states[k][top : top + step, :].astype(F32)
        total[top : top + step, :] = value.astype(BF16)
    whole = decays[0] * decays[1] * decays[2] * decays[3]
    high, low = two_parts(whole)
    line = lax.broadcasted_iota(jnp.int32, (PAD, whole.shape[1]), 0)
    tail = jnp.where(line == 0, high.astype(F32), jnp.where(line == 1, low.astype(F32), 0.0))
    total[rows:, :] = tail.astype(BF16)


def entering_kernel(place, r0, r1, r2, r3, near_odd, near_even, far, e0, e1, e2, e3):
    member, group = place[0], place[2]
    states, outs = (r0, r1, r2, r3), (e0, e1, e2, e3)
    rows = r0.shape[0] - PAD
    decays = [decay_of(state) for state in states]
    one = jnp.ones_like(decays[0])
    odd = (group & 1) == 1
    from_odd = jnp.where(odd, one, 0.0)
    from_even = jnp.where(jnp.logical_and(group >= 2, jnp.logical_not(odd)), one, 0.0)
    near_decay = from_odd * decay_of(near_odd) + from_even * decay_of(near_even)
    from_far = jnp.where(group >= 2, near_decay, 0.0)
    heads, terms = [], []
    for k in range(len(states)):
        head = one
        for source in range(len(states)):
            if source != k:
                head = head * over((member ^ source) < (member ^ k), decays[source])
        heads.append(head)
        mine = []
        for source in range(len(states)):
            if source == k:
                mine.append(None)
                continue
            factor = jnp.where((member ^ source) < (member ^ k), one, 0.0)
            for between in range(len(states)):
                if between not in (k, source):
                    inside = jnp.logical_and(
                        (member ^ between) > (member ^ source), (member ^ between) < (member ^ k)
                    )
                    factor = factor * over(inside, decays[between])
            mine.append(factor)
        terms.append(mine)
    step = 32
    for top in range(0, rows, step):
        part = slice(top, top + step)
        carried = (
            from_odd * near_odd[part, :].astype(F32)
            + from_even * near_even[part, :].astype(F32)
            + from_far * far[part, :].astype(F32)
        )
        held = [state[part, :].astype(F32) for state in states]
        for k, out in enumerate(outs):
            value = heads[k] * carried
            for source in range(len(states)):
                if source != k:
                    value = value + terms[k][source] * held[source]
            out[part, :] = value.astype(BF16)


def intra_kernel(x, b, c, step, step_bias, decay_log, skip, offset, y, carry, bias, scores, columns):
    block = x.shape[0]
    half = block // 2
    time_step, rate_sum = rates(step[...], step_bias[...], decay_log[...])
    columns[...] = rate_sum.T
    offset_col = offset_columns(offset[...])
    row = lax.broadcasted_iota(jnp.int32, (block, LANES), 0)
    for left in range(0, block, LANES):
        column = lax.broadcasted_iota(jnp.int32, (block, LANES), 1) + left
        gap = row - column
        linked = jnp.logical_and(gap >= 0, offset_col >= gap.astype(F32))
        bias[:, left : left + LANES] = jnp.where(linked, 0.0, NEG)
    scores[...] = dot(c[...], b[...], ((1,), (1,)))
    reach = rate_sum - jnp.log(time_step)
    starts = row[:, 0 : carry.shape[1]].astype(F32) + 1.0
    carry[...] = jnp.where(offset_col[:, 0 : carry.shape[1]] >= starts, jnp.exp(columns[...]), 0.0)
    lane = lax.broadcasted_iota(jnp.int32, (1, LANES), 1)
    heads = step.shape[0]
    per_tile = LANES // HEADDIM
    for tile in range(heads // per_tile):
        cols = slice(tile * LANES, (tile + 1) * LANES)
        skip_row = jnp.zeros((1, LANES), F32)
        for k in range(per_tile):
            h = tile * per_tile + k
            skip_row = jnp.where(lane // HEADDIM == k, skip[h : h + 1, 0:1], skip_row)
        for top in range(0, block, half):
            part = slice(top, top + half)
            seen = top + half
            value = skip_row * x[part, cols].astype(F32)
            for k in range(per_tile):
                h = tile * per_tile + k
                gap = columns[part, h : h + 1] - reach[h : h + 1, 0:seen] + bias[part, 0:seen]
                weights = (scores[part, 0:seen] * jnp.exp(gap)).astype(BF16)
                chosen = jnp.where(lane // HEADDIM == k, x[0:seen, cols], jnp.zeros((), BF16))
                value = value + dot(weights, chosen)
            y[part, cols] = value


def back_kernel(place, c, f0, f1, f2, f3, intra, carry, out):
    member = place[0]
    parts = (f0, f1, f2, f3)
    width = out.shape[1] // len(parts)
    for k, state in enumerate(parts):
        channel = pl.multiple_of((member ^ k) * width, width)
        scale = spread(carry[...], channel, width)
        cols = pl.ds(channel, width)
        value = intra[:, cols] + scale * dot(c[...], state[...])
        out[:, cols] = value.astype(BF16)


def exchange(array, mask):
    return lax.ppermute(array, "seq", [(i, i ^ mask) for i in range(lax.axis_size("seq"))])


def shifted(array, distance):
    count = lax.axis_size("seq")
    return lax.ppermute(array, "seq", [(i, i + distance) for i in range(count - distance)])


def earlier_groups(total, groups):
    if groups == 4:
        far = exchange(total, 2 * GROUP)
        pairs = []
        for member in range(GROUP):
            low, high = GROUP + member, 2 * GROUP + member
            pairs += [(low, high), (high, low)]
        near_even = lax.ppermute(total, "seq", pairs)
        near_odd = exchange(total, GROUP)
        return near_odd, near_even, far
    rows = total.shape[0] - PAD
    held = shifted(total, GROUP)
    distance = 1
    while distance < groups:
        earlier = shifted(held, GROUP * distance)
        decay, before = decay_of(held), decay_of(earlier)
        state = held[:rows].astype(F32) + decay * earlier[:rows].astype(F32)
        high, low = two_parts(decay * before)
        tail = jnp.concatenate([high, low, jnp.zeros((PAD - 2, high.shape[1]), BF16)], axis=0)
        held = jnp.concatenate([state.astype(BF16), tail], axis=0)
        distance *= 2
    odd = (lax.axis_index("seq") // GROUP) % 2 == 1
    nothing = jnp.zeros_like(held)
    return jnp.where(odd, held, nothing), jnp.where(odd, nothing, held), nothing


def on_device(
    ssm_input, bc_input, conv_taps, conv_bias, bc_taps, bc_bias,
    step_input, step_bias, decay_log, skip_gain, request_offset,
):
    block, channels = ssm_input.shape
    state_size = bc_input.shape[1]
    heads = step_input.shape[0]
    width = channels // GROUP
    groups = lax.axis_size("seq") // GROUP
    here = lax.axis_index("seq")
    place = jnp.stack([here % GROUP, lax.axis_index("head") % 2, here // GROUP]).astype(jnp.int32)

    swap = [(i, i ^ 1) for i in range(lax.axis_size("head"))]
    other_bc = lax.ppermute(bc_input, "head", swap)
    own_taps = jnp.concatenate([bc_taps, bc_bias[None, :]], axis=0)
    other_taps = lax.ppermute(own_taps, "head", swap)
    first_row = block - HALO
    halo = shifted(
        jnp.concatenate([ssm_input[first_row:], bc_input[first_row:], other_bc[first_row:]], axis=1), 1
    )
    halo_x = halo[:, :channels]
    halo_own = halo[:, channels : channels + state_size]
    halo_other = halo[:, channels + state_size :]
    step_col, decay_col = step_bias[:, None], decay_log[:, None]
    offset_row = request_offset[None, :]

    smem = pl.BlockSpec(memory_space=pltpu.SMEM)
    vmem = pl.BlockSpec(memory_space=pltpu.VMEM)
    slice_shape = jax.ShapeDtypeStruct((state_size + PAD, width), BF16)
    bc_shape = jax.ShapeDtypeStruct((block, state_size), BF16)
    x_conv, b_conv, c_conv, *slices = pl.pallas_call(
        front_kernel,
        out_shape=[jax.ShapeDtypeStruct(ssm_input.shape, BF16), bc_shape, bc_shape] + [slice_shape] * GROUP,
        in_specs=[smem] + [vmem] * 14,
        out_specs=[vmem] * (3 + GROUP),
        scratch_shapes=[
            pltpu.VMEM((block + 8, channels), F32),
            pltpu.VMEM((conv_taps.shape[0] - 1, block, LANES), F32),
            pltpu.VMEM((block, heads), F32),
        ],
        compiler_params=SMALL,
        name="front",
    )(
        place, ssm_input, bc_input, other_bc, halo_x, halo_own, halo_other, conv_taps, conv_bias[None, :],
        own_taps, other_taps, step_input, step_col, decay_col, offset_row,
    )
    received = [slices[0]] + [exchange(slices[k], k) for k in (1, 2, 3)]
    intra, carry = pl.pallas_call(
        intra_kernel,
        out_shape=[
            jax.ShapeDtypeStruct((block, channels), F32),
            jax.ShapeDtypeStruct((block, heads), F32),
        ],
        in_specs=[vmem] * 8,
        out_specs=[vmem] * 2,
        scratch_shapes=[
            pltpu.VMEM((block, block), F32),
            pltpu.VMEM((block, block), F32),
            pltpu.VMEM((block, heads), F32),
        ],
        compiler_params=SMALL,
        cost_estimate=pl.CostEstimate(flops=600_000_000, bytes_accessed=2_500_000, transcendentals=1_000_000),
        name="intra",
    )(x_conv, b_conv, c_conv, step_input, step_col, decay_col, skip_gain[:, None], offset_row)
    total = pl.pallas_call(
        group_kernel,
        out_shape=slice_shape,
        in_specs=[smem] + [vmem] * GROUP,
        out_specs=vmem,
        compiler_params=SMALL,
        name="group",
    )(place, *received)
    near_odd, near_even, far = earlier_groups(total, groups)
    entering = pl.pallas_call(
        entering_kernel,
        out_shape=[jax.ShapeDtypeStruct((state_size, width), BF16)] * GROUP,
        in_specs=[smem] + [vmem] * (GROUP + 3),
        out_specs=[vmem] * GROUP,
        compiler_params=SMALL,
        name="entering",
    )(place, *received, near_odd, near_even, far)
    mine = [entering[0]] + [exchange(entering[k], k) for k in (1, 2, 3)]
    return pl.pallas_call(
        back_kernel,
        out_shape=jax.ShapeDtypeStruct((block, channels), BF16),
        in_specs=[smem] + [vmem] * (GROUP + 3),
        out_specs=vmem,
        compiler_params=SMALL,
        name="back",
    )(place, c_conv, *mine, intra, carry)


def solution(mesh):
    return jax.shard_map(
        on_device,
        mesh=mesh,
        in_specs=(
            P("seq", "head"),
            P("seq", "head"),
            P(None, "head"),
            P("head"),
            P(None, "head"),
            P("head"),
            P("head", "seq"),
            P("head"),
            P("head"),
            P("head"),
            P("seq"),
        ),
        out_specs=P("seq", "head"),
        check_vma=False,
    )
```

time: 315 us -> 48.4 us (0.15)
  the two profiles are of different devices: /device:TPU:24 before, /device:TPU:16 now
where the time goes in v1:
time: 48.4 us; the launch traced here: 48 us
  waiting for transfers between devices  17 us (35%)
  starting transfers between devices  15.6 us (32%)
  Pallas kernels  9.1 us (19%)
  local copies, waits for them, and re-layouts  5.43 us (11%)
  other arithmetic  0.78 us (2%)
    ppermute x8, waiting for transfers between devices, exchange(): lax.ppermute(array, 'seq', [(i, i ^ mask) for i in range(lax.axis_size('s...  9.32 us
    ppermute x8, starting transfers between devices, exchange(): lax.ppermute(array, 'seq', [(i, i ^ mask) for i in range(lax.axis_size('s...  7.54 us
    ppermute x1, waiting for transfers between devices, earlier_groups(): near_even = lax.ppermute(total, 'seq', pairs)  4.84 us
    ppermute x1, starting transfers between devices, earlier_groups(): near_even = lax.ppermute(total, 'seq', pairs)  4.63 us
    pallas_call x1, Pallas kernels, on_device(): pl.pallas_call(front_kernel, out_shape=[jax.ShapeDtypeStruct(ssm_input.sh...  3.87 us
    unnamed x20, local copies, waits for them, and re-layouts  3.73 us
    ppermute x1, starting transfers between devices, shifted(): lax.ppermute(array, 'seq', [(i, i + distance) for i in range(count - dist...  3.39 us
    ppermute x1, waiting for transfers between devices, shifted(): lax.ppermute(array, 'seq', [(i, i + distance) for i in range(count - dist...  2.86 us
  transfers between devices with their start and end apart: 12, of which 9 were waited for; matrix products, arithmetic and copies ran while one was open for 4% of the time, Pallas kernels for 4%

profile of v1, /device:TPU:16, one launch (start us, length us, event | category | flops | bytes accessed | tf_op | source)
XLA Modules:
  0.0 48.0 jit_solution(10523120749359016321)
XLA Ops:
  0.0 0.7 %copy-done.6 = f32[256]{0:T(256)S(1)} copy-done((f32[256]{0:T(256)S(1)}, f32[256]{0:T(256)}, u32[]{:S(2)}) %copy-start.6) | copy-done | bytes 1048
  0.7 0.7 %pad_maximum_fusion.1.own_taps = f32[5,256]{1,0:T(8,128)S(1)} fusion(f32[1,256]{1,0:T(1,128)S(1)} %bitcast.12, f32[4,256]{1,0:T(4,128)} %param.15), kind=kLoop, calls=%fused_computation.1 | loop fusion | flops 1280 | bytes 10240 | tf_op jit(solution)/shard_map/concatenate | solution.py:325
  1.4 0.7 %slice.19 = bf16[16,256]{1,0:T(8,128)(2,1)S(1)} slice(bf16[256,256]{1,0:T(8,128)(2,1)} %own.1), slice={[240:256], [0:256]} | slice | bytes 16384 | tf_op jit(solution)/shard_map/slice | solution.py:329
  2.1 0.7 %slice-done = bf16[16,1024]{1,0:T(8,128)(2,1)S(1)} async-done(((bf16[256,1024]{1,0:T(8,128)(2,1)}), bf16[16,1024]{1,0:T(8,128)(2,1)S(1)}, s32[]{:S(2)}) %slice-start) | async-done | bytes 32792 | tf_op jit(solution)/shard_map/slice | solution.py:329
  2.9 3.4 %collective-permute-start.1 = (bf16[16,1536]{1,0:T(8,128)(2,1)S(1)}, bf16[16,1536]{1,0:T(8,128)(2,1)S(1)}, u32[]{:S(2)}, u32[]{:S(2)}) collective-permute-start(bf16[16,1536]{1,0:T(8,128)(2,1)S(1)} %pad_maximum_fusion), channel_id=1, source_target_pairs={{0,2},{2,4},{4,6},{6,8},{8,10},{10,12},{12,14},{14,16},{16,18},{18... | collective-permute-start | bytes 147464 | tf_op jit(solution)/shard_map/ppermute | solution.py:282
  6.3 0.7 %copy-done.7 = f32[16]{0:T(128)S(1)} copy-done((f32[16]{0:T(128)S(1)}, f32[16]{0:T(128)}, u32[]{:S(2)}) %copy-start.7) | copy-done | bytes 88
  7.1 0.7 %copy-done.8 = f32[16]{0:T(128)S(1)} copy-done((f32[16]{0:T(128)S(1)}, f32[16]{0:T(128)}, u32[]{:S(2)}) %copy-start.8) | copy-done | bytes 88
  7.7 0.1 copy.13.decay_log
  7.8 2.9 %collective-permute-done.1 = bf16[16,1536]{1,0:T(8,128)(2,1)S(1)} collective-permute-done((bf16[16,1536]{1,0:T(8,128)(2,1)S(1)}, bf16[16,1536]{1,0:T(8,128)(2,1)S(1)}, u32[]{:S(2)}, u32[]{:S(2)}) %collective-permute-start.1) | collective-permute-done | bytes 49184 | tf_op jit(solution)/shard_map/ppermute | solution.py:282
  10.7 0.7 %copy-done.2 = f32[4,1024]{1,0:T(4,128)S(1)} copy-done((f32[4,1024]{1,0:T(4,128)S(1)}, f32[4,1024]{1,0:T(4,128)}, u32[]{:S(2)}) %copy-start.2) | copy-done | bytes 16408
  11.4 1.0 %copy-done = bf16[256,1024]{1,0:T(8,128)(2,1)S(1)} copy-done((bf16[256,1024]{1,0:T(8,128)(2,1)S(1)}, bf16[256,1024]{1,0:T(8,128)(2,1)}, u32[]{:S(2)}) %copy-start) | copy-done | bytes 524312
  12.5 3.9 %front.1 = (bf16[256,1024]{1,0:T(8,128)(2,1)S(1)}, bf16[256,256]{1,0:T(8,128)(2,1)S(1)}, bf16[256,256]{1,0:T(8,128)(2,1)S(1)}, bf16[272,256]{1,0:T(8,128)(2,1)S(...) custom-call(s32[3]{0:T(128)S(1)} %pad_add_fusion.place, ...), custom_call_target="tpu_custom_call" | custom-call | tf_op jit(solution)/shard_map/front/pallas_call | solution.py:341
  16.4 1.2 %collective-permute-start.4 = (bf16[272,256]{1,0:T(8,128)(2,1)S(1)}, bf16[272,256]{1,0:T(8,128)(2,1)S(1)}, u32[]{:S(2)}, u32[]{:S(2)}) collective-permute-start(bf16[272,256]{1,0:T(8,128)(2,1)S(1)} %get-tuple-element.21), channel_id=1, source_target_pairs={{0,4},{2,6},{4,0},{6,2},{8,12},{10,14},{12,8},{14,10},{16,20},{18,... | collective-permute-start | bytes 417800 | tf_op jit(solution)/shard_map/ppermute | solution.py:277
  17.6 2.3 %collective-permute-start.5 = (bf16[272,256]{1,0:T(8,128)(2,1)S(1)}, bf16[272,256]{1,0:T(8,128)(2,1)S(1)}, u32[]{:S(2)}, u32[]{:S(2)}) collective-permute-start(bf16[272,256]{1,0:T(8,128)(2,1)S(1)} %get-tuple-element.22), channel_id=1, source_target_pairs={{0,6},{2,4},{4,2},{6,0},{8,14},{10,12},{12,10},{14,8},{16,22},{18,... | collective-permute-start | bytes 417800 | tf_op jit(solution)/shard_map/ppermute | solution.py:277
  19.9 3.1 %collective-permute-done.3.r1 = bf16[272,256]{1,0:T(8,128)(2,1)S(1)} collective-permute-done((bf16[272,256]{1,0:T(8,128)(2,1)S(1)}, bf16[272,256]{1,0:T(8,128)(2,1)S(1)}, u32[]{:S(2)}, u32[]{:S(2)}) %collective-permute-start.3) | collective-permute-done | bytes 139296 | tf_op jit(solution)/shard_map/ppermute | solution.py:277
  23.0 0.1 collective-permute-done.4.r2
  23.1 1.7 %collective-permute-done.5.r3 = bf16[272,256]{1,0:T(8,128)(2,1)S(1)} collective-permute-done((bf16[272,256]{1,0:T(8,128)(2,1)S(1)}, bf16[272,256]{1,0:T(8,128)(2,1)S(1)}, u32[]{:S(2)}, u32[]{:S(2)}) %collective-permute-start.5) | collective-permute-done | bytes 139296 | tf_op jit(solution)/shard_map/ppermute | solution.py:277
  24.7 0.7 %group.1 = bf16[272,256]{1,0:T(8,128)(2,1)S(1)} custom-call(s32[3]{0:T(128)S(1)} %pad_add_fusion.place, bf16[272,256]{1,0:T(8,128)(2,1)S(1)} %get-tuple-element.19.r0, bf16[272,256]{1,0:T(8,128)(2,1)S(1)} %collective-permute-done.3.r1, bf16[272,256]{1,0:T(8,128)(2,1)S(1)} %collective-permute-done.4.r2, bf16[272,256]{1,0:T(8,128)(2,1)S(1)} %collective-permute-done.5.r3), custom_call_target="tpu_custom_call" | custom-call | tf_op jit(solution)/shard_map/group/pallas_call | solution.py:375
  25.4 0.4 collective-permute-start.8
  25.8 4.6 %collective-permute-start.7 = (bf16[272,256]{1,0:T(8,128)(2,1)S(1)}, bf16[272,256]{1,0:T(8,128)(2,1)S(1)}, u32[]{:S(2)}, u32[]{:S(2)}) collective-permute-start(bf16[272,256]{1,0:T(8,128)(2,1)S(1)} %group.1), channel_id=1, source_target_pairs={{8,16},{16,8},{10,18},{18,10},{12,20},{20,12},{14,22},{22,14},{9,1... | collective-permute-start | bytes 417800 | tf_op jit(solution)/shard_map/ppermute | solution.py:292
  30.5 1.4 %collective-permute-done.8.far = bf16[272,256]{1,0:T(8,128)(2,1)S(1)} collective-permute-done((bf16[272,256]{1,0:T(8,128)(2,1)S(1)}, bf16[272,256]{1,0:T(8,128)(2,1)S(1)}, u32[]{:S(2)}, u32[]{:S(2)}) %collective-permute-start.8) | collective-permute-done | bytes 139296 | tf_op jit(solution)/shard_map/ppermute | solution.py:277
  31.9 4.8 %collective-permute-done.7.near_even = bf16[272,256]{1,0:T(8,128)(2,1)S(1)} collective-permute-done((bf16[272,256]{1,0:T(8,128)(2,1)S(1)}, bf16[272,256]{1,0:T(8,128)(2,1)S(1)}, u32[]{:S(2)}, u32[]{:S(2)}) %collective-permute-start.7) | collective-permute-done | bytes 139296 | tf_op jit(solution)/shard_map/ppermute | solution.py:292
  36.8 0.9 %entering.1 = (bf16[256,256]{1,0:T(8,128)(2,1)S(1)}, bf16[256,256]{1,0:T(8,128)(2,1)S(1)}, bf16[256,256]{1,0:T(8,128)(2,1)S(1)}, bf16[256,256]{1,0:T(8,128)(2,1)S(1)}) custom-call(s32[3]{0:T(128)S(1)} %pad_add_fusion.place, bf16[272,256]{1,0:T(8,128)(2,1)S(1)} %get-tuple-element.19.r0, bf16[272,256]{1,0:T(8,128)(2,1)S(1)} %collective-permute-done.3.r1, ...), custom_call_target="tpu_custom_call" | custom-call | tf_op jit(solution)/shard_map/entering/pallas_call | solution.py:384
  37.7 0.7 %collective-permute-start.9 = (bf16[256,256]{1,0:T(8,128)(2,1)S(1)}, bf16[256,256]{1,0:T(8,128)(2,1)S(1)}, u32[]{:S(2)}, u32[]{:S(2)}) collective-permute-start(bf16[256,256]{1,0:T(8,128)(2,1)S(1)} %get-tuple-element.24), channel_id=1, source_target_pairs={{0,2},{2,0},{4,6},{6,4},{8,10},{10,8},{12,14},{14,12},{16,18},{18,... | collective-permute-start | bytes 393224 | tf_op jit(solution)/shard_map/ppermute | solution.py:277
  38.4 0.8 %collective-permute-start.10 = (bf16[256,256]{1,0:T(8,128)(2,1)S(1)}, bf16[256,256]{1,0:T(8,128)(2,1)S(1)}, u32[]{:S(2)}, u32[]{:S(2)}) collective-permute-start(bf16[256,256]{1,0:T(8,128)(2,1)S(1)} %get-tuple-element.25), channel_id=1, source_target_pairs={{0,4},{2,6},{4,0},{6,2},{8,12},{10,14},{12,8},{14,10},{16,20},{18,... | collective-permute-start | bytes 393224 | tf_op jit(solution)/shard_map/ppermute | solution.py:277
  39.3 2.0 %collective-permute-start.11 = (bf16[256,256]{1,0:T(8,128)(2,1)S(1)}, bf16[256,256]{1,0:T(8,128)(2,1)S(1)}, u32[]{:S(2)}, u32[]{:S(2)}) collective-permute-start(bf16[256,256]{1,0:T(8,128)(2,1)S(1)} %get-tuple-element.26), channel_id=1, source_target_pairs={{0,6},{2,4},{4,2},{6,0},{8,14},{10,12},{12,10},{14,8},{16,22},{18,... | collective-permute-start | bytes 393224 | tf_op jit(solution)/shard_map/ppermute | solution.py:277
  41.3 0.1 copy.16.skip
  41.3 1.7 %intra.1 = (f32[256,1024]{1,0:T(8,128)S(1)}, f32[256,16]{1,0:T(8,128)S(1)}) custom-call(bf16[256,1024]{1,0:T(8,128)(2,1)S(1)} %get-tuple-element.27.x, bf16[256,256]{1,0:T(8,128)(2,1)S(1)} %get-tuple-element.28.b, bf16[256,256]{1,0:T(8,128)(2,1)S(1)} %get-tuple-element.18.c, f32[16,256]{1,0:T(8,128)S(1)} %copy-done.3, f32[16,1]{1,0:T(8,128)S(1)} %copy.12.step_bias, ...), custom_call_target="tpu_custom_call" | custom-call | flops 600000000 | bytes 2500000 | tf_op jit(solution)/shard_map/intra/pallas_call | solution.py:358
  43.1 0.8 %collective-permute-done.9.f1 = bf16[256,256]{1,0:T(8,128)(2,1)S(1)} collective-permute-done((bf16[256,256]{1,0:T(8,128)(2,1)S(1)}, bf16[256,256]{1,0:T(8,128)(2,1)S(1)}, u32[]{:S(2)}, u32[]{:S(2)}) %collective-permute-start.9) | collective-permute-done | bytes 131104 | tf_op jit(solution)/shard_map/ppermute | solution.py:277
  43.8 0.9 %collective-permute-done.10.f2 = bf16[256,256]{1,0:T(8,128)(2,1)S(1)} collective-permute-done((bf16[256,256]{1,0:T(8,128)(2,1)S(1)}, bf16[256,256]{1,0:T(8,128)(2,1)S(1)}, u32[]{:S(2)}, u32[]{:S(2)}) %collective-permute-start.10) | collective-permute-done | bytes 131104 | tf_op jit(solution)/shard_map/ppermute | solution.py:277
  44.7 1.4 %collective-permute-done.11.f3 = bf16[256,256]{1,0:T(8,128)(2,1)S(1)} collective-permute-done((bf16[256,256]{1,0:T(8,128)(2,1)S(1)}, bf16[256,256]{1,0:T(8,128)(2,1)S(1)}, u32[]{:S(2)}, u32[]{:S(2)}) %collective-permute-start.11) | collective-permute-done | bytes 131104 | tf_op jit(solution)/shard_map/ppermute | solution.py:277
  46.1 1.9 %back.1 = bf16[256,1024]{1,0:T(8,128)(2,1)} custom-call(s32[3]{0:T(128)S(1)} %pad_add_fusion.place, bf16[256,256]{1,0:T(8,128)(2,1)S(1)} %get-tuple-element.18.c, bf16[256,256]{1,0:T(8,128)(2,1)S(1)} %get-tuple-element.23.f0, bf16[256,256]{1,0:T(8,128)(2,1)S(1)} %collective-permute-done.9.f1, bf16[256,256]{1,0:T(8,128)(2,1)S(1)} %collective-permute-done.10.f2, ...), custom_call_target="tpu_custom_call" | custom-call | tf_op jit(solution)/shard_map/back/pallas_call | solution.py:393
  (29 shorter events, 0.4 us)
Async XLA Ops:
  0.0 0.7 %copy-start.6 = (f32[256]{0:T(256)S(1)}, f32[256]{0:T(256)}, u32[]{:S(2)}) copy-start(f32[256]{0:T(256)} %param.16) | copy-start | bytes 3076
  0.0 2.1 %collective-permute-start = (bf16[256,256]{1,0:T(8,128)(2,1)}, bf16[256,256]{1,0:T(8,128)(2,1)S(1)}, u32[]{:S(2)}, u32[]{:S(2)}) collective-permute-start(bf16[256,256]{1,0:T(8,128)(2,1)} %own.1), channel_id=1, source_target_pairs={{0,1},{1,0},{2,3},{3,2},{4,5},{5,4},{6,7},{7,6},{8,9},{9,8},{10,11... | collective-permute-start | bytes 393224 | tf_op jit(solution)/shard_map/ppermute | solution.py:324
  1.4 9.3 %collective-permute-start.2 = (f32[5,256]{1,0:T(8,128)S(1)}, f32[5,256]{1,0:T(8,128)S(1)}, u32[]{:S(2)}, u32[]{:S(2)}) collective-permute-start(f32[5,256]{1,0:T(8,128)S(1)} %pad_maximum_fusion.1.own_taps), channel_id=1, source_target_pairs={{0,1},{1,0},{2,3},{3,2},{4,5},{5,4},{6,7},{7,6},{8,9},{9,8},{10,11... | collective-permute-start | bytes 15368 | tf_op jit(solution)/shard_map/ppermute | solution.py:326
  2.1 0.8 %slice-start = ((bf16[256,1024]{1,0:T(8,128)(2,1)}), bf16[16,1024]{1,0:T(8,128)(2,1)S(1)}, s32[]{:S(2)}) async-start(bf16[256,1024]{1,0:T(8,128)(2,1)} %x.1), calls=%async_computation | async-start | bytes 65536 | tf_op jit(solution)/shard_map/slice | solution.py:329
  2.1 8.6 %copy-start.1 = (bf16[256,256]{1,0:T(8,128)(2,1)S(1)}, bf16[256,256]{1,0:T(8,128)(2,1)}, u32[]{:S(2)}) copy-start(bf16[256,256]{1,0:T(8,128)(2,1)} %own.1) | copy-start | bytes 393220
  2.9 7.8 %collective-permute-start.1 = (bf16[16,1536]{1,0:T(8,128)(2,1)S(1)}, bf16[16,1536]{1,0:T(8,128)(2,1)S(1)}, u32[]{:S(2)}, u32[]{:S(2)}) collective-permute-start(bf16[16,1536]{1,0:T(8,128)(2,1)S(1)} %pad_maximum_fusion), channel_id=1, source_target_pairs={{0,2},{2,4},{4,6},{6,8},{8,10},{10,12},{12,14},{14,16},{16,18},{18... | collective-permute-start | bytes 147464 | tf_op jit(solution)/shard_map/ppermute | solution.py:282
  6.3 0.7 %copy-start.7 = (f32[16]{0:T(128)S(1)}, f32[16]{0:T(128)}, u32[]{:S(2)}) copy-start(f32[16]{0:T(128)} %param.18) | copy-start | bytes 196
  7.1 0.7 %copy-start.8 = (f32[16]{0:T(128)S(1)}, f32[16]{0:T(128)}, u32[]{:S(2)}) copy-start(f32[16]{0:T(128)} %param.19) | copy-start | bytes 196
  10.7 0.7 %copy-start.2 = (f32[4,1024]{1,0:T(4,128)S(1)}, f32[4,1024]{1,0:T(4,128)}, u32[]{:S(2)}) copy-start(f32[4,1024]{1,0:T(4,128)} %taps.1) | copy-start | bytes 49156
  10.7 0.7 %copy-start.3 = (f32[16,256]{1,0:T(8,128)S(1)}, f32[16,256]{1,0:T(8,128)}, u32[]{:S(2)}) copy-start(f32[16,256]{1,0:T(8,128)} %step.3) | copy-start | bytes 49156
  10.7 0.7 %copy-start.4 = (f32[1024]{0:T(1024)S(1)}, f32[1024]{0:T(1024)}, u32[]{:S(2)}) copy-start(f32[1024]{0:T(1024)} %param.14) | copy-start | bytes 12292
  10.7 0.7 %copy-start.5 = (s32[256]{0:T(256)S(1)}, s32[256]{0:T(256)}, u32[]{:S(2)}) copy-start(s32[256]{0:T(256)} %param.21) | copy-start | bytes 3076
  11.4 1.0 %copy-start = (bf16[256,1024]{1,0:T(8,128)(2,1)S(1)}, bf16[256,1024]{1,0:T(8,128)(2,1)}, u32[]{:S(2)}) copy-start(bf16[256,1024]{1,0:T(8,128)(2,1)} %x.1) | copy-start | bytes 1572868
  16.3 6.6 %collective-permute-start.3 = (bf16[272,256]{1,0:T(8,128)(2,1)S(1)}, bf16[272,256]{1,0:T(8,128)(2,1)S(1)}, u32[]{:S(2)}, u32[]{:S(2)}) collective-permute-start(bf16[272,256]{1,0:T(8,128)(2,1)S(1)} %get-tuple-element.20), channel_id=1, source_target_pairs={{0,2},{2,0},{4,6},{6,4},{8,10},{10,8},{12,14},{14,12},{16,18},{18,... | collective-permute-start | bytes 417800 | tf_op jit(solution)/shard_map/ppermute | solution.py:277
  16.4 6.7 %collective-permute-start.4 = (bf16[272,256]{1,0:T(8,128)(2,1)S(1)}, bf16[272,256]{1,0:T(8,128)(2,1)S(1)}, u32[]{:S(2)}, u32[]{:S(2)}) collective-permute-start(bf16[272,256]{1,0:T(8,128)(2,1)S(1)} %get-tuple-element.21), channel_id=1, source_target_pairs={{0,4},{2,6},{4,0},{6,2},{8,12},{10,14},{12,8},{14,10},{16,20},{18,... | collective-permute-start | bytes 417800 | tf_op jit(solution)/shard_map/ppermute | solution.py:277
  17.6 7.1 %collective-permute-start.5 = (bf16[272,256]{1,0:T(8,128)(2,1)S(1)}, bf16[272,256]{1,0:T(8,128)(2,1)S(1)}, u32[]{:S(2)}, u32[]{:S(2)}) collective-permute-start(bf16[272,256]{1,0:T(8,128)(2,1)S(1)} %get-tuple-element.22), channel_id=1, source_target_pairs={{0,6},{2,4},{4,2},{6,0},{8,14},{10,12},{12,10},{14,8},{16,22},{18,... | collective-permute-start | bytes 417800 | tf_op jit(solution)/shard_map/ppermute | solution.py:277
  25.4 6.5 %collective-permute-start.8 = (bf16[272,256]{1,0:T(8,128)(2,1)S(1)}, bf16[272,256]{1,0:T(8,128)(2,1)S(1)}, u32[]{:S(2)}, u32[]{:S(2)}) collective-permute-start(bf16[272,256]{1,0:T(8,128)(2,1)S(1)} %group.1), channel_id=1, source_target_pairs={{0,16},{2,18},{4,20},{6,22},{8,24},{10,26},{12,28},{14,30},{16,0},... | collective-permute-start | bytes 417800 | tf_op jit(solution)/shard_map/ppermute | solution.py:277
  25.8 11.0 %collective-permute-start.7 = (bf16[272,256]{1,0:T(8,128)(2,1)S(1)}, bf16[272,256]{1,0:T(8,128)(2,1)S(1)}, u32[]{:S(2)}, u32[]{:S(2)}) collective-permute-start(bf16[272,256]{1,0:T(8,128)(2,1)S(1)} %group.1), channel_id=1, source_target_pairs={{8,16},{16,8},{10,18},{18,10},{12,20},{20,12},{14,22},{22,14},{9,1... | collective-permute-start | bytes 417800 | tf_op jit(solution)/shard_map/ppermute | solution.py:292
  30.4 6.3 %collective-permute-start.6 = (bf16[272,256]{1,0:T(8,128)(2,1)S(1)}, bf16[272,256]{1,0:T(8,128)(2,1)S(1)}, u32[]{:S(2)}, u32[]{:S(2)}) collective-permute-start(bf16[272,256]{1,0:T(8,128)(2,1)S(1)} %group.1), channel_id=1, source_target_pairs={{0,8},{2,10},{4,12},{6,14},{8,0},{10,2},{12,4},{14,6},{16,24},{18,... | collective-permute-start | bytes 417800 | tf_op jit(solution)/shard_map/ppermute | solution.py:277
  37.7 6.1 %collective-permute-start.9 = (bf16[256,256]{1,0:T(8,128)(2,1)S(1)}, bf16[256,256]{1,0:T(8,128)(2,1)S(1)}, u32[]{:S(2)}, u32[]{:S(2)}) collective-permute-start(bf16[256,256]{1,0:T(8,128)(2,1)S(1)} %get-tuple-element.24), channel_id=1, source_target_pairs={{0,2},{2,0},{4,6},{6,4},{8,10},{10,8},{12,14},{14,12},{16,18},{18,... | collective-permute-start | bytes 393224 | tf_op jit(solution)/shard_map/ppermute | solution.py:277
  38.4 6.3 %collective-permute-start.10 = (bf16[256,256]{1,0:T(8,128)(2,1)S(1)}, bf16[256,256]{1,0:T(8,128)(2,1)S(1)}, u32[]{:S(2)}, u32[]{:S(2)}) collective-permute-start(bf16[256,256]{1,0:T(8,128)(2,1)S(1)} %get-tuple-element.25), channel_id=1, source_target_pairs={{0,4},{2,6},{4,0},{6,2},{8,12},{10,14},{12,8},{14,10},{16,20},{18,... | collective-permute-start | bytes 393224 | tf_op jit(solution)/shard_map/ppermute | solution.py:277
  39.3 2.0 %copy-start.9 = (f32[16]{0:T(128)S(1)}, f32[16]{0:T(128)}, u32[]{:S(2)}) copy-start(f32[16]{0:T(128)} %param.20) | copy-start | bytes 196
  39.3 6.9 %collective-permute-start.11 = (bf16[256,256]{1,0:T(8,128)(2,1)S(1)}, bf16[256,256]{1,0:T(8,128)(2,1)S(1)}, u32[]{:S(2)}, u32[]{:S(2)}) collective-permute-start(bf16[256,256]{1,0:T(8,128)(2,1)S(1)} %get-tuple-element.26), channel_id=1, source_target_pairs={{0,6},{2,4},{4,2},{6,0},{8,14},{10,12},{12,10},{14,8},{16,22},{18,... | collective-permute-start | bytes 393224 | tf_op jit(solution)/shard_map/ppermute | solution.py:277

commit v2 on v0

v2 whole, which is shorter than its diff:
```python
import jax
import jax.numpy as jnp
from jax import lax
from jax.experimental import pallas as pl
from jax.experimental.pallas import tpu as pltpu
from jax.sharding import PartitionSpec as P

HEADDIM = 64
GROUP = 4
TAIL = 16
GATE_AT, X_LAST_AT, X_FIRST_AT, B_LAST_AT, B_FIRST_AT = 1, 4, 7, 10, 13
HALO = 16
LANES = 128
NEG = -1e30
F32 = jnp.float32
BF16 = jnp.bfloat16
PARAMS = pltpu.CompilerParams(vmem_limit_bytes=24 * 1024 * 1024)


def dot(a, b, dims=((1,), (0,))):
    return lax.dot_general(a, b, (dims, ((), ())), preferred_element_type=F32)


def two_parts(value):
    high = value.astype(BF16).astype(F32)
    return high, value - high


def silu(v):
    return 0.5 * v * (1.0 + jnp.tanh(0.5 * v))


def iota(shape, dim):
    return lax.broadcasted_iota(jnp.int32, shape, dim)


def column(scalars, count):
    row = iota((count, LANES), 0)
    value = jnp.zeros((count, LANES), F32)
    for k in range(count):
        value = jnp.where(row == k, scalars[k], value)
    return value[:, 0:1]


def spread(parts, first_channel, width):
    heads = parts.shape[1] // 2
    shape = (2 * heads, width)
    head = iota(shape, 0) & (heads - 1)
    channel = iota(shape, 1) + first_channel
    return dot(parts, (channel // HEADDIM == head).astype(F32).astype(BF16))


def turned(per_head):
    high, low = two_parts(per_head)
    return jnp.concatenate([high, low], axis=0).T.astype(BF16)


def rates(step, step_bias, decay_log):
    heads, block = step.shape
    time_step = jax.nn.softplus(step + step_bias)
    log_decay = -jnp.exp(decay_log) * time_step
    shape = (block, block)
    upto = (iota(shape, 0) <= iota(shape, 1)).astype(F32).astype(BF16)
    first, rest = two_parts(log_decay)
    second, third = two_parts(rest)
    sums = dot(jnp.concatenate([first, second, third], axis=0).astype(BF16), upto)
    return time_step, sums[0:heads] + (sums[heads : 2 * heads] + sums[2 * heads :])


def offset_columns(offset_row):
    wide = jnp.broadcast_to(offset_row.astype(F32), (LANES, offset_row.shape[1]))
    return wide.T


def lag_matrices(offset_col, count):
    block = offset_col.shape[0]
    gap = iota((block, block), 0) - iota((block, block), 1)
    offset_wide = jnp.concatenate([offset_col] * (block // LANES), axis=1)
    return [
        jnp.where(jnp.logical_and(gap == lag, offset_wide >= lag), 1.0, 0.0).astype(BF16)
        for lag in range(1, count)
    ]


def convolve(source, taps, bias, lags):
    count = len(lags) + 1
    total = taps[count - 1 : count] * source.astype(F32) + bias
    for lag, matrix in enumerate(lags, 1):
        total = total + taps[count - 1 - lag : count - lag] * dot(matrix, source)
    return total


def channels_kernel(x, taps, bias, step, step_bias, decay_log, offset, x_out, gated, aux, passing_out):
    block, channels = x.shape
    count = taps.shape[0]
    heads = step.shape[0]
    offset_col = offset_columns(offset[...])
    lags = lag_matrices(offset_col, count)
    time_step, rate_sum = rates(step[...], column(step_bias, heads), column(decay_log, heads))
    last_offset = offset[0, block - 1]
    place = iota(rate_sum.shape, 1)
    last = rate_sum[:, block - 1 : block]
    gate = jnp.exp(jnp.where(last_offset >= block - 1 - place, last - rate_sum, NEG)) * time_step
    passing = jnp.exp(last) * (last_offset >= block).astype(F32)
    passing_out[...] = jnp.broadcast_to(passing, passing_out.shape)
    gate_early = turned(gate)[0:TAIL]
    gate_late = turned(jnp.where(place >= count - 1, gate, 0.0))
    width = channels // GROUP
    for k in range(GROUP):
        cols = slice(k * width, (k + 1) * width)
        source = x[:, cols]
        before = convolve(source, taps[:, cols], bias[:, cols], lags)
        value = silu(before).astype(BF16)
        x_out[:, cols] = value
        gated[:, cols] = (value.astype(F32) * spread(gate_late, k * width, width)).astype(BF16)
        aux[0:8, cols] = before[0:8]
        early = spread(gate_early, k * width, width)
        first = source[0:TAIL].astype(F32)
        last_rows = source[block - TAIL : block].astype(F32)
        aux[8:24, cols] = jnp.concatenate(
            [early[0:1], early[0:3], last_rows[TAIL - 3 :], first[0:3], jnp.zeros((TAIL - 10, width), F32)], axis=0
        )


def states_kernel(
    place, own, other, own_taps, other_taps, own_bias, other_bias, gated, aux, passing, offset,
    s0, s1, s2, s3, b_out, b_taps, turn,
):
    member = place[0]
    first = place[1] == 0
    block, state_size = own.shape
    count = own_taps.shape[0]
    lags = lag_matrices(offset_columns(offset[...]), count)
    taps = jnp.where(first, own_taps[...], other_taps[...])
    bias = jnp.where(first, own_bias[...], other_bias[...])
    source = jnp.where(first, own[...].astype(F32), other[...].astype(F32))
    before = convolve(source.astype(BF16), taps, bias, lags)
    value = silu(before)
    b_out[...] = value.astype(BF16)
    turn[...] = value.T.astype(BF16)
    b_taps[...] = jnp.concatenate([taps, bias, jnp.zeros((8 - count - 1, state_size), F32), before[0:8]], axis=0)
    width = gated.shape[1] // GROUP
    heads = passing.shape[0]
    slice_heads = heads // GROUP
    lane = iota((heads, width), 1)
    head = iota((heads, width), 0)
    high, low = two_parts(passing[:, 0:1])
    offsets = pltpu.roll(jnp.minimum(offset[...], count - 1).astype(F32), 2 * slice_heads, 1)
    offsets = jnp.where(
        jnp.logical_and(lane[0:1] >= 2 * slice_heads, lane[0:1] < 2 * slice_heads + count - 1), offsets, 0.0
    )
    row = iota((TAIL, width), 0)
    b_tail = jnp.concatenate(
        [jnp.zeros((B_LAST_AT, width), F32), source[block - 3 :], source[0:3]], axis=0
    )
    for k, out in enumerate((s0, s1, s2, s3)):
        quarter = member ^ k
        cols = pl.ds(pl.multiple_of(quarter * width, width), width)
        out[0:state_size, :] = dot(turn[...], gated[:, cols]).astype(BF16)
        at = lane + quarter * slice_heads
        packed = jnp.where(lane < slice_heads, jnp.where(at == head, high, 0.0), 0.0)
        packed = jnp.where(jnp.logical_and(lane >= slice_heads, at == head + slice_heads), low, packed)
        packed = jnp.where(lane < 2 * slice_heads, packed, 0.0)
        misc = jnp.sum(packed, axis=0, keepdims=True) + offsets
        tail = jnp.where(row == 0, misc, jnp.where(row < B_LAST_AT, aux[8:24, cols], b_tail))
        out[state_size:, :] = tail.astype(BF16)


def tail_of(state):
    rows = state.shape[0]
    return state[rows - TAIL : rows, :].astype(F32)


def decay_of(tail):
    width = tail.shape[1]
    slice_heads = width // HEADDIM
    channel = iota((1, width), 1)
    value = jnp.zeros((1, width), F32)
    for head in range(slice_heads):
        both = tail[0:1, head : head + 1] + tail[0:1, slice_heads + head : slice_heads + head + 1]
        value = jnp.where(channel // HEADDIM == head, both, value)
    return value


def pack_decay(decay, tail):
    width = decay.shape[1]
    slice_heads = width // HEADDIM
    lane = iota((1, width), 1)
    high, low = two_parts(decay)
    row = jnp.where(lane >= 2 * slice_heads, tail[0:1], 0.0)
    for head in range(slice_heads):
        at = head * HEADDIM
        row = jnp.where(lane == head, high[:, at : at + 1], row)
        row = jnp.where(lane == slice_heads + head, low[:, at : at + 1], row)
    return row


def tail_taps(x_taps, x_bias, b_taps, count):
    width = x_taps.shape[1]
    upper = iota((TAIL, width), 0) < B_LAST_AT
    taps = [jnp.where(upper, x_taps[k : k + 1], b_taps[k : k + 1]) for k in range(count)]
    return taps, jnp.where(upper, x_bias, b_taps[count : count + 1])


def early_tokens(tail, earlier, taps, bias):
    width = tail.shape[1]
    slice_heads = width // HEADDIM
    count = len(taps)
    row = iota(tail.shape, 0)
    is_last = jnp.logical_or(
        jnp.logical_and(row >= X_LAST_AT, row < X_FIRST_AT),
        jnp.logical_and(row >= B_LAST_AT, row < B_FIRST_AT),
    )
    rows = jnp.where(is_last, earlier, tail)
    offset = jnp.full(tail.shape, -1.0, F32)
    for token in range(count - 1):
        lane = 2 * slice_heads + token
        here = jnp.logical_or(row == X_FIRST_AT + token, row == B_FIRST_AT + token)
        offset = jnp.where(here, tail[0:1, lane : lane + 1], offset)
    total = taps[count - 1] * rows + bias
    for lag in range(1, count):
        total = total + taps[count - 1 - lag] * jnp.where(offset >= lag, pltpu.roll(rows, lag, 0), 0.0)
    value = silu(total).astype(BF16).astype(F32)
    gate = pltpu.roll(tail, B_FIRST_AT - GATE_AT, 0)
    wanted = row >= B_FIRST_AT
    b = jnp.where(wanted, value, 0.0)
    x = jnp.where(wanted, pltpu.roll(value, B_FIRST_AT - X_FIRST_AT, 0) * gate, 0.0)
    return b, x


def group_kernel(place, r0, r1, r2, r3, earlier, x_taps, x_bias, b_taps, total, *, complete):
    rows = r0.shape[0] - TAIL
    width = r0.shape[1]
    count = x_taps.shape[0]
    held = (r0, r1, r2, r3)

    def run(member):
        cols = slice(member * width, (member + 1) * width)
        taps, bias = tail_taps(x_taps[:, cols], x_bias[:, cols], b_taps[...], count)
        states = [held[member ^ k] for k in range(GROUP)]
        tails = [tail_of(state) for state in states]
        decays = [decay_of(tail) for tail in tails]
        factors = [None] * GROUP
        factor = jnp.ones((1, width), F32)
        for k in reversed(range(GROUP)):
            factors[k] = factor
            factor = factor * decays[k]
        early_b, early_x = [], []
        for k in range(0 if complete else 1, GROUP):
            before = tails[k - 1] if k else tail_of(earlier)
            b, x = early_tokens(tails[k], before, taps, bias)
            early_b.append(b)
            early_x.append(x * factors[k])
        b_turned = jnp.concatenate(early_b, axis=0).T.astype(BF16)
        added = dot(b_turned, jnp.concatenate(early_x, axis=0).astype(BF16))
        step = 64
        for top in range(0, rows, step):
            part = slice(top, top + step)
            value = added[part]
            for k in range(GROUP):
                value = value + factors[k] * states[k][part, :].astype(F32)
            total[part, :] = value.astype(BF16)
        row = iota((TAIL, width), 0)
        is_last = jnp.logical_or(
            jnp.logical_and(row >= X_LAST_AT, row < X_FIRST_AT),
            jnp.logical_and(row >= B_LAST_AT, row < B_FIRST_AT),
        )
        gates = jnp.zeros((1, width), F32) if complete else factors[0]
        tail = jnp.where(is_last, tails[GROUP - 1], tails[0])
        tail = jnp.where(row < X_LAST_AT, tail * gates, tail)
        tail = jnp.where(row == 0, pack_decay(factor, tails[0]), tail)
        total[rows:, :] = tail.astype(BF16)

    for member in range(GROUP):
        pl.when(place[0] == member)(lambda member=member: run(member))


def entering_kernel(
    place, r0, r1, r2, r3, near_odd, near_even, far, x_taps, x_bias, b_taps, e0, e1, e2, e3
):
    group = place[2]
    odd = (group & 1) == 1
    one = jnp.ones((1, r0.shape[1]), F32)
    from_odd = jnp.where(odd, one, 0.0)
    from_even = jnp.where(jnp.logical_and(group >= 2, jnp.logical_not(odd)), one, 0.0)
    from_far = jnp.where(group >= 2, one, 0.0)
    rows = r0.shape[0] - TAIL
    width = r0.shape[1]
    count = x_taps.shape[0]
    held, outs = (r0, r1, r2, r3), (e0, e1, e2, e3)

    def run(member):
        cols = slice(member * width, (member + 1) * width)
        taps, bias = tail_taps(x_taps[:, cols], x_bias[:, cols], b_taps[...], count)
        states = [held[member ^ k] for k in range(GROUP)]
        targets = [outs[member ^ k] for k in range(GROUP)]
        tails = [tail_of(state) for state in states]
        near_tail = from_odd * tail_of(near_odd) + from_even * tail_of(near_even)
        far_tail = from_far * tail_of(far)
        decays = [decay_of(tail) for tail in tails]
        near_decay = decay_of(near_tail)
        far_factor = near_decay * from_far
        far_b, far_x = early_tokens(far_tail, jnp.zeros_like(far_tail), taps, bias)
        near_b, near_x = early_tokens(near_tail, far_tail, taps, bias)
        early_b, early_x = [far_b, near_b], [far_x * near_decay, near_x]
        for k in range(GROUP - 1):
            b, x = early_tokens(tails[k], tails[k - 1] if k else near_tail, taps, bias)
            early_b.append(b)
            early_x.append(x)
        b_turned = jnp.concatenate(early_b, axis=0).T.astype(BF16)
        x_rows = jnp.concatenate(early_x, axis=0).astype(BF16)
        added = [dot(b_turned[:, : 2 * TAIL], x_rows[: 2 * TAIL])]
        for k in range(GROUP - 1):
            part = slice((k + 2) * TAIL, (k + 3) * TAIL)
            added.append(dot(b_turned[:, part], x_rows[part]))
        step = 32
        for top in range(0, rows, step):
            part = slice(top, top + step)
            value = from_odd * near_odd[part, :].astype(F32) + from_even * near_even[part, :].astype(F32)
            value = value + far_factor * far[part, :].astype(F32) + added[0][part]
            targets[0][part, :] = value.astype(BF16)
            for k in range(GROUP - 1):
                value = decays[k] * value + states[k][part, :].astype(F32) + added[k + 1][part]
                targets[k + 1][part, :] = value.astype(BF16)

    for member in range(GROUP):
        pl.when(place[0] == member)(lambda member=member: run(member))


def patched(before, halo, taps, offset_col):
    width = before.shape[1]
    count = taps.shape[0]
    extended = jnp.concatenate([halo[HALO - 8 :].astype(F32), jnp.zeros((8, width), F32)], axis=0)
    total = before
    for lag in range(1, count):
        shifted_rows = extended[8 - lag : 16 - lag]
        total = total + taps[count - 1 - lag : count - lag] * jnp.where(
            offset_col[0:8, 0:1] >= lag, shifted_rows, 0.0
        )
    return silu(total)


def intra_kernel(
    place, x, aux, halo, own, other, own_taps, other_taps, own_bias, other_bias, b, b_aux, x_taps,
    step, step_bias, decay_log, skip, offset, y, c_out, carry, bias, scores, columns, x_full, b_full,
):
    first = place[1] == 0
    block, channels = x.shape
    heads = step.shape[0]
    state_size = b.shape[1]
    count = x_taps.shape[0]
    half = block // 2
    time_step, rate_sum = rates(step[...], column(step_bias, heads), column(decay_log, heads))
    columns[...] = rate_sum.T
    offset_col = offset_columns(offset[...])

    x_full[...] = x[...]
    early = patched(aux[0:8, :], halo[:, 0:channels], x_taps[...], offset_col)
    x_full[0:16, :] = jnp.concatenate([early, x[0:16, :].astype(F32)[8:16]], axis=0).astype(BF16)
    own_halo = halo[:, channels : channels + state_size].astype(F32)
    other_halo = halo[:, channels + state_size :].astype(F32)
    b_full[...] = b[...]
    early = patched(b_aux[8:16, :], jnp.where(first, own_halo, other_halo), b_aux[0:count, :], offset_col)
    b_full[0:16, :] = jnp.concatenate([early, b[0:16, :].astype(F32)[8:16]], axis=0).astype(BF16)
    c_taps = jnp.where(first, other_taps[...], own_taps[...])
    c_bias = jnp.where(first, other_bias[...], own_bias[...])
    c_source = jnp.where(first, other[...].astype(F32), own[...].astype(F32)).astype(BF16)
    before = convolve(c_source, c_taps, c_bias, lag_matrices(offset_col, count))
    c_value = silu(before)
    early = patched(before[0:8], jnp.where(first, other_halo, own_halo), c_taps, offset_col)
    c_out[...] = c_value.astype(BF16)
    c_out[0:16, :] = jnp.concatenate([early, c_value[8:16]], axis=0).astype(BF16)

    row = iota((block, LANES), 0)
    for left in range(0, block, LANES):
        gap = row - (iota((block, LANES), 1) + left)
        linked = jnp.logical_and(gap >= 0, offset_col >= gap.astype(F32))
        bias[:, left : left + LANES] = jnp.where(linked, 0.0, NEG)
    scores[...] = dot(c_out[...], b_full[...], ((1,), (1,)))
    reach = rate_sum - jnp.log(time_step)
    starts = iota(rate_sum.shape, 1) + 1
    factor = turned(jnp.where(offset[...] >= starts, jnp.exp(rate_sum), 0.0))
    width = channels // GROUP
    for k in range(GROUP):
        carry[:, k * width : (k + 1) * width] = spread(factor, k * width, width)
    lane = iota((1, LANES), 1)
    per_tile = LANES // HEADDIM
    for tile in range(heads // per_tile):
        cols = slice(tile * LANES, (tile + 1) * LANES)
        skip_row = jnp.zeros((1, LANES), F32)
        for k in range(per_tile):
            skip_row = jnp.where(lane // HEADDIM == k, skip[tile * per_tile + k], skip_row)
        for top in range(0, block, half):
            part = slice(top, top + half)
            seen = top + half
            value = skip_row * x_full[part, cols].astype(F32)
            for k in range(per_tile):
                h = tile * per_tile + k
                gap = columns[part, h : h + 1] - reach[h : h + 1, 0:seen] + bias[part, 0:seen]
                weights = (scores[part, 0:seen] * jnp.exp(gap)).astype(BF16)
                chosen = jnp.where(lane // HEADDIM == k, x_full[0:seen, cols], jnp.zeros((), BF16))
                value = value + dot(weights, chosen)
            y[part, cols] = value


def back_kernel(place, c, f0, f1, f2, f3, intra, carry, out):
    member = place[0]
    parts = (f0, f1, f2, f3)
    width = out.shape[1] // len(parts)
    for k, state in enumerate(parts):
        cols = pl.ds(pl.multiple_of((member ^ k) * width, width), width)
        value = intra[:, cols] + carry[:, cols] * dot(c[...], state[...])
        out[:, cols] = value.astype(BF16)


def exchange(array, mask):
    return lax.ppermute(array, "seq", [(i, i ^ mask) for i in range(lax.axis_size("seq"))])


def shifted(array, distance):
    count = lax.axis_size("seq")
    return lax.ppermute(array, "seq", [(i, i + distance) for i in range(count - distance)])


def scan_groups(total, groups):
    rows = total.shape[0] - TAIL
    last = shifted(total[rows:], GROUP)
    held, decay = total[:rows].astype(F32), decay_of(total[rows:].astype(F32))
    held = shifted(held, GROUP)
    decay = shifted(decay, GROUP)
    distance = 1
    while distance < groups:
        held = held + decay * shifted(held, GROUP * distance)
        decay = decay * shifted(decay, GROUP * distance)
        distance *= 2
    near_tail = jnp.concatenate([jnp.zeros((X_LAST_AT, last.shape[1]), BF16), last[X_LAST_AT:]], axis=0)
    near = jnp.concatenate([held.astype(BF16), near_tail], axis=0)
    odd = (lax.axis_index("seq") // GROUP) % 2 == 1
    nothing = jnp.zeros_like(near)
    return jnp.where(odd, near, nothing), jnp.where(odd, nothing, near), nothing


def on_device(
    ssm_input, bc_input, conv_taps, conv_bias, bc_taps, bc_bias,
    step_input, step_bias, decay_log, skip_gain, request_offset,
):
    block, channels = ssm_input.shape
    state_size = bc_input.shape[1]
    heads = step_input.shape[0]
    width = channels // GROUP
    groups = lax.axis_size("seq") // GROUP
    here = lax.axis_index("seq")
    place = jnp.stack([here % GROUP, lax.axis_index("head") % 2, here // GROUP]).astype(jnp.int32)
    smem = pl.BlockSpec(memory_space=pltpu.SMEM)
    vmem = pl.BlockSpec(memory_space=pltpu.VMEM)
    x_bias, offset_row, own_bias = conv_bias[None, :], request_offset[None, :], bc_bias[None, :]

    swap = [(i, i ^ 1) for i in range(lax.axis_size("head"))]
    other_bc, other_taps, other_bias = [lax.ppermute(part, "head", swap) for part in (bc_input, bc_taps, bc_bias)]
    other_bias = other_bias[None, :]

    x_main, gated, aux, passing = pl.pallas_call(
        channels_kernel,
        out_shape=[
            jax.ShapeDtypeStruct((block, channels), BF16),
            jax.ShapeDtypeStruct((block, channels), BF16),
            jax.ShapeDtypeStruct((24, channels), F32),
            jax.ShapeDtypeStruct((heads, LANES), F32),
        ],
        in_specs=[vmem] * 4 + [smem] * 2 + [vmem],
        out_specs=[vmem] * 4,
        compiler_params=PARAMS,
        name="channels",
    )(ssm_input, conv_taps, x_bias, step_input, step_bias, decay_log, offset_row)

    slice_shape = jax.ShapeDtypeStruct((state_size + TAIL, width), BF16)
    *slices, b_main, b_aux = pl.pallas_call(
        states_kernel,
        out_shape=[slice_shape] * GROUP
        + [jax.ShapeDtypeStruct((block, state_size), BF16), jax.ShapeDtypeStruct((16, state_size), F32)],
        in_specs=[smem] + [vmem] * 10,
        out_specs=[vmem] * (GROUP + 2),
        scratch_shapes=[pltpu.VMEM((state_size, block), BF16)],
        compiler_params=PARAMS,
        name="states",
    )(place, bc_input, other_bc, bc_taps, other_taps, own_bias, other_bias, gated, aux, passing, offset_row)
    first_row = block - HALO
    ends = jnp.concatenate([ssm_input[first_row:], bc_input[first_row:], other_bc[first_row:]], axis=1)
    ends, _ = lax.optimization_barrier((ends, slices[0]))
    halo = shifted(ends, 1)
    received = [slices[0]] + [exchange(slices[k], k) for k in (1, 2, 3)]

    direct = groups == GROUP
    if direct:
        earlier = jnp.zeros((TAIL, width), BF16)
    else:
        last = received[0]
        for k in (1, 2, 3):
            last = jnp.where((here % GROUP) ^ k == GROUP - 1, received[k], last)
        earlier = shifted(last[state_size:], GROUP)
    total = pl.pallas_call(
        lambda *refs: group_kernel(*refs, complete=not direct),
        out_shape=slice_shape,
        in_specs=[smem] + [vmem] * (GROUP + 4),
        out_specs=vmem,
        compiler_params=PARAMS,
        name="group",
    )(place, *received, earlier, conv_taps, x_bias, b_aux)
    total, halo = lax.optimization_barrier((total, halo))
    if direct:
        far = exchange(total, 2 * GROUP)
        pairs = [(GROUP + k, 2 * GROUP + k) for k in range(GROUP)]
        near_even = lax.ppermute(total, "seq", pairs + [(high, low) for low, high in pairs])
        near_odd = exchange(total, GROUP)
    else:
        near_odd, near_even, far = scan_groups(total, groups)

    entering = pl.pallas_call(
        entering_kernel,
        out_shape=[jax.ShapeDtypeStruct((state_size, width), BF16)] * GROUP,
        in_specs=[smem] + [vmem] * (GROUP + 6),
        out_specs=[vmem] * GROUP,
        compiler_params=PARAMS,
        name="entering",
    )(place, *received, near_odd, near_even, far, conv_taps, x_bias, b_aux)
    mine = [entering[0]] + [exchange(entering[k], k) for k in (1, 2, 3)]

    intra, c_conv, carry = pl.pallas_call(
        intra_kernel,
        out_shape=[
            jax.ShapeDtypeStruct((block, channels), F32),
            jax.ShapeDtypeStruct((block, state_size), BF16),
            jax.ShapeDtypeStruct((block, channels), F32),
        ],
        in_specs=[smem] + [vmem] * 13 + [smem] * 3 + [vmem],
        out_specs=[vmem] * 3,
        scratch_shapes=[
            pltpu.VMEM((block, block), F32),
            pltpu.VMEM((block, block), F32),
            pltpu.VMEM((block, heads), F32),
            pltpu.VMEM((block, channels), BF16),
            pltpu.VMEM((block, state_size), BF16),
        ],
        compiler_params=PARAMS,
        cost_estimate=pl.CostEstimate(flops=600_000_000, bytes_accessed=4_000_000, transcendentals=1_000_000),
        name="intra",
    )(
        place, x_main, aux, halo, bc_input, other_bc, bc_taps, other_taps, own_bias, other_bias, b_main, b_aux,
        conv_taps, step_input, step_bias, decay_log, skip_gain, offset_row,
    )
    return pl.pallas_call(
        back_kernel,
        out_shape=jax.ShapeDtypeStruct((block, channels), BF16),
        in_specs=[smem] + [vmem] * (GROUP + 3),
        out_specs=vmem,
        compiler_params=PARAMS,
        name="back",
    )(place, c_conv, *mine, intra, carry)


def solution(mesh):
    return jax.shard_map(
        on_device,
        mesh=mesh,
        in_specs=(
            P("seq", "head"),
            P("seq", "head"),
            P(None, "head"),
            P("head"),
            P(None, "head"),
            P("head"),
            P("head", "seq"),
            P("head"),
            P("head"),
            P("head"),
            P("seq"),
        ),
        out_specs=P("seq", "head"),
        check_vma=False,
    )
```

time: 315 us -> 43.5 us (0.14)
  the two profiles are of different devices: /device:TPU:24 before, /device:TPU:16 now
where the time goes in v2:
time: 43.5 us; the launch traced here: 43.1 us
  starting transfers between devices  16.2 us (37%)
  waiting for transfers between devices  14.2 us (33%)
  Pallas kernels  8.74 us (20%)
  local copies, waits for them, and re-layouts  3.81 us (9%)
    ppermute x8, waiting for transfers between devices, exchange(): lax.ppermute(array, 'seq', [(i, i ^ mask) for i in range(lax.axis_size('s...  9.25 us
    ppermute x8, starting transfers between devices, exchange(): lax.ppermute(array, 'seq', [(i, i ^ mask) for i in range(lax.axis_size('s...  7.29 us
    ppermute x1, starting transfers between devices, on_device(): lax.ppermute(total, 'seq', pairs + [(high, low) for low, high in pairs])  4.97 us
    ppermute x1, waiting for transfers between devices, on_device(): lax.ppermute(total, 'seq', pairs + [(high, low) for low, high in pairs])  4.9 us
    ppermute x1, starting transfers between devices, shifted(): lax.ppermute(array, 'seq', [(i, i + distance) for i in range(count - dist...  3.4 us
    unnamed x22, local copies, waits for them, and re-layouts  3.1 us
    pallas_call x1, Pallas kernels, on_device(): pl.pallas_call(intra_kernel, out_shape=[jax.ShapeDtypeStruct((block, chan...  2.09 us
    pallas_call x1, Pallas kernels, on_device(): pl.pallas_call(back_kernel, out_shape=jax.ShapeDtypeStruct((block, channe...  1.67 us
  transfers between devices with their start and end apart: 13, of which 5 were waited for; matrix products, arithmetic and copies ran while one was open for 2% of the time, Pallas kernels for 11%

profile of v2, /device:TPU:16, one launch (start us, length us, event | category | flops | bytes accessed | tf_op | source)
XLA Modules:
  0.0 43.1 jit_solution(5984163206327089248)
XLA Ops:
  0.0 0.5 %collective-permute-start.2 = (f32[256]{0:T(256)}, f32[256]{0:T(256)S(1)}, u32[]{:S(2)}, u32[]{:S(2)}) collective-permute-start(f32[256]{0:T(256)} %param.16), channel_id=1, source_target_pairs={{0,1},{1,0},{2,3},{3,2},{4,5},{5,4},{6,7},{7,6},{8,9},{9,8},{10,11... | collective-permute-start | bytes 3080 | tf_op jit(solution)/shard_map/ppermute | solution.py:459
  0.5 0.1 pad_add_fusion.place.refs_0_
  0.6 0.7 %slice.10 = bf16[16,256]{1,0:T(8,128)(2,1)S(1)} slice(bf16[256,256]{1,0:T(8,128)(2,1)} %own.3), slice={[240:256], [0:256]} | slice | bytes 16384 | tf_op jit(solution)/shard_map/slice | solution.py:488
  1.3 0.0 copy-start.6
  1.3 0.0 copy-start.8
  1.3 0.7 %copy-done.2 = f32[4,1024]{1,0:T(4,128)S(1)} copy-done((f32[4,1024]{1,0:T(4,128)S(1)}, f32[4,1024]{1,0:T(4,128)}, u32[]{:S(2)}) %copy-start.2) | copy-done | bytes 16408
  2.0 0.0 copy-done.4
  2.1 1.0 %copy-done = bf16[256,1024]{1,0:T(8,128)(2,1)S(1)} copy-done((bf16[256,1024]{1,0:T(8,128)(2,1)S(1)}, bf16[256,1024]{1,0:T(8,128)(2,1)}, u32[]{:S(2)}) %copy-start) | copy-done | bytes 524312
  3.1 1.6 %channels.1 = (bf16[256,1024]{1,0:T(8,128)(2,1)S(1)}, bf16[256,1024]{1,0:T(8,128)(2,1)S(1)}, f32[24,1024]{1,0:T(8,128)S(1)}, f32[16,128]{1,0:T(8,128)S(1)}) custom-call(bf16[256,1024]{1,0:T(8,128)(2,1)S(1)} %copy-done, f32[4,1024]{1,0:T(4,128)S(1)} %copy-done.2, f32[1,1024]{1,0:T(1,128)S(1)} %bitcast.7, f32[16,256]{1,0:T(8,128)S(1)} %copy-done.4, ...), custom_call_target="tpu_custom_call" | custom-call | tf_op jit(solution)/shard_map/channels/pallas_call | solution.py:462
  4.8 0.7 %copy-done.5 = f32[4,256]{1,0:T(4,128)S(1)} copy-done((f32[4,256]{1,0:T(4,128)S(1)}, f32[4,256]{1,0:T(4,128)}, u32[]{:S(2)}) %copy-start.5) | copy-done | bytes 4120
  5.4 0.0 copy-done.7
  5.4 1.2 %states.1 = (bf16[272,256]{1,0:T(8,128)(2,1)S(1)}, bf16[272,256]{1,0:T(8,128)(2,1)S(1)}, bf16[272,256]{1,0:T(8,128)(2,1)S(1)}, bf16[272,256]{1,0:T(8,128)(2,1)S(...) custom-call(s32[3]{0:T(128)S(1)} %pad_add_fusion.place.refs_0_, bf16[256,256]{1,0:T(8,128)(2,1)S(1)} %copy-done.1, ...), custom_call_target="tpu_custom_call" | custom-call | tf_op jit(solution)/shard_map/states/pallas_call | solution.py:477
  6.6 1.6 %collective-permute-start.3 = (bf16[272,256]{1,0:T(8,128)(2,1)S(1)}, bf16[272,256]{1,0:T(8,128)(2,1)S(1)}, u32[]{:S(2)}, u32[]{:S(2)}) collective-permute-start(bf16[272,256]{1,0:T(8,128)(2,1)S(1)} %get-tuple-element.30), channel_id=1, source_target_pairs={{0,2},{2,0},{4,6},{6,4},{8,10},{10,8},{12,14},{14,12},{16,18},{18,... | collective-permute-start | bytes 417800 | tf_op jit(solution)/shard_map/ppermute | solution.py:417
  8.2 1.5 %collective-permute-start.4 = (bf16[272,256]{1,0:T(8,128)(2,1)S(1)}, bf16[272,256]{1,0:T(8,128)(2,1)S(1)}, u32[]{:S(2)}, u32[]{:S(2)}) collective-permute-start(bf16[272,256]{1,0:T(8,128)(2,1)S(1)} %get-tuple-element.31), channel_id=1, source_target_pairs={{0,4},{2,6},{4,0},{6,2},{8,12},{10,14},{12,8},{14,10},{16,20},{18,... | collective-permute-start | bytes 417800 | tf_op jit(solution)/shard_map/ppermute | solution.py:417
  9.7 0.5 %collective-permute-start.5 = (bf16[272,256]{1,0:T(8,128)(2,1)S(1)}, bf16[272,256]{1,0:T(8,128)(2,1)S(1)}, u32[]{:S(2)}, u32[]{:S(2)}) collective-permute-start(bf16[272,256]{1,0:T(8,128)(2,1)S(1)} %get-tuple-element.32), channel_id=1, source_target_pairs={{0,6},{2,4},{4,2},{6,0},{8,14},{10,12},{12,10},{14,8},{16,22},{18,... | collective-permute-start | bytes 417800 | tf_op jit(solution)/shard_map/ppermute | solution.py:417
  10.2 3.4 %collective-permute-start.6 = (bf16[16,1536]{1,0:T(8,128)(2,1)S(1)}, bf16[16,1536]{1,0:T(8,128)(2,1)S(1)}, u32[]{:S(2)}, u32[]{:S(2)}) collective-permute-start(bf16[16,1536]{1,0:T(8,128)(2,1)S(1)} %pad_maximum_fusion), channel_id=1, source_target_pairs={{0,2},{2,4},{4,6},{6,8},{8,10},{10,12},{12,14},{14,16},{16,18},{18... | collective-permute-start | bytes 147464 | tf_op jit(solution)/shard_map/ppermute | solution.py:422
  13.6 4.3 %collective-permute-done.4.refs_3_.r2 = bf16[272,256]{1,0:T(8,128)(2,1)S(1)} collective-permute-done((bf16[272,256]{1,0:T(8,128)(2,1)S(1)}, bf16[272,256]{1,0:T(8,128)(2,1)S(1)}, u32[]{:S(2)}, u32[]{:S(2)}) %collective-permute-start.4) | collective-permute-done | bytes 139296 | tf_op jit(solution)/shard_map/ppermute | solution.py:417
  17.9 1.0 %group.1 = bf16[272,256]{1,0:T(8,128)(2,1)S(1)} custom-call(s32[3]{0:T(128)S(1)} %pad_add_fusion.place.refs_0_, bf16[272,256]{1,0:T(8,128)(2,1)S(1)} %get-tuple-element.29.refs_1_.r0, bf16[272,256]{1,0:T(8,128)(2,1)S(1)} %collective-permute-done.3.refs_2_.r1, bf16[272,256]{1,0:T(8,128)(2,1)S(1)} %collective-permute-done.4.refs_3_.r2, ...), custom_call_target="tpu_custom_call" | custom-call | tf_op jit(solution)/shard_map/group/pallas_call | solution.py:501
  18.9 0.1 collective-permute-start.9
  18.9 5.0 %collective-permute-start.8 = (bf16[272,256]{1,0:T(8,128)(2,1)S(1)}, bf16[272,256]{1,0:T(8,128)(2,1)S(1)}, u32[]{:S(2)}, u32[]{:S(2)}) collective-permute-start(bf16[272,256]{1,0:T(8,128)(2,1)S(1)} %group.1), channel_id=1, source_target_pairs={{8,16},{10,18},{12,20},{14,22},{16,8},{18,10},{20,12},{22,14},{9,1... | collective-permute-start | bytes 417800 | tf_op jit(solution)/shard_map/ppermute | solution.py:513
  23.9 0.1 collective-permute-start.7
  24.0 1.5 %collective-permute-done.9.far = bf16[272,256]{1,0:T(8,128)(2,1)S(1)} collective-permute-done((bf16[272,256]{1,0:T(8,128)(2,1)S(1)}, bf16[272,256]{1,0:T(8,128)(2,1)S(1)}, u32[]{:S(2)}, u32[]{:S(2)}) %collective-permute-start.9) | collective-permute-done | bytes 139296 | tf_op jit(solution)/shard_map/ppermute | solution.py:417
  25.5 4.9 %collective-permute-done.8.near_even = bf16[272,256]{1,0:T(8,128)(2,1)S(1)} collective-permute-done((bf16[272,256]{1,0:T(8,128)(2,1)S(1)}, bf16[272,256]{1,0:T(8,128)(2,1)S(1)}, u32[]{:S(2)}, u32[]{:S(2)}) %collective-permute-start.8) | collective-permute-done | bytes 139296 | tf_op jit(solution)/shard_map/ppermute | solution.py:513
  30.4 1.2 %entering.1 = (bf16[256,256]{1,0:T(8,128)(2,1)S(1)}, bf16[256,256]{1,0:T(8,128)(2,1)S(1)}, bf16[256,256]{1,0:T(8,128)(2,1)S(1)}, bf16[256,256]{1,0:T(8,128)(2,1)S(1)}) custom-call(s32[3]{0:T(128)S(1)} %pad_add_fusion.place.refs_0_, bf16[272,256]{1,0:T(8,128)(2,1)S(1)} %get-tuple-element.29.refs_1_.r0, ...), custom_call_target="tpu_custom_call" | custom-call | tf_op jit(solution)/shard_map/entering/pallas_call | solution.py:518
  31.7 1.1 %collective-permute-start.10 = (bf16[256,256]{1,0:T(8,128)(2,1)S(1)}, bf16[256,256]{1,0:T(8,128)(2,1)S(1)}, u32[]{:S(2)}, u32[]{:S(2)}) collective-permute-start(bf16[256,256]{1,0:T(8,128)(2,1)S(1)} %get-tuple-element.40), channel_id=1, source_target_pairs={{0,2},{2,0},{4,6},{6,4},{8,10},{10,8},{12,14},{14,12},{16,18},{18,... | collective-permute-start | bytes 393224 | tf_op jit(solution)/shard_map/ppermute | solution.py:417
  32.8 1.1 %collective-permute-start.11 = (bf16[256,256]{1,0:T(8,128)(2,1)S(1)}, bf16[256,256]{1,0:T(8,128)(2,1)S(1)}, u32[]{:S(2)}, u32[]{:S(2)}) collective-permute-start(bf16[256,256]{1,0:T(8,128)(2,1)S(1)} %get-tuple-element.41), channel_id=1, source_target_pairs={{0,4},{2,6},{4,0},{6,2},{8,12},{10,14},{12,8},{14,10},{16,20},{18,... | collective-permute-start | bytes 393224 | tf_op jit(solution)/shard_map/ppermute | solution.py:417
  33.9 1.4 %collective-permute-start.12 = (bf16[256,256]{1,0:T(8,128)(2,1)S(1)}, bf16[256,256]{1,0:T(8,128)(2,1)S(1)}, u32[]{:S(2)}, u32[]{:S(2)}) collective-permute-start(bf16[256,256]{1,0:T(8,128)(2,1)S(1)} %get-tuple-element.42), channel_id=1, source_target_pairs={{0,6},{2,4},{4,2},{6,0},{8,14},{10,12},{12,10},{14,8},{16,22},{18,... | collective-permute-start | bytes 393224 | tf_op jit(solution)/shard_map/ppermute | solution.py:417
  35.3 0.7 %copy-done.10 = f32[16]{0:T(128)S(1)} copy-done((f32[16]{0:T(128)S(1)}, f32[16]{0:T(128)}, u32[]{:S(2)}) %copy-start.10) | copy-done | bytes 88
  35.9 2.1 %intra.1 = (f32[256,1024]{1,0:T(8,128)S(1)}, bf16[256,256]{1,0:T(8,128)(2,1)S(1)}, f32[256,1024]{1,0:T(8,128)S(1)}) custom-call(s32[3]{0:T(128)S(1)} %pad_add_fusion.place.refs_0_, bf16[256,1024]{1,0:T(8,128)(2,1)S(1)} %get-tuple-element.25.x, f32[24,1024]{1,0:T(8,128)S(1)} %get-tuple-element.26.aux, bf16[16,1536]{1,0:T(8,128)(2,1)S(1)} %collective-permute-done.6.halo, ...), custom_call_target="tpu_custom_call" | custom-call | flops 600000000 | bytes 4000000 | tf_op jit(solution)/shard_map/intra/pallas_call | solution.py:528
  38.0 1.6 %collective-permute-done.11.f2 = bf16[256,256]{1,0:T(8,128)(2,1)S(1)} collective-permute-done((bf16[256,256]{1,0:T(8,128)(2,1)S(1)}, bf16[256,256]{1,0:T(8,128)(2,1)S(1)}, u32[]{:S(2)}, u32[]{:S(2)}) %collective-permute-start.11) | collective-permute-done | bytes 131104 | tf_op jit(solution)/shard_map/ppermute | solution.py:417
  39.6 1.8 %collective-permute-done.12.f3 = bf16[256,256]{1,0:T(8,128)(2,1)S(1)} collective-permute-done((bf16[256,256]{1,0:T(8,128)(2,1)S(1)}, bf16[256,256]{1,0:T(8,128)(2,1)S(1)}, u32[]{:S(2)}, u32[]{:S(2)}) %collective-permute-start.12) | collective-permute-done | bytes 131104 | tf_op jit(solution)/shard_map/ppermute | solution.py:417
  41.5 1.7 %back.1 = bf16[256,1024]{1,0:T(8,128)(2,1)} custom-call(s32[3]{0:T(128)S(1)} %pad_add_fusion.place.refs_0_, bf16[256,256]{1,0:T(8,128)(2,1)S(1)} %get-tuple-element.37.c, bf16[256,256]{1,0:T(8,128)(2,1)S(1)} %get-tuple-element.39.f0, bf16[256,256]{1,0:T(8,128)(2,1)S(1)} %collective-permute-done.10.f1, bf16[256,256]{1,0:T(8,128)(2,1)S(1)} %collective-permute-done.11.f2, ...), custom_call_target="tpu_custom_call" | custom-call | tf_op jit(solution)/shard_map/back/pallas_call | solution.py:551
  (29 shorter events, 0.1 us)
Async XLA Ops:
  0.0 4.7 %collective-permute-start = (bf16[256,256]{1,0:T(8,128)(2,1)}, bf16[256,256]{1,0:T(8,128)(2,1)S(1)}, u32[]{:S(2)}, u32[]{:S(2)}) collective-permute-start(bf16[256,256]{1,0:T(8,128)(2,1)} %own.3), channel_id=1, source_target_pairs={{0,1},{1,0},{2,3},{3,2},{4,5},{5,4},{6,7},{7,6},{8,9},{9,8},{10,11... | collective-permute-start | bytes 393224 | tf_op jit(solution)/shard_map/ppermute | solution.py:459
  0.0 4.7 %collective-permute-start.2 = (f32[256]{0:T(256)}, f32[256]{0:T(256)S(1)}, u32[]{:S(2)}, u32[]{:S(2)}) collective-permute-start(f32[256]{0:T(256)} %param.16), channel_id=1, source_target_pairs={{0,1},{1,0},{2,3},{3,2},{4,5},{5,4},{6,7},{7,6},{8,9},{9,8},{10,11... | collective-permute-start | bytes 3080 | tf_op jit(solution)/shard_map/ppermute | solution.py:459
  0.5 4.2 %collective-permute-start.1 = (f32[4,256]{1,0:T(4,128)}, f32[4,256]{1,0:T(4,128)S(1)}, u32[]{:S(2)}, u32[]{:S(2)}) collective-permute-start(f32[4,256]{1,0:T(4,128)} %own_taps.3), channel_id=1, source_target_pairs={{0,1},{1,0},{2,3},{3,2},{4,5},{5,4},{6,7},{7,6},{8,9},{9,8},{10,11... | collective-permute-start | bytes 12296 | tf_op jit(solution)/shard_map/ppermute | solution.py:459
  1.3 0.7 %copy-start.2 = (f32[4,1024]{1,0:T(4,128)S(1)}, f32[4,1024]{1,0:T(4,128)}, u32[]{:S(2)}) copy-start(f32[4,1024]{1,0:T(4,128)} %x_taps.3) | copy-start | bytes 49156
  1.3 0.7 %copy-start.3 = (f32[1024]{0:T(1024)S(1)}, f32[1024]{0:T(1024)}, u32[]{:S(2)}) copy-start(f32[1024]{0:T(1024)} %param.14) | copy-start | bytes 12292
  1.3 0.7 %copy-start.4 = (f32[16,256]{1,0:T(8,128)S(1)}, f32[16,256]{1,0:T(8,128)}, u32[]{:S(2)}) copy-start(f32[16,256]{1,0:T(8,128)} %step.3) | copy-start | bytes 49156
  1.3 0.7 %copy-start.9 = (f32[16]{0:T(128)S(1)}, f32[16]{0:T(128)}, u32[]{:S(2)}) copy-start(f32[16]{0:T(128)} %decay_log.3) | copy-start | bytes 196
  1.3 0.7 %copy-start.6 = (s32[256]{0:T(256)S(1)}, s32[256]{0:T(256)}, u32[]{:S(2)}) copy-start(s32[256]{0:T(256)} %param.21) | copy-start | bytes 3076
  1.3 0.7 %copy-start.8 = (f32[16]{0:T(128)S(1)}, f32[16]{0:T(128)}, u32[]{:S(2)}) copy-start(f32[16]{0:T(128)} %step_bias.3) | copy-start | bytes 196
  2.0 1.0 %copy-start = (bf16[256,1024]{1,0:T(8,128)(2,1)S(1)}, bf16[256,1024]{1,0:T(8,128)(2,1)}, u32[]{:S(2)}) copy-start(bf16[256,1024]{1,0:T(8,128)(2,1)} %x.1) | copy-start | bytes 1572868
  3.1 1.7 %copy-start.1 = (bf16[256,256]{1,0:T(8,128)(2,1)S(1)}, bf16[256,256]{1,0:T(8,128)(2,1)}, u32[]{:S(2)}) copy-start(bf16[256,256]{1,0:T(8,128)(2,1)} %own.3) | copy-start | bytes 393220
  4.7 0.7 %copy-start.5 = (f32[4,256]{1,0:T(4,128)S(1)}, f32[4,256]{1,0:T(4,128)}, u32[]{:S(2)}) copy-start(f32[4,256]{1,0:T(4,128)} %own_taps.3) | copy-start | bytes 12292
  4.7 0.7 %copy-start.7 = (f32[256]{0:T(256)S(1)}, f32[256]{0:T(256)}, u32[]{:S(2)}) copy-start(f32[256]{0:T(256)} %param.16) | copy-start | bytes 3076
  5.4 4.8 %slice-start = ((bf16[256,1024]{1,0:T(8,128)(2,1)}), bf16[16,1024]{1,0:T(8,128)(2,1)S(1)}, s32[]{:S(2)}) async-start(bf16[256,1024]{1,0:T(8,128)(2,1)} %x.1), calls=%async_computation | async-start | bytes 65536 | tf_op jit(solution)/shard_map/slice | solution.py:488
  6.6 7.0 %collective-permute-start.3 = (bf16[272,256]{1,0:T(8,128)(2,1)S(1)}, bf16[272,256]{1,0:T(8,128)(2,1)S(1)}, u32[]{:S(2)}, u32[]{:S(2)}) collective-permute-start(bf16[272,256]{1,0:T(8,128)(2,1)S(1)} %get-tuple-element.30), channel_id=1, source_target_pairs={{0,2},{2,0},{4,6},{6,4},{8,10},{10,8},{12,14},{14,12},{16,18},{18,... | collective-permute-start | bytes 417800 | tf_op jit(solution)/shard_map/ppermute | solution.py:417
  8.2 9.7 %collective-permute-start.4 = (bf16[272,256]{1,0:T(8,128)(2,1)S(1)}, bf16[272,256]{1,0:T(8,128)(2,1)S(1)}, u32[]{:S(2)}, u32[]{:S(2)}) collective-permute-start(bf16[272,256]{1,0:T(8,128)(2,1)S(1)} %get-tuple-element.31), channel_id=1, source_target_pairs={{0,4},{2,6},{4,0},{6,2},{8,12},{10,14},{12,8},{14,10},{16,20},{18,... | collective-permute-start | bytes 417800 | tf_op jit(solution)/shard_map/ppermute | solution.py:417
  9.7 8.2 %collective-permute-start.5 = (bf16[272,256]{1,0:T(8,128)(2,1)S(1)}, bf16[272,256]{1,0:T(8,128)(2,1)S(1)}, u32[]{:S(2)}, u32[]{:S(2)}) collective-permute-start(bf16[272,256]{1,0:T(8,128)(2,1)S(1)} %get-tuple-element.32), channel_id=1, source_target_pairs={{0,6},{2,4},{4,2},{6,0},{8,14},{10,12},{12,10},{14,8},{16,22},{18,... | collective-permute-start | bytes 417800 | tf_op jit(solution)/shard_map/ppermute | solution.py:417
  10.2 8.7 %collective-permute-start.6 = (bf16[16,1536]{1,0:T(8,128)(2,1)S(1)}, bf16[16,1536]{1,0:T(8,128)(2,1)S(1)}, u32[]{:S(2)}, u32[]{:S(2)}) collective-permute-start(bf16[16,1536]{1,0:T(8,128)(2,1)S(1)} %pad_maximum_fusion), channel_id=1, source_target_pairs={{0,2},{2,4},{4,6},{6,8},{8,10},{10,12},{12,14},{14,16},{16,18},{18... | collective-permute-start | bytes 147464 | tf_op jit(solution)/shard_map/ppermute | solution.py:422
  18.9 6.7 %collective-permute-start.9 = (bf16[272,256]{1,0:T(8,128)(2,1)S(1)}, bf16[272,256]{1,0:T(8,128)(2,1)S(1)}, u32[]{:S(2)}, u32[]{:S(2)}) collective-permute-start(bf16[272,256]{1,0:T(8,128)(2,1)S(1)} %group.1), channel_id=1, source_target_pairs={{0,16},{2,18},{4,20},{6,22},{8,24},{10,26},{12,28},{14,30},{16,0},... | collective-permute-start | bytes 417800 | tf_op jit(solution)/shard_map/ppermute | solution.py:417
  18.9 11.5 %collective-permute-start.8 = (bf16[272,256]{1,0:T(8,128)(2,1)S(1)}, bf16[272,256]{1,0:T(8,128)(2,1)S(1)}, u32[]{:S(2)}, u32[]{:S(2)}) collective-permute-start(bf16[272,256]{1,0:T(8,128)(2,1)S(1)} %group.1), channel_id=1, source_target_pairs={{8,16},{10,18},{12,20},{14,22},{16,8},{18,10},{20,12},{22,14},{9,1... | collective-permute-start | bytes 417800 | tf_op jit(solution)/shard_map/ppermute | solution.py:513
  23.9 6.5 %collective-permute-start.7 = (bf16[272,256]{1,0:T(8,128)(2,1)S(1)}, bf16[272,256]{1,0:T(8,128)(2,1)S(1)}, u32[]{:S(2)}, u32[]{:S(2)}) collective-permute-start(bf16[272,256]{1,0:T(8,128)(2,1)S(1)} %group.1), channel_id=1, source_target_pairs={{0,8},{2,10},{4,12},{6,14},{8,0},{10,2},{12,4},{14,6},{16,24},{18,... | collective-permute-start | bytes 417800 | tf_op jit(solution)/shard_map/ppermute | solution.py:417
  31.7 6.3 %collective-permute-start.10 = (bf16[256,256]{1,0:T(8,128)(2,1)S(1)}, bf16[256,256]{1,0:T(8,128)(2,1)S(1)}, u32[]{:S(2)}, u32[]{:S(2)}) collective-permute-start(bf16[256,256]{1,0:T(8,128)(2,1)S(1)} %get-tuple-element.40), channel_id=1, source_target_pairs={{0,2},{2,0},{4,6},{6,4},{8,10},{10,8},{12,14},{14,12},{16,18},{18,... | collective-permute-start | bytes 393224 | tf_op jit(solution)/shard_map/ppermute | solution.py:417
  32.8 6.8 %collective-permute-start.11 = (bf16[256,256]{1,0:T(8,128)(2,1)S(1)}, bf16[256,256]{1,0:T(8,128)(2,1)S(1)}, u32[]{:S(2)}, u32[]{:S(2)}) collective-permute-start(bf16[256,256]{1,0:T(8,128)(2,1)S(1)} %get-tuple-element.41), channel_id=1, source_target_pairs={{0,4},{2,6},{4,0},{6,2},{8,12},{10,14},{12,8},{14,10},{16,20},{18,... | collective-permute-start | bytes 393224 | tf_op jit(solution)/shard_map/ppermute | solution.py:417
  33.9 7.6 %collective-permute-start.12 = (bf16[256,256]{1,0:T(8,128)(2,1)S(1)}, bf16[256,256]{1,0:T(8,128)(2,1)S(1)}, u32[]{:S(2)}, u32[]{:S(2)}) collective-permute-start(bf16[256,256]{1,0:T(8,128)(2,1)S(1)} %get-tuple-element.42), channel_id=1, source_target_pairs={{0,6},{2,4},{4,2},{6,0},{8,14},{10,12},{12,10},{14,8},{16,22},{18,... | collective-permute-start | bytes 393224 | tf_op jit(solution)/shard_map/ppermute | solution.py:417
  35.3 0.7 %copy-start.10 = (f32[16]{0:T(128)S(1)}, f32[16]{0:T(128)}, u32[]{:S(2)}) copy-start(f32[16]{0:T(128)} %skip.1) | copy-start | bytes 196

commit v3 on v2

--- a/solution.py
+++ b/solution.py
@@ -34,12 +34,22 @@
     return lax.broadcasted_iota(jnp.int32, shape, dim)
 
 
-def column(scalars, count):
-    row = iota((count, LANES), 0)
-    value = jnp.zeros((count, LANES), F32)
-    for k in range(count):
-        value = jnp.where(row == k, scalars[k], value)
-    return value[:, 0:1]
+def member_here():
+    return lax.axis_index("seq") % GROUP
+
+
+def group_here():
+    return lax.axis_index("seq") // GROUP
+
+
+def holds_b():
+    return lax.axis_index("head") % 2 == 0
+
+
+def column(row):
+    shape = (row.shape[1], row.shape[1])
+    wide = jnp.broadcast_to(row, shape)
+    return jnp.sum(jnp.where(iota(shape, 0) == iota(shape, 1), wide, 0.0), axis=1, keepdims=True)
 
 
 def spread(parts, first_channel, width):
@@ -90,44 +100,65 @@
     return total
 
 
-def channels_kernel(x, taps, bias, step, step_bias, decay_log, offset, x_out, gated, aux, passing_out):
+def channels_kernel(
+    x_hbm, taps_hbm, bias_hbm, own_hbm, own_taps_hbm, own_bias_hbm, step_hbm, offset_hbm,
+    step_bias_hbm, decay_hbm, skip_hbm,
+    x_out, gated, aux, passing_out, step_out, sums_out, taps, bias, own, own_taps, own_bias, offset,
+    x, step, step_bias, decay_log, skip, sems,
+):
     block, channels = x.shape
     count = taps.shape[0]
     heads = step.shape[0]
+    width = channels // GROUP
+    whole = [
+        (offset_hbm, offset), (step_hbm, step), (step_bias_hbm, step_bias), (decay_hbm, decay_log),
+        (skip_hbm, skip), (taps_hbm, taps), (bias_hbm, bias),
+    ]
+    later = [(own_hbm, own), (own_taps_hbm, own_taps), (own_bias_hbm, own_bias)]
+    parts = [slice(k * width, (k + 1) * width) for k in range(GROUP)]
+    pairs = whole + [(x_hbm.at[:, cols], x.at[:, cols]) for cols in parts] + later
+    copies = [pltpu.make_async_copy(*pair, sems.at[k]) for k, pair in enumerate(pairs)]
+    for copy in copies:
+        copy.start()
+    for copy in copies[: len(whole)]:
+        copy.wait()
     offset_col = offset_columns(offset[...])
     lags = lag_matrices(offset_col, count)
-    time_step, rate_sum = rates(step[...], column(step_bias, heads), column(decay_log, heads))
+    time_step, rate_sum = rates(step[...], column(step_bias[...]), column(decay_log[...]))
+    step_out[...] = time_step
+    sums_out[...] = rate_sum
     last_offset = offset[0, block - 1]
     place = iota(rate_sum.shape, 1)
     last = rate_sum[:, block - 1 : block]
     gate = jnp.exp(jnp.where(last_offset >= block - 1 - place, last - rate_sum, NEG)) * time_step
     passing = jnp.exp(last) * (last_offset >= block).astype(F32)
     passing_out[...] = jnp.broadcast_to(passing, passing_out.shape)
-    gate_early = turned(gate)[0:TAIL]
-    gate_late = turned(jnp.where(place >= count - 1, gate, 0.0))
-    width = channels // GROUP
-    for k in range(GROUP):
-        cols = slice(k * width, (k + 1) * width)
+    early_parts = turned(jnp.where(place == count - 1, column(skip[...]), gate))[0:TAIL]
+    late_parts = turned(jnp.where(place >= count - 1, gate, 0.0))
+    for k, cols in enumerate(parts):
+        copies[len(whole) + k].wait()
         source = x[:, cols]
         before = convolve(source, taps[:, cols], bias[:, cols], lags)
         value = silu(before).astype(BF16)
         x_out[:, cols] = value
-        gated[:, cols] = (value.astype(F32) * spread(gate_late, k * width, width)).astype(BF16)
+        gated[:, cols] = (value.astype(F32) * spread(late_parts, k * width, width)).astype(BF16)
         aux[0:8, cols] = before[0:8]
-        early = spread(gate_early, k * width, width)
+        early = spread(early_parts, k * width, width)
         first = source[0:TAIL].astype(F32)
         last_rows = source[block - TAIL : block].astype(F32)
         aux[8:24, cols] = jnp.concatenate(
-            [early[0:1], early[0:3], last_rows[TAIL - 3 :], first[0:3], jnp.zeros((TAIL - 10, width), F32)], axis=0
+            [early[3:4], early[0:3], last_rows[TAIL - 3 :], first[0:3], jnp.zeros((TAIL - 10, width), F32)], axis=0
         )
+    for copy in copies[len(whole) + GROUP :]:
+        copy.wait()
 
 
 def states_kernel(
-    place, own, other, own_taps, other_taps, own_bias, other_bias, gated, aux, passing, offset,
-    s0, s1, s2, s3, b_out, b_taps, turn,
+    own, other, own_taps, other_taps, own_bias, other_bias, gated, aux, passing, offset,
+    s0, s1, s2, s3, b_out, b_taps, ends, turn,
 ):
-    member = place[0]
-    first = place[1] == 0
+    member = member_here()
+    first = holds_b()
     block, state_size = own.shape
     count = own_taps.shape[0]
     lags = lag_matrices(offset_columns(offset[...]), count)
@@ -139,8 +170,15 @@
     b_out[...] = value.astype(BF16)
     turn[...] = value.T.astype(BF16)
     b_taps[...] = jnp.concatenate([taps, bias, jnp.zeros((8 - count - 1, state_size), F32), before[0:8]], axis=0)
-    width = gated.shape[1] // GROUP
+    channels = gated.shape[1]
+    width = channels // GROUP
     heads = passing.shape[0]
+    blank = HALO - 3
+    ends[:, 0:channels] = jnp.concatenate(
+        [jnp.zeros((blank, channels), F32), aux[8 + X_LAST_AT : 8 + X_LAST_AT + 3, :]], axis=0
+    ).astype(BF16)
+    ends[:, channels : channels + state_size] = own[block - HALO : block, :]
+    ends[:, channels + state_size :] = other[block - HALO : block, :]
     slice_heads = heads // GROUP
     lane = iota((heads, width), 1)
     head = iota((heads, width), 0)
@@ -228,7 +266,7 @@
     return b, x
 
 
-def group_kernel(place, r0, r1, r2, r3, earlier, x_taps, x_bias, b_taps, total, *, complete):
+def group_kernel(r0, r1, r2, r3, earlier, x_taps, x_bias, b_taps, total, *, complete):
     rows = r0.shape[0] - TAIL
     width = r0.shape[1]
     count = x_taps.shape[0]
@@ -272,13 +310,13 @@
         total[rows:, :] = tail.astype(BF16)
 
     for member in range(GROUP):
-        pl.when(place[0] == member)(lambda member=member: run(member))
+        pl.when(member_here() == member)(lambda member=member: run(member))
 
 
 def entering_kernel(
-    place, r0, r1, r2, r3, near_odd, near_even, far, x_taps, x_bias, b_taps, e0, e1, e2, e3
+    r0, r1, r2, r3, near_odd, near_even, far, x_taps, x_bias, b_taps, e0, e1, e2, e3
 ):
-    group = place[2]
+    group = group_here()
     odd = (group & 1) == 1
     one = jnp.ones((1, r0.shape[1]), F32)
     from_odd = jnp.where(odd, one, 0.0)
@@ -324,7 +362,7 @@
                 targets[k + 1][part, :] = value.astype(BF16)
 
     for member in range(GROUP):
-        pl.when(place[0] == member)(lambda member=member: run(member))
+        pl.when(member_here() == member)(lambda member=member: run(member))
 
 
 def patched(before, halo, taps, offset_col):
@@ -341,16 +379,16 @@
 
 
 def intra_kernel(
-    place, x, aux, halo, own, other, own_taps, other_taps, own_bias, other_bias, b, b_aux, x_taps,
-    step, step_bias, decay_log, skip, offset, y, c_out, carry, bias, scores, columns, x_full, b_full,
+    x, aux, halo, own, other, own_taps, other_taps, own_bias, other_bias, b, b_aux, x_taps,
+    step, sums, offset, y, c_out, carry, bias, scores, columns, x_full, b_full,
 ):
-    first = place[1] == 0
+    first = holds_b()
     block, channels = x.shape
     heads = step.shape[0]
     state_size = b.shape[1]
     count = x_taps.shape[0]
     half = block // 2
-    time_step, rate_sum = rates(step[...], column(step_bias, heads), column(decay_log, heads))
+    time_step, rate_sum = step[...], sums[...]
     columns[...] = rate_sum.T
     offset_col = offset_columns(offset[...])
 
@@ -387,9 +425,7 @@
     per_tile = LANES // HEADDIM
     for tile in range(heads // per_tile):
         cols = slice(tile * LANES, (tile + 1) * LANES)
-        skip_row = jnp.zeros((1, LANES), F32)
-        for k in range(per_tile):
-            skip_row = jnp.where(lane // HEADDIM == k, skip[tile * per_tile + k], skip_row)
+        skip_row = aux[8:9, cols]
         for top in range(0, block, half):
             part = slice(top, top + half)
             seen = top + half
@@ -403,14 +439,19 @@
             y[part, cols] = value
 
 
-def back_kernel(place, c, f0, f1, f2, f3, intra, carry, out):
-    member = place[0]
-    parts = (f0, f1, f2, f3)
-    width = out.shape[1] // len(parts)
+def back_kernel(c, *refs, first):
+    *parts, intra, carry, out, held, sems = refs
+    member = member_here()
+    width = out.shape[1] // GROUP
+    copies = []
     for k, state in enumerate(parts):
-        cols = pl.ds(pl.multiple_of((member ^ k) * width, width), width)
+        cols = pl.ds(pl.multiple_of((member ^ (first + k)) * width, width), width)
         value = intra[:, cols] + carry[:, cols] * dot(c[...], state[...])
-        out[:, cols] = value.astype(BF16)
+        held[k] = value.astype(BF16)
+        copies.append(pltpu.make_async_copy(held.at[k], out.at[:, cols], sems.at[k]))
+        copies[-1].start()
+    for copy in copies:
+        copy.wait()
 
 
 def exchange(array, mask):
@@ -450,43 +491,66 @@
     width = channels // GROUP
     groups = lax.axis_size("seq") // GROUP
     here = lax.axis_index("seq")
-    place = jnp.stack([here % GROUP, lax.axis_index("head") % 2, here // GROUP]).astype(jnp.int32)
-    smem = pl.BlockSpec(memory_space=pltpu.SMEM)
+    hbm = pl.BlockSpec(memory_space=pltpu.HBM)
     vmem = pl.BlockSpec(memory_space=pltpu.VMEM)
-    x_bias, offset_row, own_bias = conv_bias[None, :], request_offset[None, :], bc_bias[None, :]
 
     swap = [(i, i ^ 1) for i in range(lax.axis_size("head"))]
     other_bc, other_taps, other_bias = [lax.ppermute(part, "head", swap) for part in (bc_input, bc_taps, bc_bias)]
     other_bias = other_bias[None, :]
 
-    x_main, gated, aux, passing = pl.pallas_call(
+    x_main, gated, aux, passing, time_step, rate_sum, x_taps, x_bias, own, own_taps, own_bias, offset = pl.pallas_call(
         channels_kernel,
         out_shape=[
             jax.ShapeDtypeStruct((block, channels), BF16),
             jax.ShapeDtypeStruct((block, channels), BF16),
             jax.ShapeDtypeStruct((24, channels), F32),
             jax.ShapeDtypeStruct((heads, LANES), F32),
+            jax.ShapeDtypeStruct((heads, block), F32),
+            jax.ShapeDtypeStruct((heads, block), F32),
+            jax.ShapeDtypeStruct(conv_taps.shape, F32),
+            jax.ShapeDtypeStruct((1, channels), F32),
+            jax.ShapeDtypeStruct(bc_input.shape, BF16),
+            jax.ShapeDtypeStruct(bc_taps.shape, F32),
+            jax.ShapeDtypeStruct((1, state_size), F32),
+            jax.ShapeDtypeStruct((1, block), jnp.int32),
         ],
-        in_specs=[vmem] * 4 + [smem] * 2 + [vmem],
-        out_specs=[vmem] * 4,
+        in_specs=[hbm] * 11,
+        out_specs=[vmem] * 12,
+        scratch_shapes=[
+            pltpu.VMEM((block, channels), BF16),
+            pltpu.VMEM((heads, block), F32),
+            pltpu.VMEM((1, heads), F32),
+            pltpu.VMEM((1, heads), F32),
+            pltpu.VMEM((1, heads), F32),
+            pltpu.SemaphoreType.DMA((10 + GROUP,)),
+        ],
         compiler_params=PARAMS,
         name="channels",
-    )(ssm_input, conv_taps, x_bias, step_input, step_bias, decay_log, offset_row)
+    )(
+        *[
+            pltpu.with_memory_space_constraint(array, pltpu.HBM)
+            for array in (
+                ssm_input, conv_taps, conv_bias[None, :], bc_input, bc_taps, bc_bias[None, :], step_input,
+                request_offset[None, :], step_bias[None, :], decay_log[None, :], skip_gain[None, :],
+            )
+        ]
+    )
 
     slice_shape = jax.ShapeDtypeStruct((state_size + TAIL, width), BF16)
-    *slices, b_main, b_aux = pl.pallas_call(
+    *slices, b_main, b_aux, ends = pl.pallas_call(
         states_kernel,
         out_shape=[slice_shape] * GROUP
-        + [jax.ShapeDtypeStruct((block, state_size), BF16), jax.ShapeDtypeStruct((16, state_size), F32)],
-        in_specs=[smem] + [vmem] * 10,
-        out_specs=[vmem] * (GROUP + 2),
+        + [
+            jax.ShapeDtypeStruct((block, state_size), BF16),
+            jax.ShapeDtypeStruct((16, state_size), F32),
+            jax.ShapeDtypeStruct((HALO, channels + 2 * state_size), BF16),
+        ],
+        in_specs=[vmem] * 10,
+        out_specs=[vmem] * (GROUP + 3),
         scratch_shapes=[pltpu.VMEM((state_size, block), BF16)],
         compiler_params=PARAMS,
         name="states",
-    )(place, bc_input, other_bc, bc_taps, other_taps, own_bias, other_bias, gated, aux, passing, offset_row)
-    first_row = block - HALO
-    ends = jnp.concatenate([ssm_input[first_row:], bc_input[first_row:], other_bc[first_row:]], axis=1)
-    ends, _ = lax.optimization_barrier((ends, slices[0]))
+    )(own, other_bc, own_taps, other_taps, own_bias, other_bias, gated, aux, passing, offset)
     halo = shifted(ends, 1)
     received = [slices[0]] + [exchange(slices[k], k) for k in (1, 2, 3)]
 
@@ -501,11 +565,11 @@
     total = pl.pallas_call(
         lambda *refs: group_kernel(*refs, complete=not direct),
         out_shape=slice_shape,
-        in_specs=[smem] + [vmem] * (GROUP + 4),
+        in_specs=[vmem] * (GROUP + 4),
         out_specs=vmem,
         compiler_params=PARAMS,
         name="group",
-    )(place, *received, earlier, conv_taps, x_bias, b_aux)
+    )(*received, earlier, x_taps, x_bias, b_aux)
     total, halo = lax.optimization_barrier((total, halo))
     if direct:
         far = exchange(total, 2 * GROUP)
@@ -518,11 +582,11 @@
     entering = pl.pallas_call(
         entering_kernel,
         out_shape=[jax.ShapeDtypeStruct((state_size, width), BF16)] * GROUP,
-        in_specs=[smem] + [vmem] * (GROUP + 6),
+        in_specs=[vmem] * (GROUP + 6),
         out_specs=[vmem] * GROUP,
         compiler_params=PARAMS,
         name="entering",
-    )(place, *received, near_odd, near_even, far, conv_taps, x_bias, b_aux)
+    )(*received, near_odd, near_even, far, x_taps, x_bias, b_aux)
     mine = [entering[0]] + [exchange(entering[k], k) for k in (1, 2, 3)]
 
     intra, c_conv, carry = pl.pallas_call(
@@ -532,7 +596,7 @@
             jax.ShapeDtypeStruct((block, state_size), BF16),
             jax.ShapeDtypeStruct((block, channels), F32),
         ],
-        in_specs=[smem] + [vmem] * 13 + [smem] * 3 + [vmem],
+        in_specs=[vmem] * 15,
         out_specs=[vmem] * 3,
         scratch_shapes=[
             pltpu.VMEM((block, block), F32),
@@ -545,17 +609,34 @@
         cost_estimate=pl.CostEstimate(flops=600_000_000, bytes_accessed=4_000_000, transcendentals=1_000_000),
         name="intra",
     )(
-        place, x_main, aux, halo, bc_input, other_bc, bc_taps, other_taps, own_bias, other_bias, b_main, b_aux,
-        conv_taps, step_input, step_bias, decay_log, skip_gain, offset_row,
+        x_main, aux, halo, own, other_bc, own_taps, other_taps, own_bias, other_bias, b_main, b_aux,
+        x_taps, time_step, rate_sum, offset,
     )
-    return pl.pallas_call(
-        back_kernel,
-        out_shape=jax.ShapeDtypeStruct((block, channels), BF16),
-        in_specs=[smem] + [vmem] * (GROUP + 3),
-        out_specs=vmem,
+    out_shape = jax.ShapeDtypeStruct((block, channels), BF16)
+    early = GROUP - 1
+    partial = pl.pallas_call(
+        lambda *refs: back_kernel(*refs, first=0),
+        out_shape=out_shape,
+        in_specs=[vmem] * (early + 3),
+        out_specs=hbm,
+        scratch_shapes=[pltpu.VMEM((early, block, width), BF16), pltpu.SemaphoreType.DMA((early,))],
         compiler_params=PARAMS,
         name="back",
-    )(place, c_conv, *mine, intra, carry)
+    )(c_conv, *mine[:early], intra, carry)
+
+    def last_slice(c, state, intra, carry, partial, out, held, sems):
+        back_kernel(c, state, intra, carry, out, held, sems, first=early)
+
+    return pl.pallas_call(
+        last_slice,
+        out_shape=out_shape,
+        in_specs=[vmem] * 4 + [hbm],
+        out_specs=hbm,
+        scratch_shapes=[pltpu.VMEM((1, block, width), BF16), pltpu.SemaphoreType.DMA((1,))],
+        input_output_aliases={4: 0},
+        compiler_params=PARAMS,
+        name="last",
+    )(c_conv, mine[early], intra, carry, partial)
 
 
 def solution(mesh):

time: 43.5 us -> 39 us (0.90)
  the two profiles are of different devices: /device:TPU:16 before, /device:TPU:22 now
where the time goes in v3:
time: 39 us; the launch traced here: 38.8 us
  starting transfers between devices  16 us (41%)
  waiting for transfers between devices  14.9 us (38%)
  Pallas kernels  7.8 us (20%)
    ppermute x8, waiting for transfers between devices, exchange(): lax.ppermute(array, 'seq', [(i, i ^ mask) for i in range(lax.axis_size('s...  9.69 us
    ppermute x8, starting transfers between devices, exchange(): lax.ppermute(array, 'seq', [(i, i ^ mask) for i in range(lax.axis_size('s...  7.52 us
    ppermute x1, waiting for transfers between devices, on_device(): lax.ppermute(total, 'seq', pairs + [(high, low) for low, high in pairs])  4.91 us
    ppermute x1, starting transfers between devices, on_device(): lax.ppermute(total, 'seq', pairs + [(high, low) for low, high in pairs])  4.59 us
    ppermute x1, starting transfers between devices, shifted(): lax.ppermute(array, 'seq', [(i, i + distance) for i in range(count - dist...  3.38 us
    pallas_call x1, Pallas kernels, on_device(): pl.pallas_call(channels_kernel, out_shape=[jax.ShapeDtypeStruct((block, c...  2.69 us
    pallas_call x1, Pallas kernels, on_device(): pl.pallas_call(intra_kernel, out_shape=[jax.ShapeDtypeStruct((block, chan...  1.53 us
    pallas_call x1, Pallas kernels, on_device(): pl.pallas_call(lambda *refs: back_kernel(*refs, first=0), out_shape=out_s...  1 us
  transfers between devices with their start and end apart: 13, of which 7 were waited for; matrix products, arithmetic and copies ran while one was open for 0% of the time, Pallas kernels for 14%

profile of v3, /device:TPU:22, one launch (start us, length us, event | category | flops | bytes accessed | tf_op | source)
XLA Modules:
  0.0 38.8 jit_solution(7365683001244968624)
XLA Ops:
  0.0 0.0 collective-permute-start
  0.0 0.5 %collective-permute-start.1 = (f32[4,256]{1,0:T(4,128)}, f32[4,256]{1,0:T(4,128)S(1)}, u32[]{:S(2)}, u32[]{:S(2)}) collective-permute-start(f32[4,256]{1,0:T(4,128)} %own_taps_hbm.1), channel_id=1, source_target_pairs={{0,1},{1,0},{2,3},{3,2},{4,5},{5,4},{6,7},{7,6},{8,9},{9,8},{10,11... | collective-permute-start | bytes 12296 | tf_op jit(solution)/shard_map/ppermute | solution.py:498
  0.5 0.0 collective-permute-start.2
  0.5 2.7 %channels.1 = (bf16[256,1024]{1,0:T(8,128)(2,1)S(1)}, bf16[256,1024]{1,0:T(8,128)(2,1)S(1)}, f32[24,1024]{1,0:T(8,128)S(1)}, f32[16,128]{1,0:T(8,128)S(1)}, f32[...) custom-call(bf16[256,1024]{1,0:T(8,128)(2,1)} %x_hbm.1, ...), custom_call_target="tpu_custom_call" | custom-call | tf_op jit(solution)/shard_map/channels/pallas_call | solution.py:501
  3.2 0.0 collective-permute-done.2
  3.2 0.0 collective-permute-done.1.other_taps
  3.2 0.0 collective-permute-done.other
  3.2 0.7 %states.1 = (bf16[272,256]{1,0:T(8,128)(2,1)S(1)}, bf16[272,256]{1,0:T(8,128)(2,1)S(1)}, bf16[272,256]{1,0:T(8,128)(2,1)S(1)}, bf16[272,256]{1,0:T(8,128)(2,1)S(...) custom-call(bf16[256,256]{1,0:T(8,128)(2,1)S(1)} %get-tuple-element.35.own, ...), custom_call_target="tpu_custom_call" | custom-call | tf_op jit(solution)/shard_map/states/pallas_call | solution.py:540
  3.9 0.6 %collective-permute-start.3 = (bf16[272,256]{1,0:T(8,128)(2,1)S(1)}, bf16[272,256]{1,0:T(8,128)(2,1)S(1)}, u32[]{:S(2)}, u32[]{:S(2)}) collective-permute-start(bf16[272,256]{1,0:T(8,128)(2,1)S(1)} %get-tuple-element.42), channel_id=1, source_target_pairs={{0,2},{2,0},{4,6},{6,4},{8,10},{10,8},{12,14},{14,12},{16,18},{18,... | collective-permute-start | bytes 417800 | tf_op jit(solution)/shard_map/ppermute | solution.py:458
  4.5 0.5 %collective-permute-start.4 = (bf16[272,256]{1,0:T(8,128)(2,1)S(1)}, bf16[272,256]{1,0:T(8,128)(2,1)S(1)}, u32[]{:S(2)}, u32[]{:S(2)}) collective-permute-start(bf16[272,256]{1,0:T(8,128)(2,1)S(1)} %get-tuple-element.43), channel_id=1, source_target_pairs={{0,4},{2,6},{4,0},{6,2},{8,12},{10,14},{12,8},{14,10},{16,20},{18,... | collective-permute-start | bytes 417800 | tf_op jit(solution)/shard_map/ppermute | solution.py:458
  5.0 2.4 %collective-permute-start.5 = (bf16[272,256]{1,0:T(8,128)(2,1)S(1)}, bf16[272,256]{1,0:T(8,128)(2,1)S(1)}, u32[]{:S(2)}, u32[]{:S(2)}) collective-permute-start(bf16[272,256]{1,0:T(8,128)(2,1)S(1)} %get-tuple-element.44), channel_id=1, source_target_pairs={{0,6},{2,4},{4,2},{6,0},{8,14},{10,12},{12,10},{14,8},{16,22},{18,... | collective-permute-start | bytes 417800 | tf_op jit(solution)/shard_map/ppermute | solution.py:458
  7.5 3.4 %collective-permute-start.6 = (bf16[16,1536]{1,0:T(8,128)(2,1)S(1)}, bf16[16,1536]{1,0:T(8,128)(2,1)S(1)}, u32[]{:S(2)}, u32[]{:S(2)}) collective-permute-start(bf16[16,1536]{1,0:T(8,128)(2,1)S(1)} %get-tuple-element.48), channel_id=1, source_target_pairs={{0,2},{2,4},{4,6},{6,8},{8,10},{10,12},{12,14},{14,16},{16,18},{18... | collective-permute-start | bytes 147464 | tf_op jit(solution)/shard_map/ppermute | solution.py:463
  10.8 0.0 collective-permute-done.3.refs_1_.r1
  10.9 2.3 %collective-permute-done.4.refs_2_.r2 = bf16[272,256]{1,0:T(8,128)(2,1)S(1)} collective-permute-done((bf16[272,256]{1,0:T(8,128)(2,1)S(1)}, bf16[272,256]{1,0:T(8,128)(2,1)S(1)}, u32[]{:S(2)}, u32[]{:S(2)}) %collective-permute-start.4) | collective-permute-done | bytes 139296 | tf_op jit(solution)/shard_map/ppermute | solution.py:458
  13.1 0.3 collective-permute-done.5.refs_3_.r3
  13.4 0.4 %group.1 = bf16[272,256]{1,0:T(8,128)(2,1)S(1)} custom-call(bf16[272,256]{1,0:T(8,128)(2,1)S(1)} %get-tuple-element.41.refs_0_.r0, bf16[272,256]{1,0:T(8,128)(2,1)S(1)} %collective-permute-done.3.refs_1_.r1, bf16[272,256]{1,0:T(8,128)(2,1)S(1)} %collective-permute-done.4.refs_2_.r2, bf16[272,256]{1,0:T(8,128)(2,1)S(1)} %collective-permute-done.5.refs_3_.r3, ...), custom_call_target="tpu_custom_call" | custom-call | tf_op jit(solution)/shard_map/group/pallas_call | solution.py:565
  13.8 0.3 collective-permute-done.6.halo
  14.1 0.3 collective-permute-start.9
  14.4 4.6 %collective-permute-start.8 = (bf16[272,256]{1,0:T(8,128)(2,1)S(1)}, bf16[272,256]{1,0:T(8,128)(2,1)S(1)}, u32[]{:S(2)}, u32[]{:S(2)}) collective-permute-start(bf16[272,256]{1,0:T(8,128)(2,1)S(1)} %group.1), channel_id=1, source_target_pairs={{8,16},{10,18},{12,20},{14,22},{16,8},{18,10},{20,12},{22,14},{9,1... | collective-permute-start | bytes 417800 | tf_op jit(solution)/shard_map/ppermute | solution.py:577
  19.0 0.1 collective-permute-start.7
  19.1 2.3 %collective-permute-done.9.far = bf16[272,256]{1,0:T(8,128)(2,1)S(1)} collective-permute-done((bf16[272,256]{1,0:T(8,128)(2,1)S(1)}, bf16[272,256]{1,0:T(8,128)(2,1)S(1)}, u32[]{:S(2)}, u32[]{:S(2)}) %collective-permute-start.9) | collective-permute-done | bytes 139296 | tf_op jit(solution)/shard_map/ppermute | solution.py:458
  21.4 4.9 %collective-permute-done.8.near_even = bf16[272,256]{1,0:T(8,128)(2,1)S(1)} collective-permute-done((bf16[272,256]{1,0:T(8,128)(2,1)S(1)}, bf16[272,256]{1,0:T(8,128)(2,1)S(1)}, u32[]{:S(2)}, u32[]{:S(2)}) %collective-permute-start.8) | collective-permute-done | bytes 139296 | tf_op jit(solution)/shard_map/ppermute | solution.py:577
  26.3 0.0 collective-permute-done.7.near_odd
  26.3 0.7 %entering.1 = (bf16[256,256]{1,0:T(8,128)(2,1)S(1)}, bf16[256,256]{1,0:T(8,128)(2,1)S(1)}, bf16[256,256]{1,0:T(8,128)(2,1)S(1)}, bf16[256,256]{1,0:T(8,128)(2,1)S(1)}) custom-call(bf16[272,256]{1,0:T(8,128)(2,1)S(1)} %get-tuple-element.41.refs_0_.r0, bf16[272,256]{1,0:T(8,128)(2,1)S(1)} %collective-permute-done.3.refs_1_.r1, ...), custom_call_target="tpu_custom_call" | custom-call | tf_op jit(solution)/shard_map/entering/pallas_call | solution.py:582
  27.0 2.0 %collective-permute-start.11 = (bf16[256,256]{1,0:T(8,128)(2,1)S(1)}, bf16[256,256]{1,0:T(8,128)(2,1)S(1)}, u32[]{:S(2)}, u32[]{:S(2)}) collective-permute-start(bf16[256,256]{1,0:T(8,128)(2,1)S(1)} %get-tuple-element.59), channel_id=1, source_target_pairs={{0,2},{2,0},{4,6},{6,4},{8,10},{10,8},{12,14},{14,12},{16,18},{18,... | collective-permute-start | bytes 393224 | tf_op jit(solution)/shard_map/ppermute | solution.py:458
  29.0 1.6 %collective-permute-start.10 = (bf16[256,256]{1,0:T(8,128)(2,1)S(1)}, bf16[256,256]{1,0:T(8,128)(2,1)S(1)}, u32[]{:S(2)}, u32[]{:S(2)}) collective-permute-start(bf16[256,256]{1,0:T(8,128)(2,1)S(1)} %get-tuple-element.55), channel_id=1, source_target_pairs={{0,6},{2,4},{4,2},{6,0},{8,14},{10,12},{12,10},{14,8},{16,22},{18,... | collective-permute-start | bytes 393224 | tf_op jit(solution)/shard_map/ppermute | solution.py:458
  30.6 1.5 %intra.1 = (f32[256,1024]{1,0:T(8,128)S(1)}, bf16[256,256]{1,0:T(8,128)(2,1)S(1)}, f32[256,1024]{1,0:T(8,128)S(1)}) custom-call(bf16[256,1024]{1,0:T(8,128)(2,1)S(1)} %get-tuple-element.33.x, f32[24,1024]{1,0:T(8,128)S(1)} %get-tuple-element.34.aux, bf16[16,1536]{1,0:T(8,128)(2,1)S(1)} %collective-permute-done.6.halo, ...), custom_call_target="tpu_custom_call" | custom-call | flops 600000000 | bytes 4000000 | tf_op jit(solution)/shard_map/intra/pallas_call | solution.py:592
  32.1 0.8 %collective-permute-done.11.refs_2_ = bf16[256,256]{1,0:T(8,128)(2,1)S(1)} collective-permute-done((bf16[256,256]{1,0:T(8,128)(2,1)S(1)}, bf16[256,256]{1,0:T(8,128)(2,1)S(1)}, u32[]{:S(2)}, u32[]{:S(2)}) %collective-permute-start.11) | collective-permute-done | bytes 131104 | tf_op jit(solution)/shard_map/ppermute | solution.py:458
  32.9 4.1 %collective-permute-done.12.refs_3_ = bf16[256,256]{1,0:T(8,128)(2,1)S(1)} collective-permute-done((bf16[256,256]{1,0:T(8,128)(2,1)S(1)}, bf16[256,256]{1,0:T(8,128)(2,1)S(1)}, u32[]{:S(2)}, u32[]{:S(2)}) %collective-permute-start.12) | collective-permute-done | bytes 131104 | tf_op jit(solution)/shard_map/ppermute | solution.py:458
  36.9 1.0 %back.1.partial = bf16[256,1024]{1,0:T(8,128)(2,1)} custom-call(bf16[256,256]{1,0:T(8,128)(2,1)S(1)} %get-tuple-element.53.refs_0_.c, bf16[256,256]{1,0:T(8,128)(2,1)S(1)} %get-tuple-element.58.refs_1_, bf16[256,256]{1,0:T(8,128)(2,1)S(1)} %collective-permute-done.11.refs_2_, bf16[256,256]{1,0:T(8,128)(2,1)S(1)} %collective-permute-done.12.refs_3_, ...), custom_call_target="tpu_custom_call" | custom-call | tf_op jit(solution)/shard_map/back/pallas_call | solution.py:617
  37.9 0.0 collective-permute-done.10.state
  37.9 0.9 %last.1 = bf16[256,1024]{1,0:T(8,128)(2,1)} custom-call(bf16[256,256]{1,0:T(8,128)(2,1)S(1)} %get-tuple-element.53.refs_0_.c, bf16[256,256]{1,0:T(8,128)(2,1)S(1)} %collective-permute-done.10.state, f32[256,1024]{1,0:T(8,128)S(1)} %get-tuple-element.56.refs_4_.intra, ...), custom_call_target="tpu_custom_call", output_to_operand_aliasing={{}: (4, {})} | custom-call | tf_op jit(solution)/shard_map/last/pallas_call | solution.py:630
  (2 shorter events, 0.0 us)
Async XLA Ops:
  0.0 3.2 %collective-permute-start = (bf16[256,256]{1,0:T(8,128)(2,1)}, bf16[256,256]{1,0:T(8,128)(2,1)S(1)}, u32[]{:S(2)}, u32[]{:S(2)}) collective-permute-start(bf16[256,256]{1,0:T(8,128)(2,1)} %own_hbm.1), channel_id=1, source_target_pairs={{0,1},{1,0},{2,3},{3,2},{4,5},{5,4},{6,7},{7,6},{8,9},{9,8},{10,11... | collective-permute-start | bytes 393224 | tf_op jit(solution)/shard_map/ppermute | solution.py:498
  0.0 3.2 %collective-permute-start.1 = (f32[4,256]{1,0:T(4,128)}, f32[4,256]{1,0:T(4,128)S(1)}, u32[]{:S(2)}, u32[]{:S(2)}) collective-permute-start(f32[4,256]{1,0:T(4,128)} %own_taps_hbm.1), channel_id=1, source_target_pairs={{0,1},{1,0},{2,3},{3,2},{4,5},{5,4},{6,7},{7,6},{8,9},{9,8},{10,11... | collective-permute-start | bytes 12296 | tf_op jit(solution)/shard_map/ppermute | solution.py:498
  0.5 2.7 %collective-permute-start.2 = (f32[256]{0:T(256)}, f32[256]{0:T(256)S(1)}, u32[]{:S(2)}, u32[]{:S(2)}) collective-permute-start(f32[256]{0:T(256)} %param.16), channel_id=1, source_target_pairs={{0,1},{1,0},{2,3},{3,2},{4,5},{5,4},{6,7},{7,6},{8,9},{9,8},{10,11... | collective-permute-start | bytes 3080 | tf_op jit(solution)/shard_map/ppermute | solution.py:498
  3.9 6.9 %collective-permute-start.3 = (bf16[272,256]{1,0:T(8,128)(2,1)S(1)}, bf16[272,256]{1,0:T(8,128)(2,1)S(1)}, u32[]{:S(2)}, u32[]{:S(2)}) collective-permute-start(bf16[272,256]{1,0:T(8,128)(2,1)S(1)} %get-tuple-element.42), channel_id=1, source_target_pairs={{0,2},{2,0},{4,6},{6,4},{8,10},{10,8},{12,14},{14,12},{16,18},{18,... | collective-permute-start | bytes 417800 | tf_op jit(solution)/shard_map/ppermute | solution.py:458
  4.5 8.6 %collective-permute-start.4 = (bf16[272,256]{1,0:T(8,128)(2,1)S(1)}, bf16[272,256]{1,0:T(8,128)(2,1)S(1)}, u32[]{:S(2)}, u32[]{:S(2)}) collective-permute-start(bf16[272,256]{1,0:T(8,128)(2,1)S(1)} %get-tuple-element.43), channel_id=1, source_target_pairs={{0,4},{2,6},{4,0},{6,2},{8,12},{10,14},{12,8},{14,10},{16,20},{18,... | collective-permute-start | bytes 417800 | tf_op jit(solution)/shard_map/ppermute | solution.py:458
  5.0 8.4 %collective-permute-start.5 = (bf16[272,256]{1,0:T(8,128)(2,1)S(1)}, bf16[272,256]{1,0:T(8,128)(2,1)S(1)}, u32[]{:S(2)}, u32[]{:S(2)}) collective-permute-start(bf16[272,256]{1,0:T(8,128)(2,1)S(1)} %get-tuple-element.44), channel_id=1, source_target_pairs={{0,6},{2,4},{4,2},{6,0},{8,14},{10,12},{12,10},{14,8},{16,22},{18,... | collective-permute-start | bytes 417800 | tf_op jit(solution)/shard_map/ppermute | solution.py:458
  7.5 6.6 %collective-permute-start.6 = (bf16[16,1536]{1,0:T(8,128)(2,1)S(1)}, bf16[16,1536]{1,0:T(8,128)(2,1)S(1)}, u32[]{:S(2)}, u32[]{:S(2)}) collective-permute-start(bf16[16,1536]{1,0:T(8,128)(2,1)S(1)} %get-tuple-element.48), channel_id=1, source_target_pairs={{0,2},{2,4},{4,6},{6,8},{8,10},{10,12},{12,14},{14,16},{16,18},{18... | collective-permute-start | bytes 147464 | tf_op jit(solution)/shard_map/ppermute | solution.py:463
  14.1 7.3 %collective-permute-start.9 = (bf16[272,256]{1,0:T(8,128)(2,1)S(1)}, bf16[272,256]{1,0:T(8,128)(2,1)S(1)}, u32[]{:S(2)}, u32[]{:S(2)}) collective-permute-start(bf16[272,256]{1,0:T(8,128)(2,1)S(1)} %group.1), channel_id=1, source_target_pairs={{0,16},{2,18},{4,20},{6,22},{8,24},{10,26},{12,28},{14,30},{16,0},... | collective-permute-start | bytes 417800 | tf_op jit(solution)/shard_map/ppermute | solution.py:458
  14.4 11.9 %collective-permute-start.8 = (bf16[272,256]{1,0:T(8,128)(2,1)S(1)}, bf16[272,256]{1,0:T(8,128)(2,1)S(1)}, u32[]{:S(2)}, u32[]{:S(2)}) collective-permute-start(bf16[272,256]{1,0:T(8,128)(2,1)S(1)} %group.1), channel_id=1, source_target_pairs={{8,16},{10,18},{12,20},{14,22},{16,8},{18,10},{20,12},{22,14},{9,1... | collective-permute-start | bytes 417800 | tf_op jit(solution)/shard_map/ppermute | solution.py:577
  19.0 7.3 %collective-permute-start.7 = (bf16[272,256]{1,0:T(8,128)(2,1)S(1)}, bf16[272,256]{1,0:T(8,128)(2,1)S(1)}, u32[]{:S(2)}, u32[]{:S(2)}) collective-permute-start(bf16[272,256]{1,0:T(8,128)(2,1)S(1)} %group.1), channel_id=1, source_target_pairs={{0,8},{2,10},{4,12},{6,14},{8,0},{10,2},{12,4},{14,6},{16,24},{18,... | collective-permute-start | bytes 417800 | tf_op jit(solution)/shard_map/ppermute | solution.py:458
  27.0 5.9 %collective-permute-start.11 = (bf16[256,256]{1,0:T(8,128)(2,1)S(1)}, bf16[256,256]{1,0:T(8,128)(2,1)S(1)}, u32[]{:S(2)}, u32[]{:S(2)}) collective-permute-start(bf16[256,256]{1,0:T(8,128)(2,1)S(1)} %get-tuple-element.59), channel_id=1, source_target_pairs={{0,2},{2,0},{4,6},{6,4},{8,10},{10,8},{12,14},{14,12},{16,18},{18,... | collective-permute-start | bytes 393224 | tf_op jit(solution)/shard_map/ppermute | solution.py:458
  29.0 7.9 %collective-permute-start.12 = (bf16[256,256]{1,0:T(8,128)(2,1)S(1)}, bf16[256,256]{1,0:T(8,128)(2,1)S(1)}, u32[]{:S(2)}, u32[]{:S(2)}) collective-permute-start(bf16[256,256]{1,0:T(8,128)(2,1)S(1)} %get-tuple-element.60), channel_id=1, source_target_pairs={{0,4},{2,6},{4,0},{6,2},{8,12},{10,14},{12,8},{14,10},{16,20},{18,... | collective-permute-start | bytes 393224 | tf_op jit(solution)/shard_map/ppermute | solution.py:458
  29.0 9.0 %collective-permute-start.10 = (bf16[256,256]{1,0:T(8,128)(2,1)S(1)}, bf16[256,256]{1,0:T(8,128)(2,1)S(1)}, u32[]{:S(2)}, u32[]{:S(2)}) collective-permute-start(bf16[256,256]{1,0:T(8,128)(2,1)S(1)} %get-tuple-element.55), channel_id=1, source_target_pairs={{0,6},{2,4},{4,2},{6,0},{8,14},{10,12},{12,10},{14,8},{16,22},{18,... | collective-permute-start | bytes 393224 | tf_op jit(solution)/shard_map/ppermute | solution.py:458

commit v4 on v3

--- a/solution.py
+++ b/solution.py
@@ -100,30 +100,49 @@
     return total
 
 
+def quarter(k, width):
+    return pl.ds(pl.multiple_of((member_here() ^ k) * width, width), width)
+
+
+def channel_slice(k, slot, x, taps, bias, lags, late_parts, early_parts, x_out, gated, aux):
+    block = x.shape[0]
+    width = x.shape[1] // GROUP
+    cols, to = quarter(k, width), slice(slot * width, (slot + 1) * width)
+    source = x[:, cols]
+    before = convolve(source, taps[:, cols], bias[:, cols], [lags[lag] for lag in range(lags.shape[0])])
+    value = silu(before).astype(BF16)
+    x_out[:, to] = value
+    first_channel = (member_here() ^ k) * width
+    gated[:, to] = (value.astype(F32) * spread(late_parts[...], first_channel, width)).astype(BF16)
+    aux[0:8, to] = before[0:8]
+    early = spread(early_parts[...], first_channel, width)
+    first = source[0:TAIL].astype(F32)
+    last_rows = source[block - TAIL : block].astype(F32)
+    aux[8:24, to] = jnp.concatenate(
+        [early[3:4], early[0:3], last_rows[TAIL - 3 :], first[0:3], jnp.zeros((TAIL - 10, width), F32)], axis=0
+    )
+
+
 def channels_kernel(
     x_hbm, taps_hbm, bias_hbm, own_hbm, own_taps_hbm, own_bias_hbm, step_hbm, offset_hbm,
     step_bias_hbm, decay_hbm, skip_hbm,
-    x_out, gated, aux, passing_out, step_out, sums_out, taps, bias, own, own_taps, own_bias, offset,
-    x, step, step_bias, decay_log, skip, sems,
+    x_out, gated, aux, passing_out, step_out, sums_out, x, taps, bias, own, own_taps, own_bias, offset,
+    lags, late_parts, early_parts, step, step_bias, decay_log, skip, sems,
 ):
-    block, channels = x.shape
+    block = x.shape[0]
     count = taps.shape[0]
-    heads = step.shape[0]
-    width = channels // GROUP
-    whole = [
-        (offset_hbm, offset), (step_hbm, step), (step_bias_hbm, step_bias), (decay_hbm, decay_log),
-        (skip_hbm, skip), (taps_hbm, taps), (bias_hbm, bias),
+    pairs = [
+        (x_hbm, x), (offset_hbm, offset), (step_hbm, step), (step_bias_hbm, step_bias), (decay_hbm, decay_log),
+        (skip_hbm, skip), (taps_hbm, taps), (bias_hbm, bias), (own_taps_hbm, own_taps), (own_bias_hbm, own_bias),
+        (own_hbm, own),
     ]
-    later = [(own_hbm, own), (own_taps_hbm, own_taps), (own_bias_hbm, own_bias)]
-    parts = [slice(k * width, (k + 1) * width) for k in range(GROUP)]
-    pairs = whole + [(x_hbm.at[:, cols], x.at[:, cols]) for cols in parts] + later
     copies = [pltpu.make_async_copy(*pair, sems.at[k]) for k, pair in enumerate(pairs)]
     for copy in copies:
         copy.start()
-    for copy in copies[: len(whole)]:
+    for copy in copies[1:8]:
         copy.wait()
-    offset_col = offset_columns(offset[...])
-    lags = lag_matrices(offset_col, count)
+    for lag, matrix in enumerate(lag_matrices(offset_columns(offset[...]), count)):
+        lags[lag] = matrix
     time_step, rate_sum = rates(step[...], column(step_bias[...]), column(decay_log[...]))
     step_out[...] = time_step
     sums_out[...] = rate_sum
@@ -133,53 +152,20 @@
     gate = jnp.exp(jnp.where(last_offset >= block - 1 - place, last - rate_sum, NEG)) * time_step
     passing = jnp.exp(last) * (last_offset >= block).astype(F32)
     passing_out[...] = jnp.broadcast_to(passing, passing_out.shape)
-    early_parts = turned(jnp.where(place == count - 1, column(skip[...]), gate))[0:TAIL]
-    late_parts = turned(jnp.where(place >= count - 1, gate, 0.0))
-    for k, cols in enumerate(parts):
-        copies[len(whole) + k].wait()
-        source = x[:, cols]
-        before = convolve(source, taps[:, cols], bias[:, cols], lags)
-        value = silu(before).astype(BF16)
-        x_out[:, cols] = value
-        gated[:, cols] = (value.astype(F32) * spread(late_parts, k * width, width)).astype(BF16)
-        aux[0:8, cols] = before[0:8]
-        early = spread(early_parts, k * width, width)
-        first = source[0:TAIL].astype(F32)
-        last_rows = source[block - TAIL : block].astype(F32)
-        aux[8:24, cols] = jnp.concatenate(
-            [early[3:4], early[0:3], last_rows[TAIL - 3 :], first[0:3], jnp.zeros((TAIL - 10, width), F32)], axis=0
-        )
-    for copy in copies[len(whole) + GROUP :]:
+    early_parts[...] = turned(jnp.where(place == count - 1, column(skip[...]), gate))[0:TAIL]
+    late_parts[...] = turned(jnp.where(place >= count - 1, gate, 0.0))
+    copies[0].wait()
+    for slot, k in enumerate((1, 2, 3)):
+        channel_slice(k, slot, x, taps, bias, lags, late_parts, early_parts, x_out, gated, aux)
+    for copy in copies[8:]:
         copy.wait()
 
 
-def states_kernel(
-    own, other, own_taps, other_taps, own_bias, other_bias, gated, aux, passing, offset,
-    s0, s1, s2, s3, b_out, b_taps, ends, turn,
-):
-    member = member_here()
-    first = holds_b()
-    block, state_size = own.shape
-    count = own_taps.shape[0]
-    lags = lag_matrices(offset_columns(offset[...]), count)
-    taps = jnp.where(first, own_taps[...], other_taps[...])
-    bias = jnp.where(first, own_bias[...], other_bias[...])
-    source = jnp.where(first, own[...].astype(F32), other[...].astype(F32))
-    before = convolve(source.astype(BF16), taps, bias, lags)
-    value = silu(before)
-    b_out[...] = value.astype(BF16)
-    turn[...] = value.T.astype(BF16)
-    b_taps[...] = jnp.concatenate([taps, bias, jnp.zeros((8 - count - 1, state_size), F32), before[0:8]], axis=0)
-    channels = gated.shape[1]
-    width = channels // GROUP
+def message(out, k, state, passing, offset, count, gates_and_x, b_tail):
+    rows, width = state.shape
     heads = passing.shape[0]
-    blank = HALO - 3
-    ends[:, 0:channels] = jnp.concatenate(
-        [jnp.zeros((blank, channels), F32), aux[8 + X_LAST_AT : 8 + X_LAST_AT + 3, :]], axis=0
-    ).astype(BF16)
-    ends[:, channels : channels + state_size] = own[block - HALO : block, :]
-    ends[:, channels + state_size :] = other[block - HALO : block, :]
     slice_heads = heads // GROUP
+    out[0:rows, :] = state.astype(BF16)
     lane = iota((heads, width), 1)
     head = iota((heads, width), 0)
     high, low = two_parts(passing[:, 0:1])
@@ -187,21 +173,50 @@
     offsets = jnp.where(
         jnp.logical_and(lane[0:1] >= 2 * slice_heads, lane[0:1] < 2 * slice_heads + count - 1), offsets, 0.0
     )
+    at = lane + (member_here() ^ k) * slice_heads
+    packed = jnp.where(lane < slice_heads, jnp.where(at == head, high, 0.0), 0.0)
+    packed = jnp.where(jnp.logical_and(lane >= slice_heads, at == head + slice_heads), low, packed)
+    packed = jnp.where(lane < 2 * slice_heads, packed, 0.0)
+    misc = jnp.sum(packed, axis=0, keepdims=True) + offsets
     row = iota((TAIL, width), 0)
-    b_tail = jnp.concatenate(
-        [jnp.zeros((B_LAST_AT, width), F32), source[block - 3 :], source[0:3]], axis=0
+    tail = jnp.where(row == 0, misc, jnp.where(row < B_LAST_AT, gates_and_x, b_tail))
+    out[rows:, :] = tail.astype(BF16)
+
+
+def states_kernel(
+    x, own, other, own_taps, other_taps, own_bias, other_bias, lags, gated, aux, passing, offset,
+    s1, s2, s3, b_out, b_taps, b_tail, turn, ends,
+):
+    first = holds_b()
+    block, state_size = own.shape
+    count = own_taps.shape[0]
+    channels = x.shape[1]
+    ends[:, 0:channels] = x[block - HALO : block, :]
+    ends[:, channels : channels + state_size] = own[block - HALO : block, :]
+    ends[:, channels + state_size :] = other[block - HALO : block, :]
+    taps = jnp.where(first, own_taps[...], other_taps[...])
+    bias = jnp.where(first, own_bias[...], other_bias[...])
+    source = jnp.where(first, own[...].astype(F32), other[...].astype(F32))
+    before = convolve(source.astype(BF16), taps, bias, [lags[lag] for lag in range(count - 1)])
+    value = silu(before)
+    b_out[...] = value.astype(BF16)
+    turn[...] = value.T.astype(BF16)
+    b_taps[...] = jnp.concatenate([taps, bias, jnp.zeros((8 - count - 1, state_size), F32), before[0:8]], axis=0)
+    b_tail[...] = jnp.concatenate(
+        [jnp.zeros((B_LAST_AT, state_size), F32), source[block - 3 :], source[0:3]], axis=0
     )
-    for k, out in enumerate((s0, s1, s2, s3)):
-        quarter = member ^ k
-        cols = pl.ds(pl.multiple_of(quarter * width, width), width)
-        out[0:state_size, :] = dot(turn[...], gated[:, cols]).astype(BF16)
-        at = lane + quarter * slice_heads
-        packed = jnp.where(lane < slice_heads, jnp.where(at == head, high, 0.0), 0.0)
-        packed = jnp.where(jnp.logical_and(lane >= slice_heads, at == head + slice_heads), low, packed)
-        packed = jnp.where(lane < 2 * slice_heads, packed, 0.0)
-        misc = jnp.sum(packed, axis=0, keepdims=True) + offsets
-        tail = jnp.where(row == 0, misc, jnp.where(row < B_LAST_AT, aux[8:24, cols], b_tail))
-        out[state_size:, :] = tail.astype(BF16)
+    width = gated.shape[1] // (GROUP - 1)
+    for slot, (k, out) in enumerate(((1, s1), (2, s2), (3, s3))):
+        cols = slice(slot * width, (slot + 1) * width)
+        message(out, k, dot(turn[...], gated[:, cols]), passing, offset, count, aux[8:24, cols], b_tail[...])
+
+
+def rest_kernel(
+    x, taps, bias, lags, late_parts, early_parts, passing, offset, turn, b_tail, s0, x_out, aux, gated,
+):
+    channel_slice(0, 0, x, taps, bias, lags, late_parts, early_parts, x_out, gated, aux)
+    state = dot(turn[...], gated[...])
+    message(s0, 0, state, passing, offset, taps.shape[0], aux[8:24, :], b_tail[...])
 
 
 def tail_of(state):
@@ -266,7 +281,7 @@
     return b, x
 
 
-def group_kernel(r0, r1, r2, r3, earlier, x_taps, x_bias, b_taps, total, *, complete):
+def group_kernel(r3, r1, r2, r0, earlier, x_taps, x_bias, b_taps, total, *, complete):
     rows = r0.shape[0] - TAIL
     width = r0.shape[1]
     count = x_taps.shape[0]
@@ -314,7 +329,7 @@
 
 
 def entering_kernel(
-    r0, r1, r2, r3, near_odd, near_even, far, x_taps, x_bias, b_taps, e0, e1, e2, e3
+    r3, r1, r2, r0, near_even, far, near_odd, x_taps, x_bias, b_taps, e0, e1, e2, e3
 ):
     group = group_here()
     odd = (group & 1) == 1
@@ -379,22 +394,28 @@
 
 
 def intra_kernel(
-    x, aux, halo, own, other, own_taps, other_taps, own_bias, other_bias, b, b_aux, x_taps,
-    step, sums, offset, y, c_out, carry, bias, scores, columns, x_full, b_full,
+    x_early, x_late, aux_early, aux_late, halo, own, other, own_taps, other_taps, own_bias, other_bias, b, b_aux,
+    x_taps, step, sums, offset, lags, y, c_out, carry, bias, scores, columns, x_full, b_full, aux,
 ):
     first = holds_b()
-    block, channels = x.shape
+    block, channels = x_full.shape
     heads = step.shape[0]
     state_size = b.shape[1]
+    width = channels // GROUP
+    for k, (part, rows, slot) in enumerate(
+        ((x_late, aux_late, 0), (x_early, aux_early, 0), (x_early, aux_early, 1), (x_early, aux_early, 2))
+    ):
+        source = slice(slot * width, (slot + 1) * width)
+        x_full[:, quarter(k, width)] = part[:, source]
+        aux[:, quarter(k, width)] = rows[0:16, source]
     count = x_taps.shape[0]
     half = block // 2
     time_step, rate_sum = step[...], sums[...]
     columns[...] = rate_sum.T
     offset_col = offset_columns(offset[...])
 
-    x_full[...] = x[...]
     early = patched(aux[0:8, :], halo[:, 0:channels], x_taps[...], offset_col)
-    x_full[0:16, :] = jnp.concatenate([early, x[0:16, :].astype(F32)[8:16]], axis=0).astype(BF16)
+    x_full[0:16, :] = jnp.concatenate([early, x_full[0:16, :].astype(F32)[8:16]], axis=0).astype(BF16)
     own_halo = halo[:, channels : channels + state_size].astype(F32)
     other_halo = halo[:, channels + state_size :].astype(F32)
     b_full[...] = b[...]
@@ -403,7 +424,7 @@
     c_taps = jnp.where(first, other_taps[...], own_taps[...])
     c_bias = jnp.where(first, other_bias[...], own_bias[...])
     c_source = jnp.where(first, other[...].astype(F32), own[...].astype(F32)).astype(BF16)
-    before = convolve(c_source, c_taps, c_bias, lag_matrices(offset_col, count))
+    before = convolve(c_source, c_taps, c_bias, [lags[lag] for lag in range(count - 1)])
     c_value = silu(before)
     early = patched(before[0:8], jnp.where(first, other_halo, own_halo), c_taps, offset_col)
     c_out[...] = c_value.astype(BF16)
@@ -418,7 +439,6 @@
     reach = rate_sum - jnp.log(time_step)
     starts = iota(rate_sum.shape, 1) + 1
     factor = turned(jnp.where(offset[...] >= starts, jnp.exp(rate_sum), 0.0))
-    width = channels // GROUP
     for k in range(GROUP):
         carry[:, k * width : (k + 1) * width] = spread(factor, k * width, width)
     lane = iota((1, LANES), 1)
@@ -439,13 +459,12 @@
             y[part, cols] = value
 
 
-def back_kernel(c, *refs, first):
-    *parts, intra, carry, out, held, sems = refs
+def back_kernel(c, f3, f1, f2, f0, intra, carry, out, held, sems):
     member = member_here()
     width = out.shape[1] // GROUP
     copies = []
-    for k, state in enumerate(parts):
-        cols = pl.ds(pl.multiple_of((member ^ (first + k)) * width, width), width)
+    for k, state in enumerate((f0, f1, f2, f3)):
+        cols = pl.ds(pl.multiple_of((member ^ k) * width, width), width)
         value = intra[:, cols] + carry[:, cols] * dot(c[...], state[...])
         held[k] = value.astype(BF16)
         copies.append(pltpu.make_async_copy(held.at[k], out.at[:, cols], sems.at[k]))
@@ -498,31 +517,39 @@
     other_bc, other_taps, other_bias = [lax.ppermute(part, "head", swap) for part in (bc_input, bc_taps, bc_bias)]
     other_bias = other_bias[None, :]
 
-    x_main, gated, aux, passing, time_step, rate_sum, x_taps, x_bias, own, own_taps, own_bias, offset = pl.pallas_call(
+    others = jax.ShapeDtypeStruct((block, (GROUP - 1) * width), BF16)
+    slice_shape = jax.ShapeDtypeStruct((state_size + TAIL, width), BF16)
+    (
+        x_early, gated, aux_early, passing, time_step, rate_sum, x, x_taps, x_bias, own, own_taps, own_bias, offset,
+        lags, late_parts, early_parts,
+    ) = pl.pallas_call(
         channels_kernel,
         out_shape=[
-            jax.ShapeDtypeStruct((block, channels), BF16),
-            jax.ShapeDtypeStruct((block, channels), BF16),
-            jax.ShapeDtypeStruct((24, channels), F32),
+            others,
+            others,
+            jax.ShapeDtypeStruct((24, (GROUP - 1) * width), F32),
             jax.ShapeDtypeStruct((heads, LANES), F32),
             jax.ShapeDtypeStruct((heads, block), F32),
             jax.ShapeDtypeStruct((heads, block), F32),
+            jax.ShapeDtypeStruct((block, channels), BF16),
             jax.ShapeDtypeStruct(conv_taps.shape, F32),
             jax.ShapeDtypeStruct((1, channels), F32),
             jax.ShapeDtypeStruct(bc_input.shape, BF16),
             jax.ShapeDtypeStruct(bc_taps.shape, F32),
             jax.ShapeDtypeStruct((1, state_size), F32),
             jax.ShapeDtypeStruct((1, block), jnp.int32),
+            jax.ShapeDtypeStruct((conv_taps.shape[0] - 1, block, block), BF16),
+            jax.ShapeDtypeStruct((block, 2 * heads), BF16),
+            jax.ShapeDtypeStruct((TAIL, 2 * heads), BF16),
         ],
         in_specs=[hbm] * 11,
-        out_specs=[vmem] * 12,
+        out_specs=[vmem] * 16,
         scratch_shapes=[
-            pltpu.VMEM((block, channels), BF16),
             pltpu.VMEM((heads, block), F32),
             pltpu.VMEM((1, heads), F32),
             pltpu.VMEM((1, heads), F32),
             pltpu.VMEM((1, heads), F32),
-            pltpu.SemaphoreType.DMA((10 + GROUP,)),
+            pltpu.SemaphoreType.DMA((11,)),
         ],
         compiler_params=PARAMS,
         name="channels",
@@ -535,24 +562,40 @@
             )
         ]
     )
-
-    slice_shape = jax.ShapeDtypeStruct((state_size + TAIL, width), BF16)
-    *slices, b_main, b_aux, ends = pl.pallas_call(
+    s1, s2, s3, b_main, b_aux, b_tail, turn, ends = pl.pallas_call(
         states_kernel,
-        out_shape=[slice_shape] * GROUP
-        + [
+        out_shape=[
+            slice_shape,
+            slice_shape,
+            slice_shape,
             jax.ShapeDtypeStruct((block, state_size), BF16),
             jax.ShapeDtypeStruct((16, state_size), F32),
+            jax.ShapeDtypeStruct((TAIL, state_size), F32),
+            jax.ShapeDtypeStruct((state_size, block), BF16),
             jax.ShapeDtypeStruct((HALO, channels + 2 * state_size), BF16),
         ],
-        in_specs=[vmem] * 10,
-        out_specs=[vmem] * (GROUP + 3),
-        scratch_shapes=[pltpu.VMEM((state_size, block), BF16)],
+        in_specs=[vmem] * 12,
+        out_specs=[vmem] * 8,
         compiler_params=PARAMS,
         name="states",
-    )(own, other_bc, own_taps, other_taps, own_bias, other_bias, gated, aux, passing, offset)
+    )(x, own, other_bc, own_taps, other_taps, own_bias, other_bias, lags, gated, aux_early, passing, offset)
+    r1, r2, r3 = exchange(s1, 1), exchange(s2, 2), exchange(s3, 3)
     halo = shifted(ends, 1)
-    received = [slices[0]] + [exchange(slices[k], k) for k in (1, 2, 3)]
+    s0, x_late, aux_late = pl.pallas_call(
+        rest_kernel,
+        out_shape=[
+            slice_shape,
+            jax.ShapeDtypeStruct((block, width), BF16),
+            jax.ShapeDtypeStruct((24, width), F32),
+        ],
+        in_specs=[vmem] * 10,
+        out_specs=[vmem] * 3,
+        scratch_shapes=[pltpu.VMEM((block, width), BF16)],
+        compiler_params=PARAMS,
+        cost_estimate=pl.CostEstimate(flops=400_000_000, bytes_accessed=2_000_000, transcendentals=200_000),
+        name="rest",
+    )(x, x_taps, x_bias, lags, late_parts, early_parts, passing, offset, turn, b_tail)
+    received = [s0, r1, r2, r3]
 
     direct = groups == GROUP
     if direct:
@@ -569,7 +612,7 @@
         out_specs=vmem,
         compiler_params=PARAMS,
         name="group",
-    )(*received, earlier, x_taps, x_bias, b_aux)
+    )(r3, r1, r2, s0, earlier, x_taps, x_bias, b_aux)
     total, halo = lax.optimization_barrier((total, halo))
     if direct:
         far = exchange(total, 2 * GROUP)
@@ -586,7 +629,7 @@
         out_specs=[vmem] * GROUP,
         compiler_params=PARAMS,
         name="entering",
-    )(*received, near_odd, near_even, far, x_taps, x_bias, b_aux)
+    )(r3, r1, r2, s0, near_even, far, near_odd, x_taps, x_bias, b_aux)
     mine = [entering[0]] + [exchange(entering[k], k) for k in (1, 2, 3)]
 
     intra, c_conv, carry = pl.pallas_call(
@@ -596,7 +639,7 @@
             jax.ShapeDtypeStruct((block, state_size), BF16),
             jax.ShapeDtypeStruct((block, channels), F32),
         ],
-        in_specs=[vmem] * 15,
+        in_specs=[vmem] * 18,
         out_specs=[vmem] * 3,
         scratch_shapes=[
             pltpu.VMEM((block, block), F32),
@@ -604,39 +647,25 @@
             pltpu.VMEM((block, heads), F32),
             pltpu.VMEM((block, channels), BF16),
             pltpu.VMEM((block, state_size), BF16),
+            pltpu.VMEM((16, channels), F32),
         ],
         compiler_params=PARAMS,
         cost_estimate=pl.CostEstimate(flops=600_000_000, bytes_accessed=4_000_000, transcendentals=1_000_000),
         name="intra",
     )(
-        x_main, aux, halo, own, other_bc, own_taps, other_taps, own_bias, other_bias, b_main, b_aux,
-        x_taps, time_step, rate_sum, offset,
+        x_early, x_late, aux_early, aux_late, halo, own, other_bc, own_taps, other_taps, own_bias, other_bias,
+        b_main, b_aux, x_taps, time_step, rate_sum, offset, lags,
     )
     out_shape = jax.ShapeDtypeStruct((block, channels), BF16)
-    early = GROUP - 1
-    partial = pl.pallas_call(
-        lambda *refs: back_kernel(*refs, first=0),
+    return pl.pallas_call(
+        back_kernel,
         out_shape=out_shape,
-        in_specs=[vmem] * (early + 3),
+        in_specs=[vmem] * (GROUP + 3),
         out_specs=hbm,
-        scratch_shapes=[pltpu.VMEM((early, block, width), BF16), pltpu.SemaphoreType.DMA((early,))],
+        scratch_shapes=[pltpu.VMEM((GROUP, block, width), BF16), pltpu.SemaphoreType.DMA((GROUP,))],
         compiler_params=PARAMS,
         name="back",
-    )(c_conv, *mine[:early], intra, carry)
-
-    def last_slice(c, state, intra, carry, partial, out, held, sems):
-        back_kernel(c, state, intra, carry, out, held, sems, first=early)
-
-    return pl.pallas_call(
-        last_slice,
-        out_shape=out_shape,
-        in_specs=[vmem] * 4 + [hbm],
-        out_specs=hbm,
-        scratch_shapes=[pltpu.VMEM((1, block, width), BF16), pltpu.SemaphoreType.DMA((1,))],
-        input_output_aliases={4: 0},
-        compiler_params=PARAMS,
-        name="last",
-    )(c_conv, mine[early], intra, carry, partial)
+    )(c_conv, mine[3], mine[1], mine[2], mine[0], intra, carry)
 
 
 def solution(mesh):

time: 39 us -> 37.9 us (0.972)
  the two profiles are of different devices: /device:TPU:22 before, /device:TPU:8 now
where the time goes in v4:
time: 37.9 us; the launch traced here: 37.7 us
  starting transfers between devices  16.4 us (43%)
  waiting for transfers between devices  14.1 us (37%)
  Pallas kernels  7.06 us (19%)
    ppermute x8, waiting for transfers between devices, exchange(): lax.ppermute(array, 'seq', [(i, i ^ mask) for i in range(lax.axis_size('s...  11.2 us
    ppermute x8, starting transfers between devices, exchange(): lax.ppermute(array, 'seq', [(i, i ^ mask) for i in range(lax.axis_size('s...  10.1 us
    ppermute x1, starting transfers between devices, shifted(): lax.ppermute(array, 'seq', [(i, i + distance) for i in range(count - dist...  3.39 us
    ppermute x1, waiting for transfers between devices, on_device(): lax.ppermute(total, 'seq', pairs + [(high, low) for low, high in pairs])  2.61 us
    ppermute x1, starting transfers between devices, on_device(): lax.ppermute(total, 'seq', pairs + [(high, low) for low, high in pairs])  2.35 us
    pallas_call x1, Pallas kernels, on_device(): pl.pallas_call(channels_kernel, out_shape=[others, others, jax.ShapeDtype...  2.2 us
    pallas_call x1, Pallas kernels, on_device(): pl.pallas_call(intra_kernel, out_shape=[jax.ShapeDtypeStruct((block, chan...  1.5 us
    pallas_call x1, Pallas kernels, on_device(): pl.pallas_call(back_kernel, out_shape=out_shape, in_specs=[vmem] * (GROUP...  1.06 us
  transfers between devices with their start and end apart: 13, of which 8 were waited for; matrix products, arithmetic and copies ran while one was open for 0% of the time, Pallas kernels for 12%

profile of v4, /device:TPU:8, one launch (start us, length us, event | category | flops | bytes accessed | tf_op | source)
XLA Modules:
  0.0 37.7 jit_solution(16249735515979747116)
XLA Ops:
  0.0 0.0 collective-permute-start
  0.0 0.5 %collective-permute-start.1 = (f32[4,256]{1,0:T(4,128)}, f32[4,256]{1,0:T(4,128)S(1)}, u32[]{:S(2)}, u32[]{:S(2)}) collective-permute-start(f32[4,256]{1,0:T(4,128)} %own_taps_hbm.1), channel_id=1, source_target_pairs={{0,1},{1,0},{2,3},{3,2},{4,5},{5,4},{6,7},{7,6},{8,9},{9,8},{10,11... | collective-permute-start | bytes 12296 | tf_op jit(solution)/shard_map/ppermute | solution.py:517
  0.5 0.0 collective-permute-start.2
  0.5 2.2 %channels.1 = (bf16[256,768]{1,0:T(8,128)(2,1)S(1)}, bf16[256,768]{1,0:T(8,128)(2,1)S(1)}, f32[24,768]{1,0:T(8,128)S(1)}, f32[16,128]{1,0:T(8,128)S(1)}, f32[16,...) custom-call(bf16[256,1024]{1,0:T(8,128)(2,1)} %x_hbm.1, ...), custom_call_target="tpu_custom_call" | custom-call | tf_op jit(solution)/shard_map/channels/pallas_call | solution.py:525
  2.7 0.0 collective-permute-done.1.other_taps
  2.7 0.0 collective-permute-done.other
  2.8 0.6 %states.1 = (bf16[272,256]{1,0:T(8,128)(2,1)S(1)}, bf16[272,256]{1,0:T(8,128)(2,1)S(1)}, bf16[272,256]{1,0:T(8,128)(2,1)S(1)}, bf16[256,256]{1,0:T(8,128)(2,1)S(...) custom-call(bf16[256,1024]{1,0:T(8,128)(2,1)S(1)} %get-tuple-element, ...), custom_call_target="tpu_custom_call" | custom-call | tf_op jit(solution)/shard_map/states/pallas_call | solution.py:565
  3.4 2.5 %collective-permute-start.3 = (bf16[272,256]{1,0:T(8,128)(2,1)S(1)}, bf16[272,256]{1,0:T(8,128)(2,1)S(1)}, u32[]{:S(2)}, u32[]{:S(2)}) collective-permute-start(bf16[272,256]{1,0:T(8,128)(2,1)S(1)} %get-tuple-element.59), channel_id=1, source_target_pairs={{0,6},{2,4},{4,2},{6,0},{8,14},{10,12},{12,10},{14,8},{16,22},{18,... | collective-permute-start | bytes 417800 | tf_op jit(solution)/shard_map/ppermute | solution.py:477
  5.9 0.5 %collective-permute-start.4 = (bf16[272,256]{1,0:T(8,128)(2,1)S(1)}, bf16[272,256]{1,0:T(8,128)(2,1)S(1)}, u32[]{:S(2)}, u32[]{:S(2)}) collective-permute-start(bf16[272,256]{1,0:T(8,128)(2,1)S(1)} %get-tuple-element.60), channel_id=1, source_target_pairs={{0,2},{2,0},{4,6},{6,4},{8,10},{10,8},{12,14},{14,12},{16,18},{18,... | collective-permute-start | bytes 417800 | tf_op jit(solution)/shard_map/ppermute | solution.py:477
  6.5 0.5 %collective-permute-start.5 = (bf16[272,256]{1,0:T(8,128)(2,1)S(1)}, bf16[272,256]{1,0:T(8,128)(2,1)S(1)}, u32[]{:S(2)}, u32[]{:S(2)}) collective-permute-start(bf16[272,256]{1,0:T(8,128)(2,1)S(1)} %get-tuple-element.61), channel_id=1, source_target_pairs={{0,4},{2,6},{4,0},{6,2},{8,12},{10,14},{12,8},{14,10},{16,20},{18,... | collective-permute-start | bytes 417800 | tf_op jit(solution)/shard_map/ppermute | solution.py:477
  7.0 3.4 %collective-permute-start.6 = (bf16[16,1536]{1,0:T(8,128)(2,1)S(1)}, bf16[16,1536]{1,0:T(8,128)(2,1)S(1)}, u32[]{:S(2)}, u32[]{:S(2)}) collective-permute-start(bf16[16,1536]{1,0:T(8,128)(2,1)S(1)} %get-tuple-element.64), channel_id=1, source_target_pairs={{0,2},{2,4},{4,6},{6,8},{8,10},{10,12},{12,14},{14,16},{16,18},{18... | collective-permute-start | bytes 147464 | tf_op jit(solution)/shard_map/ppermute | solution.py:482
  10.4 0.6 %rest.1 = (bf16[272,256]{1,0:T(8,128)(2,1)S(1)}, bf16[256,256]{1,0:T(8,128)(2,1)S(1)}, f32[24,256]{1,0:T(8,128)S(1)}) custom-call(bf16[256,1024]{1,0:T(8,128)(2,1)S(1)} %get-tuple-element.42.x, f32[4,1024]{1,0:T(4,128)S(1)} %get-tuple-element.43.taps.refs_5_.x_taps, f32[1,1024]{1,0:T(1,128)S(1)} %get-tuple-element.44.bias.refs_6_.x_bias, ...), custom_call_target="tpu_custom_call" | custom-call | flops 400000000 | bytes 2000000 | tf_op jit(solution)/shard_map/rest/pallas_call | solution.py:584
  10.9 0.0 collective-permute-done.3.refs_0_.r3
  10.9 3.0 %collective-permute-done.4.refs_1_.r1 = bf16[272,256]{1,0:T(8,128)(2,1)S(1)} collective-permute-done((bf16[272,256]{1,0:T(8,128)(2,1)S(1)}, bf16[272,256]{1,0:T(8,128)(2,1)S(1)}, u32[]{:S(2)}, u32[]{:S(2)}) %collective-permute-start.4) | collective-permute-done | bytes 139296 | tf_op jit(solution)/shard_map/ppermute | solution.py:477
  13.9 0.0 collective-permute-done.5.refs_2_.r2
  14.0 0.4 %group.1 = bf16[272,256]{1,0:T(8,128)(2,1)S(1)} custom-call(bf16[272,256]{1,0:T(8,128)(2,1)S(1)} %collective-permute-done.3.refs_0_.r3, bf16[272,256]{1,0:T(8,128)(2,1)S(1)} %collective-permute-done.4.refs_1_.r1, bf16[272,256]{1,0:T(8,128)(2,1)S(1)} %collective-permute-done.5.refs_2_.r2, bf16[272,256]{1,0:T(8,128)(2,1)S(1)} %get-tuple-element.62.refs_3_.r0, ...), custom_call_target="tpu_custom_call" | custom-call | tf_op jit(solution)/shard_map/group/pallas_call | solution.py:608
  14.4 0.3 collective-permute-done.6.halo
  14.7 0.1 collective-permute-start.9
  14.9 2.9 %collective-permute-start.8 = (bf16[272,256]{1,0:T(8,128)(2,1)S(1)}, bf16[272,256]{1,0:T(8,128)(2,1)S(1)}, u32[]{:S(2)}, u32[]{:S(2)}) collective-permute-start(bf16[272,256]{1,0:T(8,128)(2,1)S(1)} %group.1), channel_id=1, source_target_pairs={{0,16},{2,18},{4,20},{6,22},{8,24},{10,26},{12,28},{14,30},{16,0},... | collective-permute-start | bytes 417800 | tf_op jit(solution)/shard_map/ppermute | solution.py:477
  17.8 2.3 %collective-permute-start.7 = (bf16[272,256]{1,0:T(8,128)(2,1)S(1)}, bf16[272,256]{1,0:T(8,128)(2,1)S(1)}, u32[]{:S(2)}, u32[]{:S(2)}) collective-permute-start(bf16[272,256]{1,0:T(8,128)(2,1)S(1)} %group.1), channel_id=1, source_target_pairs={{8,16},{10,18},{12,20},{14,22},{16,8},{18,10},{20,12},{22,14},{9,1... | collective-permute-start | bytes 417800 | tf_op jit(solution)/shard_map/ppermute | solution.py:620
  20.1 0.6 %collective-permute-done.9.near_odd = bf16[272,256]{1,0:T(8,128)(2,1)S(1)} collective-permute-done((bf16[272,256]{1,0:T(8,128)(2,1)S(1)}, bf16[272,256]{1,0:T(8,128)(2,1)S(1)}, u32[]{:S(2)}, u32[]{:S(2)}) %collective-permute-start.9) | collective-permute-done | bytes 139296 | tf_op jit(solution)/shard_map/ppermute | solution.py:477
  20.7 3.9 %collective-permute-done.8.far = bf16[272,256]{1,0:T(8,128)(2,1)S(1)} collective-permute-done((bf16[272,256]{1,0:T(8,128)(2,1)S(1)}, bf16[272,256]{1,0:T(8,128)(2,1)S(1)}, u32[]{:S(2)}, u32[]{:S(2)}) %collective-permute-start.8) | collective-permute-done | bytes 139296 | tf_op jit(solution)/shard_map/ppermute | solution.py:477
  24.6 2.6 %collective-permute-done.7.near_even = bf16[272,256]{1,0:T(8,128)(2,1)S(1)} collective-permute-done((bf16[272,256]{1,0:T(8,128)(2,1)S(1)}, bf16[272,256]{1,0:T(8,128)(2,1)S(1)}, u32[]{:S(2)}, u32[]{:S(2)}) %collective-permute-start.7) | collective-permute-done | bytes 139296 | tf_op jit(solution)/shard_map/ppermute | solution.py:620
  27.3 0.7 %entering.1 = (bf16[256,256]{1,0:T(8,128)(2,1)S(1)}, bf16[256,256]{1,0:T(8,128)(2,1)S(1)}, bf16[256,256]{1,0:T(8,128)(2,1)S(1)}, bf16[256,256]{1,0:T(8,128)(2,1)S(1)}) custom-call(bf16[272,256]{1,0:T(8,128)(2,1)S(1)} %collective-permute-done.3.refs_0_.r3, bf16[272,256]{1,0:T(8,128)(2,1)S(1)} %collective-permute-done.4.refs_1_.r1, ...), custom_call_target="tpu_custom_call" | custom-call | tf_op jit(solution)/shard_map/entering/pallas_call | solution.py:625
  27.9 2.0 %collective-permute-start.10 = (bf16[256,256]{1,0:T(8,128)(2,1)S(1)}, bf16[256,256]{1,0:T(8,128)(2,1)S(1)}, u32[]{:S(2)}, u32[]{:S(2)}) collective-permute-start(bf16[256,256]{1,0:T(8,128)(2,1)S(1)} %get-tuple-element.71), channel_id=1, source_target_pairs={{0,6},{2,4},{4,2},{6,0},{8,14},{10,12},{12,10},{14,8},{16,22},{18,... | collective-permute-start | bytes 393224 | tf_op jit(solution)/shard_map/ppermute | solution.py:477
  29.9 0.9 %collective-permute-start.11 = (bf16[256,256]{1,0:T(8,128)(2,1)S(1)}, bf16[256,256]{1,0:T(8,128)(2,1)S(1)}, u32[]{:S(2)}, u32[]{:S(2)}) collective-permute-start(bf16[256,256]{1,0:T(8,128)(2,1)S(1)} %get-tuple-element.72), channel_id=1, source_target_pairs={{0,2},{2,0},{4,6},{6,4},{8,10},{10,8},{12,14},{14,12},{16,18},{18,... | collective-permute-start | bytes 393224 | tf_op jit(solution)/shard_map/ppermute | solution.py:477
  30.8 0.7 %collective-permute-start.12 = (bf16[256,256]{1,0:T(8,128)(2,1)S(1)}, bf16[256,256]{1,0:T(8,128)(2,1)S(1)}, u32[]{:S(2)}, u32[]{:S(2)}) collective-permute-start(bf16[256,256]{1,0:T(8,128)(2,1)S(1)} %get-tuple-element.73), channel_id=1, source_target_pairs={{0,4},{2,6},{4,0},{6,2},{8,12},{10,14},{12,8},{14,10},{16,20},{18,... | collective-permute-start | bytes 393224 | tf_op jit(solution)/shard_map/ppermute | solution.py:477
  31.5 1.5 %intra.1 = (f32[256,1024]{1,0:T(8,128)S(1)}, bf16[256,256]{1,0:T(8,128)(2,1)S(1)}, f32[256,1024]{1,0:T(8,128)S(1)}) custom-call(bf16[256,768]{1,0:T(8,128)(2,1)S(1)} %get-tuple-element.41.x_early, bf16[256,256]{1,0:T(8,128)(2,1)S(1)} %get-tuple-element.57.x_late, f32[24,768]{1,0:T(8,128)S(1)} %get-tuple-element.54.aux.aux_early, ...), custom_call_target="tpu_custom_call" | custom-call | flops 600000000 | bytes 4000000 | tf_op jit(solution)/shard_map/intra/pallas_call | solution.py:635
  33.0 2.2 %collective-permute-done.10.f3 = bf16[256,256]{1,0:T(8,128)(2,1)S(1)} collective-permute-done((bf16[256,256]{1,0:T(8,128)(2,1)S(1)}, bf16[256,256]{1,0:T(8,128)(2,1)S(1)}, u32[]{:S(2)}, u32[]{:S(2)}) %collective-permute-start.10) | collective-permute-done | bytes 131104 | tf_op jit(solution)/shard_map/ppermute | solution.py:477
  35.2 1.2 %collective-permute-done.11.f1 = bf16[256,256]{1,0:T(8,128)(2,1)S(1)} collective-permute-done((bf16[256,256]{1,0:T(8,128)(2,1)S(1)}, bf16[256,256]{1,0:T(8,128)(2,1)S(1)}, u32[]{:S(2)}, u32[]{:S(2)}) %collective-permute-start.11) | collective-permute-done | bytes 131104 | tf_op jit(solution)/shard_map/ppermute | solution.py:477
  36.5 0.1 collective-permute-done.12.f2
  36.6 1.1 %back.1 = bf16[256,1024]{1,0:T(8,128)(2,1)} custom-call(bf16[256,256]{1,0:T(8,128)(2,1)S(1)} %get-tuple-element.69.c, bf16[256,256]{1,0:T(8,128)(2,1)S(1)} %collective-permute-done.10.f3, bf16[256,256]{1,0:T(8,128)(2,1)S(1)} %collective-permute-done.11.f1, bf16[256,256]{1,0:T(8,128)(2,1)S(1)} %collective-permute-done.12.f2, ...), custom_call_target="tpu_custom_call" | custom-call | tf_op jit(solution)/shard_map/back/pallas_call | solution.py:660
  (2 shorter events, 0.0 us)
Async XLA Ops:
  0.0 2.7 %collective-permute-start = (bf16[256,256]{1,0:T(8,128)(2,1)}, bf16[256,256]{1,0:T(8,128)(2,1)S(1)}, u32[]{:S(2)}, u32[]{:S(2)}) collective-permute-start(bf16[256,256]{1,0:T(8,128)(2,1)} %own_hbm.1), channel_id=1, source_target_pairs={{0,1},{1,0},{2,3},{3,2},{4,5},{5,4},{6,7},{7,6},{8,9},{9,8},{10,11... | collective-permute-start | bytes 393224 | tf_op jit(solution)/shard_map/ppermute | solution.py:517
  0.0 2.7 %collective-permute-start.1 = (f32[4,256]{1,0:T(4,128)}, f32[4,256]{1,0:T(4,128)S(1)}, u32[]{:S(2)}, u32[]{:S(2)}) collective-permute-start(f32[4,256]{1,0:T(4,128)} %own_taps_hbm.1), channel_id=1, source_target_pairs={{0,1},{1,0},{2,3},{3,2},{4,5},{5,4},{6,7},{7,6},{8,9},{9,8},{10,11... | collective-permute-start | bytes 12296 | tf_op jit(solution)/shard_map/ppermute | solution.py:517
  0.5 2.2 %collective-permute-start.2 = (f32[256]{0:T(256)}, f32[256]{0:T(256)S(1)}, u32[]{:S(2)}, u32[]{:S(2)}) collective-permute-start(f32[256]{0:T(256)} %param.16), channel_id=1, source_target_pairs={{0,1},{1,0},{2,3},{3,2},{4,5},{5,4},{6,7},{7,6},{8,9},{9,8},{10,11... | collective-permute-start | bytes 3080 | tf_op jit(solution)/shard_map/ppermute | solution.py:517
  3.4 7.5 %collective-permute-start.3 = (bf16[272,256]{1,0:T(8,128)(2,1)S(1)}, bf16[272,256]{1,0:T(8,128)(2,1)S(1)}, u32[]{:S(2)}, u32[]{:S(2)}) collective-permute-start(bf16[272,256]{1,0:T(8,128)(2,1)S(1)} %get-tuple-element.59), channel_id=1, source_target_pairs={{0,6},{2,4},{4,2},{6,0},{8,14},{10,12},{12,10},{14,8},{16,22},{18,... | collective-permute-start | bytes 417800 | tf_op jit(solution)/shard_map/ppermute | solution.py:477
  5.9 8.0 %collective-permute-start.4 = (bf16[272,256]{1,0:T(8,128)(2,1)S(1)}, bf16[272,256]{1,0:T(8,128)(2,1)S(1)}, u32[]{:S(2)}, u32[]{:S(2)}) collective-permute-start(bf16[272,256]{1,0:T(8,128)(2,1)S(1)} %get-tuple-element.60), channel_id=1, source_target_pairs={{0,2},{2,0},{4,6},{6,4},{8,10},{10,8},{12,14},{14,12},{16,18},{18,... | collective-permute-start | bytes 417800 | tf_op jit(solution)/shard_map/ppermute | solution.py:477
  6.5 7.5 %collective-permute-start.5 = (bf16[272,256]{1,0:T(8,128)(2,1)S(1)}, bf16[272,256]{1,0:T(8,128)(2,1)S(1)}, u32[]{:S(2)}, u32[]{:S(2)}) collective-permute-start(bf16[272,256]{1,0:T(8,128)(2,1)S(1)} %get-tuple-element.61), channel_id=1, source_target_pairs={{0,4},{2,6},{4,0},{6,2},{8,12},{10,14},{12,8},{14,10},{16,20},{18,... | collective-permute-start | bytes 417800 | tf_op jit(solution)/shard_map/ppermute | solution.py:477
  7.0 7.8 %collective-permute-start.6 = (bf16[16,1536]{1,0:T(8,128)(2,1)S(1)}, bf16[16,1536]{1,0:T(8,128)(2,1)S(1)}, u32[]{:S(2)}, u32[]{:S(2)}) collective-permute-start(bf16[16,1536]{1,0:T(8,128)(2,1)S(1)} %get-tuple-element.64), channel_id=1, source_target_pairs={{0,2},{2,4},{4,6},{6,8},{8,10},{10,12},{12,14},{14,16},{16,18},{18... | collective-permute-start | bytes 147464 | tf_op jit(solution)/shard_map/ppermute | solution.py:482
  14.7 6.0 %collective-permute-start.9 = (bf16[272,256]{1,0:T(8,128)(2,1)S(1)}, bf16[272,256]{1,0:T(8,128)(2,1)S(1)}, u32[]{:S(2)}, u32[]{:S(2)}) collective-permute-start(bf16[272,256]{1,0:T(8,128)(2,1)S(1)} %group.1), channel_id=1, source_target_pairs={{0,8},{2,10},{4,12},{6,14},{8,0},{10,2},{12,4},{14,6},{16,24},{18,... | collective-permute-start | bytes 417800 | tf_op jit(solution)/shard_map/ppermute | solution.py:477
  14.9 9.8 %collective-permute-start.8 = (bf16[272,256]{1,0:T(8,128)(2,1)S(1)}, bf16[272,256]{1,0:T(8,128)(2,1)S(1)}, u32[]{:S(2)}, u32[]{:S(2)}) collective-permute-start(bf16[272,256]{1,0:T(8,128)(2,1)S(1)} %group.1), channel_id=1, source_target_pairs={{0,16},{2,18},{4,20},{6,22},{8,24},{10,26},{12,28},{14,30},{16,0},... | collective-permute-start | bytes 417800 | tf_op jit(solution)/shard_map/ppermute | solution.py:477
  17.8 9.5 %collective-permute-start.7 = (bf16[272,256]{1,0:T(8,128)(2,1)S(1)}, bf16[272,256]{1,0:T(8,128)(2,1)S(1)}, u32[]{:S(2)}, u32[]{:S(2)}) collective-permute-start(bf16[272,256]{1,0:T(8,128)(2,1)S(1)} %group.1), channel_id=1, source_target_pairs={{8,16},{10,18},{12,20},{14,22},{16,8},{18,10},{20,12},{22,14},{9,1... | collective-permute-start | bytes 417800 | tf_op jit(solution)/shard_map/ppermute | solution.py:620
  27.9 7.3 %collective-permute-start.10 = (bf16[256,256]{1,0:T(8,128)(2,1)S(1)}, bf16[256,256]{1,0:T(8,128)(2,1)S(1)}, u32[]{:S(2)}, u32[]{:S(2)}) collective-permute-start(bf16[256,256]{1,0:T(8,128)(2,1)S(1)} %get-tuple-element.71), channel_id=1, source_target_pairs={{0,6},{2,4},{4,2},{6,0},{8,14},{10,12},{12,10},{14,8},{16,22},{18,... | collective-permute-start | bytes 393224 | tf_op jit(solution)/shard_map/ppermute | solution.py:477
  29.9 6.6 %collective-permute-start.11 = (bf16[256,256]{1,0:T(8,128)(2,1)S(1)}, bf16[256,256]{1,0:T(8,128)(2,1)S(1)}, u32[]{:S(2)}, u32[]{:S(2)}) collective-permute-start(bf16[256,256]{1,0:T(8,128)(2,1)S(1)} %get-tuple-element.72), channel_id=1, source_target_pairs={{0,2},{2,0},{4,6},{6,4},{8,10},{10,8},{12,14},{14,12},{16,18},{18,... | collective-permute-start | bytes 393224 | tf_op jit(solution)/shard_map/ppermute | solution.py:477
  30.8 5.8 %collective-permute-start.12 = (bf16[256,256]{1,0:T(8,128)(2,1)S(1)}, bf16[256,256]{1,0:T(8,128)(2,1)S(1)}, u32[]{:S(2)}, u32[]{:S(2)}) collective-permute-start(bf16[256,256]{1,0:T(8,128)(2,1)S(1)} %get-tuple-element.73), channel_id=1, source_target_pairs={{0,4},{2,6},{4,0},{6,2},{8,12},{10,14},{12,8},{14,10},{16,20},{18,... | collective-permute-start | bytes 393224 | tf_op jit(solution)/shard_map/ppermute | solution.py:477

commit v5 on v4

--- a/solution.py
+++ b/solution.py
@@ -329,13 +329,11 @@
 
 
 def entering_kernel(
-    r3, r1, r2, r0, near_even, far, near_odd, x_taps, x_bias, b_taps, e0, e1, e2, e3
+    r3, r1, r2, r0, far, near, x_taps, x_bias, b_taps, e0, e1, e2, e3
 ):
     group = group_here()
-    odd = (group & 1) == 1
     one = jnp.ones((1, r0.shape[1]), F32)
-    from_odd = jnp.where(odd, one, 0.0)
-    from_even = jnp.where(jnp.logical_and(group >= 2, jnp.logical_not(odd)), one, 0.0)
+    from_near = jnp.where(group >= 1, one, 0.0)
     from_far = jnp.where(group >= 2, one, 0.0)
     rows = r0.shape[0] - TAIL
     width = r0.shape[1]
@@ -348,7 +346,7 @@
         states = [held[member ^ k] for k in range(GROUP)]
         targets = [outs[member ^ k] for k in range(GROUP)]
         tails = [tail_of(state) for state in states]
-        near_tail = from_odd * tail_of(near_odd) + from_even * tail_of(near_even)
+        near_tail = from_near * tail_of(near)
         far_tail = from_far * tail_of(far)
         decays = [decay_of(tail) for tail in tails]
         near_decay = decay_of(near_tail)
@@ -369,8 +367,7 @@
         step = 32
         for top in range(0, rows, step):
             part = slice(top, top + step)
-            value = from_odd * near_odd[part, :].astype(F32) + from_even * near_even[part, :].astype(F32)
-            value = value + far_factor * far[part, :].astype(F32) + added[0][part]
+            value = from_near * near[part, :].astype(F32) + far_factor * far[part, :].astype(F32) + added[0][part]
             targets[0][part, :] = value.astype(BF16)
             for k in range(GROUP - 1):
                 value = decays[k] * value + states[k][part, :].astype(F32) + added[k + 1][part]
@@ -477,6 +474,11 @@
     return lax.ppermute(array, "seq", [(i, i ^ mask) for i in range(lax.axis_size("seq"))])
 
 
+def turned_on(array, distance):
+    count = lax.axis_size("seq")
+    return lax.ppermute(array, "seq", [(i, (i + distance) % count) for i in range(count)])
+
+
 def shifted(array, distance):
     count = lax.axis_size("seq")
     return lax.ppermute(array, "seq", [(i, i + distance) for i in range(count - distance)])
@@ -495,9 +497,7 @@
         distance *= 2
     near_tail = jnp.concatenate([jnp.zeros((X_LAST_AT, last.shape[1]), BF16), last[X_LAST_AT:]], axis=0)
     near = jnp.concatenate([held.astype(BF16), near_tail], axis=0)
-    odd = (lax.axis_index("seq") // GROUP) % 2 == 1
-    nothing = jnp.zeros_like(near)
-    return jnp.where(odd, near, nothing), jnp.where(odd, nothing, near), nothing
+    return near, jnp.zeros_like(near)
 
 
 def on_device(
@@ -615,21 +615,19 @@
     )(r3, r1, r2, s0, earlier, x_taps, x_bias, b_aux)
     total, halo = lax.optimization_barrier((total, halo))
     if direct:
-        far = exchange(total, 2 * GROUP)
-        pairs = [(GROUP + k, 2 * GROUP + k) for k in range(GROUP)]
-        near_even = lax.ppermute(total, "seq", pairs + [(high, low) for low, high in pairs])
-        near_odd = exchange(total, GROUP)
+        far = shifted(total, 2 * GROUP)
+        near = turned_on(total, GROUP)
     else:
-        near_odd, near_even, far = scan_groups(total, groups)
+        near, far = scan_groups(total, groups)
 
     entering = pl.pallas_call(
         entering_kernel,
         out_shape=[jax.ShapeDtypeStruct((state_size, width), BF16)] * GROUP,
-        in_specs=[vmem] * (GROUP + 6),
+        in_specs=[vmem] * (GROUP + 5),
         out_specs=[vmem] * GROUP,
         compiler_params=PARAMS,
         name="entering",
-    )(r3, r1, r2, s0, near_even, far, near_odd, x_taps, x_bias, b_aux)
+    )(r3, r1, r2, s0, far, near, x_taps, x_bias, b_aux)
     mine = [entering[0]] + [exchange(entering[k], k) for k in (1, 2, 3)]
 
     intra, c_conv, carry = pl.pallas_call(

time: 37.9 us -> 36 us (0.950)
  the two profiles are of different devices: /device:TPU:8 before, /device:TPU:24 now
where the time goes in v5:
time: 36 us; the launch traced here: 35.9 us
  waiting for transfers between devices  16.4 us (46%)
  starting transfers between devices  12.3 us (34%)
  Pallas kernels  7.05 us (20%)
    ppermute x6, starting transfers between devices, exchange(): lax.ppermute(array, 'seq', [(i, i ^ mask) for i in range(lax.axis_size('s...  7.11 us
    ppermute x6, waiting for transfers between devices, exchange(): lax.ppermute(array, 'seq', [(i, i ^ mask) for i in range(lax.axis_size('s...  6.14 us
    ppermute x1, waiting for transfers between devices, turned_on(): lax.ppermute(array, 'seq', [(i, (i + distance) % count) for i in range(co...  5.16 us
    ppermute x2, waiting for transfers between devices, shifted(): lax.ppermute(array, 'seq', [(i, i + distance) for i in range(count - dist...  5.11 us
    ppermute x2, starting transfers between devices, shifted(): lax.ppermute(array, 'seq', [(i, i + distance) for i in range(count - dist...  4.67 us
    pallas_call x1, Pallas kernels, on_device(): pl.pallas_call(channels_kernel, out_shape=[others, others, jax.ShapeDtype...  2.2 us
    pallas_call x1, Pallas kernels, on_device(): pl.pallas_call(intra_kernel, out_shape=[jax.ShapeDtypeStruct((block, chan...  1.5 us
    pallas_call x1, Pallas kernels, on_device(): pl.pallas_call(back_kernel, out_shape=out_shape, in_specs=[vmem] * (GROUP...  1.06 us
  transfers between devices with their start and end apart: 12, of which 7 were waited for; matrix products, arithmetic and copies ran while one was open for 0% of the time, Pallas kernels for 13%

profile of v5, /device:TPU:24, one launch (start us, length us, event | category | flops | bytes accessed | tf_op | source)
XLA Modules:
  0.0 35.9 jit_solution(601034852217898290)
XLA Ops:
  0.0 0.0 collective-permute-start
  0.0 0.5 %collective-permute-start.1 = (f32[4,256]{1,0:T(4,128)}, f32[4,256]{1,0:T(4,128)S(1)}, u32[]{:S(2)}, u32[]{:S(2)}) collective-permute-start(f32[4,256]{1,0:T(4,128)} %own_taps_hbm.1), channel_id=1, source_target_pairs={{0,1},{1,0},{2,3},{3,2},{4,5},{5,4},{6,7},{7,6},{8,9},{9,8},{10,11... | collective-permute-start | bytes 12296 | tf_op jit(solution)/shard_map/ppermute | solution.py:517
  0.5 0.0 collective-permute-start.2
  0.5 2.2 %channels.1 = (bf16[256,768]{1,0:T(8,128)(2,1)S(1)}, bf16[256,768]{1,0:T(8,128)(2,1)S(1)}, f32[24,768]{1,0:T(8,128)S(1)}, f32[16,128]{1,0:T(8,128)S(1)}, f32[16,...) custom-call(bf16[256,1024]{1,0:T(8,128)(2,1)} %x_hbm.1, ...), custom_call_target="tpu_custom_call" | custom-call | tf_op jit(solution)/shard_map/channels/pallas_call | solution.py:525
  2.7 0.0 collective-permute-done.2
  2.7 0.0 collective-permute-done.1.other_taps
  2.7 0.0 collective-permute-done.other
  2.8 0.6 %states.1 = (bf16[272,256]{1,0:T(8,128)(2,1)S(1)}, bf16[272,256]{1,0:T(8,128)(2,1)S(1)}, bf16[272,256]{1,0:T(8,128)(2,1)S(1)}, bf16[256,256]{1,0:T(8,128)(2,1)S(...) custom-call(bf16[256,1024]{1,0:T(8,128)(2,1)S(1)} %get-tuple-element, ...), custom_call_target="tpu_custom_call" | custom-call | tf_op jit(solution)/shard_map/states/pallas_call | solution.py:565
  3.4 2.5 %collective-permute-start.3 = (bf16[272,256]{1,0:T(8,128)(2,1)S(1)}, bf16[272,256]{1,0:T(8,128)(2,1)S(1)}, u32[]{:S(2)}, u32[]{:S(2)}) collective-permute-start(bf16[272,256]{1,0:T(8,128)(2,1)S(1)} %get-tuple-element.59), channel_id=1, source_target_pairs={{0,6},{2,4},{4,2},{6,0},{8,14},{10,12},{12,10},{14,8},{16,22},{18,... | collective-permute-start | bytes 417800 | tf_op jit(solution)/shard_map/ppermute | solution.py:474
  5.9 0.5 %collective-permute-start.4 = (bf16[272,256]{1,0:T(8,128)(2,1)S(1)}, bf16[272,256]{1,0:T(8,128)(2,1)S(1)}, u32[]{:S(2)}, u32[]{:S(2)}) collective-permute-start(bf16[272,256]{1,0:T(8,128)(2,1)S(1)} %get-tuple-element.60), channel_id=1, source_target_pairs={{0,2},{2,0},{4,6},{6,4},{8,10},{10,8},{12,14},{14,12},{16,18},{18,... | collective-permute-start | bytes 417800 | tf_op jit(solution)/shard_map/ppermute | solution.py:474
  6.5 0.5 %collective-permute-start.5 = (bf16[272,256]{1,0:T(8,128)(2,1)S(1)}, bf16[272,256]{1,0:T(8,128)(2,1)S(1)}, u32[]{:S(2)}, u32[]{:S(2)}) collective-permute-start(bf16[272,256]{1,0:T(8,128)(2,1)S(1)} %get-tuple-element.61), channel_id=1, source_target_pairs={{0,4},{2,6},{4,0},{6,2},{8,12},{10,14},{12,8},{14,10},{16,20},{18,... | collective-permute-start | bytes 417800 | tf_op jit(solution)/shard_map/ppermute | solution.py:474
  7.0 3.4 %collective-permute-start.6 = (bf16[16,1536]{1,0:T(8,128)(2,1)S(1)}, bf16[16,1536]{1,0:T(8,128)(2,1)S(1)}, u32[]{:S(2)}, u32[]{:S(2)}) collective-permute-start(bf16[16,1536]{1,0:T(8,128)(2,1)S(1)} %get-tuple-element.64), channel_id=1, source_target_pairs={{0,2},{2,4},{4,6},{6,8},{8,10},{10,12},{12,14},{14,16},{16,18},{18... | collective-permute-start | bytes 147464 | tf_op jit(solution)/shard_map/ppermute | solution.py:484
  10.4 0.6 %rest.1 = (bf16[272,256]{1,0:T(8,128)(2,1)S(1)}, bf16[256,256]{1,0:T(8,128)(2,1)S(1)}, f32[24,256]{1,0:T(8,128)S(1)}) custom-call(bf16[256,1024]{1,0:T(8,128)(2,1)S(1)} %get-tuple-element.42.x, f32[4,1024]{1,0:T(4,128)S(1)} %get-tuple-element.43.taps.refs_5_.x_taps, f32[1,1024]{1,0:T(1,128)S(1)} %get-tuple-element.44.bias.refs_6_.x_bias, ...), custom_call_target="tpu_custom_call" | custom-call | flops 400000000 | bytes 2000000 | tf_op jit(solution)/shard_map/rest/pallas_call | solution.py:584
  10.9 0.0 collective-permute-done.3.refs_0_.r3
  10.9 3.0 %collective-permute-done.4.refs_1_.r1 = bf16[272,256]{1,0:T(8,128)(2,1)S(1)} collective-permute-done((bf16[272,256]{1,0:T(8,128)(2,1)S(1)}, bf16[272,256]{1,0:T(8,128)(2,1)S(1)}, u32[]{:S(2)}, u32[]{:S(2)}) %collective-permute-start.4) | collective-permute-done | bytes 139296 | tf_op jit(solution)/shard_map/ppermute | solution.py:474
  13.9 0.0 collective-permute-done.5.refs_2_.r2
  14.0 0.4 %group.1 = bf16[272,256]{1,0:T(8,128)(2,1)S(1)} custom-call(bf16[272,256]{1,0:T(8,128)(2,1)S(1)} %collective-permute-done.3.refs_0_.r3, bf16[272,256]{1,0:T(8,128)(2,1)S(1)} %collective-permute-done.4.refs_1_.r1, bf16[272,256]{1,0:T(8,128)(2,1)S(1)} %collective-permute-done.5.refs_2_.r2, bf16[272,256]{1,0:T(8,128)(2,1)S(1)} %get-tuple-element.62.refs_3_.r0, ...), custom_call_target="tpu_custom_call" | custom-call | tf_op jit(solution)/shard_map/group/pallas_call | solution.py:608
  14.4 0.3 collective-permute-done.6.halo
  14.7 0.0 collective-permute-start.8
  14.7 1.3 %collective-permute-start.7 = (bf16[272,256]{1,0:T(8,128)(2,1)S(1)}, bf16[272,256]{1,0:T(8,128)(2,1)S(1)}, u32[]{:S(2)}, u32[]{:S(2)}) collective-permute-start(bf16[272,256]{1,0:T(8,128)(2,1)S(1)} %group.1), channel_id=1, source_target_pairs={{0,16},{2,18},{4,20},{6,22},{8,24},{10,26},{12,28},{14,30},{1,17},... | collective-permute-start | bytes 417800 | tf_op jit(solution)/shard_map/ppermute | solution.py:484
  16.0 5.2 %collective-permute-done.8.near = bf16[272,256]{1,0:T(8,128)(2,1)S(1)} collective-permute-done((bf16[272,256]{1,0:T(8,128)(2,1)S(1)}, bf16[272,256]{1,0:T(8,128)(2,1)S(1)}, u32[]{:S(2)}, u32[]{:S(2)}) %collective-permute-start.8) | collective-permute-done | bytes 139296 | tf_op jit(solution)/shard_map/ppermute | solution.py:479
  21.2 4.8 %collective-permute-done.7.far = bf16[272,256]{1,0:T(8,128)(2,1)S(1)} collective-permute-done((bf16[272,256]{1,0:T(8,128)(2,1)S(1)}, bf16[272,256]{1,0:T(8,128)(2,1)S(1)}, u32[]{:S(2)}, u32[]{:S(2)}) %collective-permute-start.7) | collective-permute-done | bytes 139296 | tf_op jit(solution)/shard_map/ppermute | solution.py:484
  25.9 0.7 %entering.1 = (bf16[256,256]{1,0:T(8,128)(2,1)S(1)}, bf16[256,256]{1,0:T(8,128)(2,1)S(1)}, bf16[256,256]{1,0:T(8,128)(2,1)S(1)}, bf16[256,256]{1,0:T(8,128)(2,1)S(1)}) custom-call(bf16[272,256]{1,0:T(8,128)(2,1)S(1)} %collective-permute-done.3.refs_0_.r3, bf16[272,256]{1,0:T(8,128)(2,1)S(1)} %collective-permute-done.4.refs_1_.r1, ...), custom_call_target="tpu_custom_call" | custom-call | tf_op jit(solution)/shard_map/entering/pallas_call | solution.py:623
  26.6 2.0 %collective-permute-start.9 = (bf16[256,256]{1,0:T(8,128)(2,1)S(1)}, bf16[256,256]{1,0:T(8,128)(2,1)S(1)}, u32[]{:S(2)}, u32[]{:S(2)}) collective-permute-start(bf16[256,256]{1,0:T(8,128)(2,1)S(1)} %get-tuple-element.71), channel_id=1, source_target_pairs={{0,6},{2,4},{4,2},{6,0},{8,14},{10,12},{12,10},{14,8},{16,22},{18,... | collective-permute-start | bytes 393224 | tf_op jit(solution)/shard_map/ppermute | solution.py:474
  28.6 0.9 %collective-permute-start.10 = (bf16[256,256]{1,0:T(8,128)(2,1)S(1)}, bf16[256,256]{1,0:T(8,128)(2,1)S(1)}, u32[]{:S(2)}, u32[]{:S(2)}) collective-permute-start(bf16[256,256]{1,0:T(8,128)(2,1)S(1)} %get-tuple-element.72), channel_id=1, source_target_pairs={{0,2},{2,0},{4,6},{6,4},{8,10},{10,8},{12,14},{14,12},{16,18},{18,... | collective-permute-start | bytes 393224 | tf_op jit(solution)/shard_map/ppermute | solution.py:474
  29.5 0.7 %collective-permute-start.11 = (bf16[256,256]{1,0:T(8,128)(2,1)S(1)}, bf16[256,256]{1,0:T(8,128)(2,1)S(1)}, u32[]{:S(2)}, u32[]{:S(2)}) collective-permute-start(bf16[256,256]{1,0:T(8,128)(2,1)S(1)} %get-tuple-element.73), channel_id=1, source_target_pairs={{0,4},{2,6},{4,0},{6,2},{8,12},{10,14},{12,8},{14,10},{16,20},{18,... | collective-permute-start | bytes 393224 | tf_op jit(solution)/shard_map/ppermute | solution.py:474
  30.2 1.5 %intra.1 = (f32[256,1024]{1,0:T(8,128)S(1)}, bf16[256,256]{1,0:T(8,128)(2,1)S(1)}, f32[256,1024]{1,0:T(8,128)S(1)}) custom-call(bf16[256,768]{1,0:T(8,128)(2,1)S(1)} %get-tuple-element.41.x_early, bf16[256,256]{1,0:T(8,128)(2,1)S(1)} %get-tuple-element.57.x_late, f32[24,768]{1,0:T(8,128)S(1)} %get-tuple-element.54.aux.aux_early, ...), custom_call_target="tpu_custom_call" | custom-call | flops 600000000 | bytes 4000000 | tf_op jit(solution)/shard_map/intra/pallas_call | solution.py:633
  31.7 1.7 %collective-permute-done.9.f3 = bf16[256,256]{1,0:T(8,128)(2,1)S(1)} collective-permute-done((bf16[256,256]{1,0:T(8,128)(2,1)S(1)}, bf16[256,256]{1,0:T(8,128)(2,1)S(1)}, u32[]{:S(2)}, u32[]{:S(2)}) %collective-permute-start.9) | collective-permute-done | bytes 131104 | tf_op jit(solution)/shard_map/ppermute | solution.py:474
  33.4 1.1 %collective-permute-done.10.f1 = bf16[256,256]{1,0:T(8,128)(2,1)S(1)} collective-permute-done((bf16[256,256]{1,0:T(8,128)(2,1)S(1)}, bf16[256,256]{1,0:T(8,128)(2,1)S(1)}, u32[]{:S(2)}, u32[]{:S(2)}) %collective-permute-start.10) | collective-permute-done | bytes 131104 | tf_op jit(solution)/shard_map/ppermute | solution.py:474
  34.6 0.2 collective-permute-done.11.f2
  34.8 1.1 %back.1 = bf16[256,1024]{1,0:T(8,128)(2,1)} custom-call(bf16[256,256]{1,0:T(8,128)(2,1)S(1)} %get-tuple-element.69.c, bf16[256,256]{1,0:T(8,128)(2,1)S(1)} %collective-permute-done.9.f3, bf16[256,256]{1,0:T(8,128)(2,1)S(1)} %collective-permute-done.10.f1, bf16[256,256]{1,0:T(8,128)(2,1)S(1)} %collective-permute-done.11.f2, ...), custom_call_target="tpu_custom_call" | custom-call | tf_op jit(solution)/shard_map/back/pallas_call | solution.py:658
  (1 shorter events, 0.0 us)
Async XLA Ops:
  0.0 2.7 %collective-permute-start = (bf16[256,256]{1,0:T(8,128)(2,1)}, bf16[256,256]{1,0:T(8,128)(2,1)S(1)}, u32[]{:S(2)}, u32[]{:S(2)}) collective-permute-start(bf16[256,256]{1,0:T(8,128)(2,1)} %own_hbm.1), channel_id=1, source_target_pairs={{0,1},{1,0},{2,3},{3,2},{4,5},{5,4},{6,7},{7,6},{8,9},{9,8},{10,11... | collective-permute-start | bytes 393224 | tf_op jit(solution)/shard_map/ppermute | solution.py:517
  0.0 2.7 %collective-permute-start.1 = (f32[4,256]{1,0:T(4,128)}, f32[4,256]{1,0:T(4,128)S(1)}, u32[]{:S(2)}, u32[]{:S(2)}) collective-permute-start(f32[4,256]{1,0:T(4,128)} %own_taps_hbm.1), channel_id=1, source_target_pairs={{0,1},{1,0},{2,3},{3,2},{4,5},{5,4},{6,7},{7,6},{8,9},{9,8},{10,11... | collective-permute-start | bytes 12296 | tf_op jit(solution)/shard_map/ppermute | solution.py:517
  0.5 2.2 %collective-permute-start.2 = (f32[256]{0:T(256)}, f32[256]{0:T(256)S(1)}, u32[]{:S(2)}, u32[]{:S(2)}) collective-permute-start(f32[256]{0:T(256)} %param.16), channel_id=1, source_target_pairs={{0,1},{1,0},{2,3},{3,2},{4,5},{5,4},{6,7},{7,6},{8,9},{9,8},{10,11... | collective-permute-start | bytes 3080 | tf_op jit(solution)/shard_map/ppermute | solution.py:517
  3.4 7.5 %collective-permute-start.3 = (bf16[272,256]{1,0:T(8,128)(2,1)S(1)}, bf16[272,256]{1,0:T(8,128)(2,1)S(1)}, u32[]{:S(2)}, u32[]{:S(2)}) collective-permute-start(bf16[272,256]{1,0:T(8,128)(2,1)S(1)} %get-tuple-element.59), channel_id=1, source_target_pairs={{0,6},{2,4},{4,2},{6,0},{8,14},{10,12},{12,10},{14,8},{16,22},{18,... | collective-permute-start | bytes 417800 | tf_op jit(solution)/shard_map/ppermute | solution.py:474
  5.9 8.0 %collective-permute-start.4 = (bf16[272,256]{1,0:T(8,128)(2,1)S(1)}, bf16[272,256]{1,0:T(8,128)(2,1)S(1)}, u32[]{:S(2)}, u32[]{:S(2)}) collective-permute-start(bf16[272,256]{1,0:T(8,128)(2,1)S(1)} %get-tuple-element.60), channel_id=1, source_target_pairs={{0,2},{2,0},{4,6},{6,4},{8,10},{10,8},{12,14},{14,12},{16,18},{18,... | collective-permute-start | bytes 417800 | tf_op jit(solution)/shard_map/ppermute | solution.py:474
  6.5 7.5 %collective-permute-start.5 = (bf16[272,256]{1,0:T(8,128)(2,1)S(1)}, bf16[272,256]{1,0:T(8,128)(2,1)S(1)}, u32[]{:S(2)}, u32[]{:S(2)}) collective-permute-start(bf16[272,256]{1,0:T(8,128)(2,1)S(1)} %get-tuple-element.61), channel_id=1, source_target_pairs={{0,4},{2,6},{4,0},{6,2},{8,12},{10,14},{12,8},{14,10},{16,20},{18,... | collective-permute-start | bytes 417800 | tf_op jit(solution)/shard_map/ppermute | solution.py:474
  7.0 7.8 %collective-permute-start.6 = (bf16[16,1536]{1,0:T(8,128)(2,1)S(1)}, bf16[16,1536]{1,0:T(8,128)(2,1)S(1)}, u32[]{:S(2)}, u32[]{:S(2)}) collective-permute-start(bf16[16,1536]{1,0:T(8,128)(2,1)S(1)} %get-tuple-element.64), channel_id=1, source_target_pairs={{0,2},{2,4},{4,6},{6,8},{8,10},{10,12},{12,14},{14,16},{16,18},{18... | collective-permute-start | bytes 147464 | tf_op jit(solution)/shard_map/ppermute | solution.py:484
  14.7 6.4 %collective-permute-start.8 = (bf16[272,256]{1,0:T(8,128)(2,1)S(1)}, bf16[272,256]{1,0:T(8,128)(2,1)S(1)}, u32[]{:S(2)}, u32[]{:S(2)}) collective-permute-start(bf16[272,256]{1,0:T(8,128)(2,1)S(1)} %group.1), channel_id=1, source_target_pairs={{0,8},{2,10},{4,12},{6,14},{8,16},{10,18},{12,20},{14,22},{16,24},... | collective-permute-start | bytes 417800 | tf_op jit(solution)/shard_map/ppermute | solution.py:479
  14.7 11.2 %collective-permute-start.7 = (bf16[272,256]{1,0:T(8,128)(2,1)S(1)}, bf16[272,256]{1,0:T(8,128)(2,1)S(1)}, u32[]{:S(2)}, u32[]{:S(2)}) collective-permute-start(bf16[272,256]{1,0:T(8,128)(2,1)S(1)} %group.1), channel_id=1, source_target_pairs={{0,16},{2,18},{4,20},{6,22},{8,24},{10,26},{12,28},{14,30},{1,17},... | collective-permute-start | bytes 417800 | tf_op jit(solution)/shard_map/ppermute | solution.py:484
  26.6 6.8 %collective-permute-start.9 = (bf16[256,256]{1,0:T(8,128)(2,1)S(1)}, bf16[256,256]{1,0:T(8,128)(2,1)S(1)}, u32[]{:S(2)}, u32[]{:S(2)}) collective-permute-start(bf16[256,256]{1,0:T(8,128)(2,1)S(1)} %get-tuple-element.71), channel_id=1, source_target_pairs={{0,6},{2,4},{4,2},{6,0},{8,14},{10,12},{12,10},{14,8},{16,22},{18,... | collective-permute-start | bytes 393224 | tf_op jit(solution)/shard_map/ppermute | solution.py:474
  28.6 6.0 %collective-permute-start.10 = (bf16[256,256]{1,0:T(8,128)(2,1)S(1)}, bf16[256,256]{1,0:T(8,128)(2,1)S(1)}, u32[]{:S(2)}, u32[]{:S(2)}) collective-permute-start(bf16[256,256]{1,0:T(8,128)(2,1)S(1)} %get-tuple-element.72), channel_id=1, source_target_pairs={{0,2},{2,0},{4,6},{6,4},{8,10},{10,8},{12,14},{14,12},{16,18},{18,... | collective-permute-start | bytes 393224 | tf_op jit(solution)/shard_map/ppermute | solution.py:474
  29.5 5.3 %collective-permute-start.11 = (bf16[256,256]{1,0:T(8,128)(2,1)S(1)}, bf16[256,256]{1,0:T(8,128)(2,1)S(1)}, u32[]{:S(2)}, u32[]{:S(2)}) collective-permute-start(bf16[256,256]{1,0:T(8,128)(2,1)S(1)} %get-tuple-element.73), channel_id=1, source_target_pairs={{0,4},{2,6},{4,0},{6,2},{8,12},{10,14},{12,8},{14,10},{16,20},{18,... | collective-permute-start | bytes 393224 | tf_op jit(solution)/shard_map/ppermute | solution.py:474

commit v6 on v5

--- a/solution.py
+++ b/solution.py
@@ -26,8 +26,8 @@
     return high, value - high
 
 
-def silu(v):
-    return 0.5 * v * (1.0 + jnp.tanh(0.5 * v))
+def silu(half):
+    return half + half * jnp.tanh(half)
 
 
 def iota(shape, dim):
@@ -132,17 +132,18 @@
     block = x.shape[0]
     count = taps.shape[0]
     pairs = [
-        (x_hbm, x), (offset_hbm, offset), (step_hbm, step), (step_bias_hbm, step_bias), (decay_hbm, decay_log),
-        (skip_hbm, skip), (taps_hbm, taps), (bias_hbm, bias), (own_taps_hbm, own_taps), (own_bias_hbm, own_bias),
-        (own_hbm, own),
+        (offset_hbm, offset), (step_hbm, step), (step_bias_hbm, step_bias), (decay_hbm, decay_log),
+        (x_hbm, x), (taps_hbm, taps), (bias_hbm, bias), (skip_hbm, skip), (own_taps_hbm, own_taps),
+        (own_bias_hbm, own_bias), (own_hbm, own),
     ]
     copies = [pltpu.make_async_copy(*pair, sems.at[k]) for k, pair in enumerate(pairs)]
     for copy in copies:
         copy.start()
-    for copy in copies[1:8]:
-        copy.wait()
+    copies[0].wait()
     for lag, matrix in enumerate(lag_matrices(offset_columns(offset[...]), count)):
         lags[lag] = matrix
+    for copy in copies[1:4]:
+        copy.wait()
     time_step, rate_sum = rates(step[...], column(step_bias[...]), column(decay_log[...]))
     step_out[...] = time_step
     sums_out[...] = rate_sum
@@ -152,13 +153,18 @@
     gate = jnp.exp(jnp.where(last_offset >= block - 1 - place, last - rate_sum, NEG)) * time_step
     passing = jnp.exp(last) * (last_offset >= block).astype(F32)
     passing_out[...] = jnp.broadcast_to(passing, passing_out.shape)
+    for copy in copies[4:8]:
+        copy.wait()
+    taps[...] = 0.5 * taps[...]
+    bias[...] = 0.5 * bias[...]
     early_parts[...] = turned(jnp.where(place == count - 1, column(skip[...]), gate))[0:TAIL]
     late_parts[...] = turned(jnp.where(place >= count - 1, gate, 0.0))
-    copies[0].wait()
     for slot, k in enumerate((1, 2, 3)):
         channel_slice(k, slot, x, taps, bias, lags, late_parts, early_parts, x_out, gated, aux)
     for copy in copies[8:]:
         copy.wait()
+    own_taps[...] = 0.5 * own_taps[...]
+    own_bias[...] = 0.5 * own_bias[...]
 
 
 def message(out, k, state, passing, offset, count, gates_and_x, b_tail):
@@ -194,8 +200,8 @@
     ends[:, 0:channels] = x[block - HALO : block, :]
     ends[:, channels : channels + state_size] = own[block - HALO : block, :]
     ends[:, channels + state_size :] = other[block - HALO : block, :]
-    taps = jnp.where(first, own_taps[...], other_taps[...])
-    bias = jnp.where(first, own_bias[...], other_bias[...])
+    taps = jnp.where(first, own_taps[...], 0.5 * other_taps[...])
+    bias = jnp.where(first, own_bias[...], 0.5 * other_bias[...])
     source = jnp.where(first, own[...].astype(F32), other[...].astype(F32))
     before = convolve(source.astype(BF16), taps, bias, [lags[lag] for lag in range(count - 1)])
     value = silu(before)
@@ -304,8 +310,8 @@
             b, x = early_tokens(tails[k], before, taps, bias)
             early_b.append(b)
             early_x.append(x * factors[k])
-        b_turned = jnp.concatenate(early_b, axis=0).T.astype(BF16)
-        added = dot(b_turned, jnp.concatenate(early_x, axis=0).astype(BF16))
+        b_rows = jnp.concatenate(early_b, axis=0).astype(BF16)
+        added = dot(b_rows, jnp.concatenate(early_x, axis=0).astype(BF16), ((0,), (0,)))
         step = 64
         for top in range(0, rows, step):
             part = slice(top, top + step)
@@ -358,12 +364,12 @@
             b, x = early_tokens(tails[k], tails[k - 1] if k else near_tail, taps, bias)
             early_b.append(b)
             early_x.append(x)
-        b_turned = jnp.concatenate(early_b, axis=0).T.astype(BF16)
+        b_rows = jnp.concatenate(early_b, axis=0).astype(BF16)
         x_rows = jnp.concatenate(early_x, axis=0).astype(BF16)
-        added = [dot(b_turned[:, : 2 * TAIL], x_rows[: 2 * TAIL])]
+        added = [dot(b_rows[: 2 * TAIL], x_rows[: 2 * TAIL], ((0,), (0,)))]
         for k in range(GROUP - 1):
             part = slice((k + 2) * TAIL, (k + 3) * TAIL)
-            added.append(dot(b_turned[:, part], x_rows[part]))
+            added.append(dot(b_rows[part], x_rows[part], ((0,), (0,))))
         step = 32
         for top in range(0, rows, step):
             part = slice(top, top + step)
@@ -418,8 +424,8 @@
     b_full[...] = b[...]
     early = patched(b_aux[8:16, :], jnp.where(first, own_halo, other_halo), b_aux[0:count, :], offset_col)
     b_full[0:16, :] = jnp.concatenate([early, b[0:16, :].astype(F32)[8:16]], axis=0).astype(BF16)
-    c_taps = jnp.where(first, other_taps[...], own_taps[...])
-    c_bias = jnp.where(first, other_bias[...], own_bias[...])
+    c_taps = jnp.where(first, 0.5 * other_taps[...], own_taps[...])
+    c_bias = jnp.where(first, 0.5 * other_bias[...], own_bias[...])
     c_source = jnp.where(first, other[...].astype(F32), own[...].astype(F32)).astype(BF16)
     before = convolve(c_source, c_taps, c_bias, [lags[lag] for lag in range(count - 1)])
     c_value = silu(before)

time: 36 us -> 35.7 us (level)
  transfers between devices with their start and end apart: 12 -> 12, of which waited for: 7 -> 7; matrix products, arithmetic and copies ran while one was open for 0% -> 0% of each run, Pallas kernels for 13% -> 12%
where the time goes in v6:
time: 35.7 us; the launch traced here: 35.5 us
  waiting for transfers between devices  16.4 us (46%)
  starting transfers between devices  12.3 us (34%)
  Pallas kernels  6.72 us (19%)
    ppermute x6, starting transfers between devices, exchange(): lax.ppermute(array, 'seq', [(i, i ^ mask) for i in range(lax.axis_size('s...  7.11 us
    ppermute x6, waiting for transfers between devices, exchange(): lax.ppermute(array, 'seq', [(i, i ^ mask) for i in range(lax.axis_size('s...  6.15 us
    ppermute x1, waiting for transfers between devices, turned_on(): lax.ppermute(array, 'seq', [(i, (i + distance) % count) for i in range(co...  5.16 us
    ppermute x2, waiting for transfers between devices, shifted(): lax.ppermute(array, 'seq', [(i, i + distance) for i in range(count - dist...  5.11 us
    ppermute x2, starting transfers between devices, shifted(): lax.ppermute(array, 'seq', [(i, i + distance) for i in range(count - dist...  4.67 us
    pallas_call x1, Pallas kernels, on_device(): pl.pallas_call(channels_kernel, out_shape=[others, others, jax.ShapeDtype...  1.96 us
    pallas_call x1, Pallas kernels, on_device(): pl.pallas_call(intra_kernel, out_shape=[jax.ShapeDtypeStruct((block, chan...  1.49 us
    pallas_call x1, Pallas kernels, on_device(): pl.pallas_call(back_kernel, out_shape=out_shape, in_specs=[vmem] * (GROUP...  1.06 us
  transfers between devices with their start and end apart: 12, of which 7 were waited for; matrix products, arithmetic and copies ran while one was open for 0% of the time, Pallas kernels for 12%

profile of v6, /device:TPU:24, one launch (start us, length us, event | category | flops | bytes accessed | tf_op | source)
XLA Modules:
  0.0 35.5 jit_solution(4076112336116259662)
XLA Ops:
  0.0 0.0 collective-permute-start
  0.0 0.5 %collective-permute-start.1 = (f32[4,256]{1,0:T(4,128)}, f32[4,256]{1,0:T(4,128)S(1)}, u32[]{:S(2)}, u32[]{:S(2)}) collective-permute-start(f32[4,256]{1,0:T(4,128)} %own_taps_hbm.1), channel_id=1, source_target_pairs={{0,1},{1,0},{2,3},{3,2},{4,5},{5,4},{6,7},{7,6},{8,9},{9,8},{10,11... | collective-permute-start | bytes 12296 | tf_op jit(solution)/shard_map/ppermute | solution.py:523
  0.5 0.0 collective-permute-start.2
  0.5 2.0 %channels.1 = (bf16[256,768]{1,0:T(8,128)(2,1)S(1)}, bf16[256,768]{1,0:T(8,128)(2,1)S(1)}, f32[24,768]{1,0:T(8,128)S(1)}, f32[16,128]{1,0:T(8,128)S(1)}, f32[16,...) custom-call(bf16[256,1024]{1,0:T(8,128)(2,1)} %x_hbm.1, ...), custom_call_target="tpu_custom_call" | custom-call | tf_op jit(solution)/shard_map/channels/pallas_call | solution.py:531
  2.5 0.0 collective-permute-done.2
  2.5 0.0 collective-permute-done.1.other_taps
  2.5 0.0 collective-permute-done.other
  2.5 0.6 %states.1 = (bf16[272,256]{1,0:T(8,128)(2,1)S(1)}, bf16[272,256]{1,0:T(8,128)(2,1)S(1)}, bf16[272,256]{1,0:T(8,128)(2,1)S(1)}, bf16[256,256]{1,0:T(8,128)(2,1)S(...) custom-call(bf16[256,1024]{1,0:T(8,128)(2,1)S(1)} %get-tuple-element, ...), custom_call_target="tpu_custom_call" | custom-call | tf_op jit(solution)/shard_map/states/pallas_call | solution.py:571
  3.2 2.5 %collective-permute-start.3 = (bf16[272,256]{1,0:T(8,128)(2,1)S(1)}, bf16[272,256]{1,0:T(8,128)(2,1)S(1)}, u32[]{:S(2)}, u32[]{:S(2)}) collective-permute-start(bf16[272,256]{1,0:T(8,128)(2,1)S(1)} %get-tuple-element.59), channel_id=1, source_target_pairs={{0,6},{2,4},{4,2},{6,0},{8,14},{10,12},{12,10},{14,8},{16,22},{18,... | collective-permute-start | bytes 417800 | tf_op jit(solution)/shard_map/ppermute | solution.py:480
  5.7 0.5 %collective-permute-start.4 = (bf16[272,256]{1,0:T(8,128)(2,1)S(1)}, bf16[272,256]{1,0:T(8,128)(2,1)S(1)}, u32[]{:S(2)}, u32[]{:S(2)}) collective-permute-start(bf16[272,256]{1,0:T(8,128)(2,1)S(1)} %get-tuple-element.60), channel_id=1, source_target_pairs={{0,2},{2,0},{4,6},{6,4},{8,10},{10,8},{12,14},{14,12},{16,18},{18,... | collective-permute-start | bytes 417800 | tf_op jit(solution)/shard_map/ppermute | solution.py:480
  6.2 0.5 %collective-permute-start.5 = (bf16[272,256]{1,0:T(8,128)(2,1)S(1)}, bf16[272,256]{1,0:T(8,128)(2,1)S(1)}, u32[]{:S(2)}, u32[]{:S(2)}) collective-permute-start(bf16[272,256]{1,0:T(8,128)(2,1)S(1)} %get-tuple-element.61), channel_id=1, source_target_pairs={{0,4},{2,6},{4,0},{6,2},{8,12},{10,14},{12,8},{14,10},{16,20},{18,... | collective-permute-start | bytes 417800 | tf_op jit(solution)/shard_map/ppermute | solution.py:480
  6.7 3.4 %collective-permute-start.6 = (bf16[16,1536]{1,0:T(8,128)(2,1)S(1)}, bf16[16,1536]{1,0:T(8,128)(2,1)S(1)}, u32[]{:S(2)}, u32[]{:S(2)}) collective-permute-start(bf16[16,1536]{1,0:T(8,128)(2,1)S(1)} %get-tuple-element.64), channel_id=1, source_target_pairs={{0,2},{2,4},{4,6},{6,8},{8,10},{10,12},{12,14},{14,16},{16,18},{18... | collective-permute-start | bytes 147464 | tf_op jit(solution)/shard_map/ppermute | solution.py:490
  10.1 0.6 %rest.1 = (bf16[272,256]{1,0:T(8,128)(2,1)S(1)}, bf16[256,256]{1,0:T(8,128)(2,1)S(1)}, f32[24,256]{1,0:T(8,128)S(1)}) custom-call(bf16[256,1024]{1,0:T(8,128)(2,1)S(1)} %get-tuple-element.42.x, f32[4,1024]{1,0:T(4,128)S(1)} %get-tuple-element.43.taps.refs_5_.x_taps, f32[1,1024]{1,0:T(1,128)S(1)} %get-tuple-element.44.bias.refs_6_.x_bias, ...), custom_call_target="tpu_custom_call" | custom-call | flops 400000000 | bytes 2000000 | tf_op jit(solution)/shard_map/rest/pallas_call | solution.py:590
  10.7 0.0 collective-permute-done.3.refs_0_.r3
  10.7 3.0 %collective-permute-done.4.refs_1_.r1 = bf16[272,256]{1,0:T(8,128)(2,1)S(1)} collective-permute-done((bf16[272,256]{1,0:T(8,128)(2,1)S(1)}, bf16[272,256]{1,0:T(8,128)(2,1)S(1)}, u32[]{:S(2)}, u32[]{:S(2)}) %collective-permute-start.4) | collective-permute-done | bytes 139296 | tf_op jit(solution)/shard_map/ppermute | solution.py:480
  13.7 0.0 collective-permute-done.5.refs_2_.r2
  13.7 0.4 %group.1 = bf16[272,256]{1,0:T(8,128)(2,1)S(1)} custom-call(bf16[272,256]{1,0:T(8,128)(2,1)S(1)} %collective-permute-done.3.refs_0_.r3, bf16[272,256]{1,0:T(8,128)(2,1)S(1)} %collective-permute-done.4.refs_1_.r1, bf16[272,256]{1,0:T(8,128)(2,1)S(1)} %collective-permute-done.5.refs_2_.r2, bf16[272,256]{1,0:T(8,128)(2,1)S(1)} %get-tuple-element.62.refs_3_.r0, ...), custom_call_target="tpu_custom_call" | custom-call | tf_op jit(solution)/shard_map/group/pallas_call | solution.py:614
  14.1 0.3 collective-permute-done.6.halo
  14.5 0.0 collective-permute-start.8
  14.5 1.3 %collective-permute-start.7 = (bf16[272,256]{1,0:T(8,128)(2,1)S(1)}, bf16[272,256]{1,0:T(8,128)(2,1)S(1)}, u32[]{:S(2)}, u32[]{:S(2)}) collective-permute-start(bf16[272,256]{1,0:T(8,128)(2,1)S(1)} %group.1), channel_id=1, source_target_pairs={{0,16},{2,18},{4,20},{6,22},{8,24},{10,26},{12,28},{14,30},{1,17},... | collective-permute-start | bytes 417800 | tf_op jit(solution)/shard_map/ppermute | solution.py:490
  15.8 5.2 %collective-permute-done.8.near = bf16[272,256]{1,0:T(8,128)(2,1)S(1)} collective-permute-done((bf16[272,256]{1,0:T(8,128)(2,1)S(1)}, bf16[272,256]{1,0:T(8,128)(2,1)S(1)}, u32[]{:S(2)}, u32[]{:S(2)}) %collective-permute-start.8) | collective-permute-done | bytes 139296 | tf_op jit(solution)/shard_map/ppermute | solution.py:485
  20.9 4.8 %collective-permute-done.7.far = bf16[272,256]{1,0:T(8,128)(2,1)S(1)} collective-permute-done((bf16[272,256]{1,0:T(8,128)(2,1)S(1)}, bf16[272,256]{1,0:T(8,128)(2,1)S(1)}, u32[]{:S(2)}, u32[]{:S(2)}) %collective-permute-start.7) | collective-permute-done | bytes 139296 | tf_op jit(solution)/shard_map/ppermute | solution.py:490
  25.7 0.6 %entering.1 = (bf16[256,256]{1,0:T(8,128)(2,1)S(1)}, bf16[256,256]{1,0:T(8,128)(2,1)S(1)}, bf16[256,256]{1,0:T(8,128)(2,1)S(1)}, bf16[256,256]{1,0:T(8,128)(2,1)S(1)}) custom-call(bf16[272,256]{1,0:T(8,128)(2,1)S(1)} %collective-permute-done.3.refs_0_.r3, bf16[272,256]{1,0:T(8,128)(2,1)S(1)} %collective-permute-done.4.refs_1_.r1, ...), custom_call_target="tpu_custom_call" | custom-call | tf_op jit(solution)/shard_map/entering/pallas_call | solution.py:629
  26.3 2.0 %collective-permute-start.9 = (bf16[256,256]{1,0:T(8,128)(2,1)S(1)}, bf16[256,256]{1,0:T(8,128)(2,1)S(1)}, u32[]{:S(2)}, u32[]{:S(2)}) collective-permute-start(bf16[256,256]{1,0:T(8,128)(2,1)S(1)} %get-tuple-element.71), channel_id=1, source_target_pairs={{0,6},{2,4},{4,2},{6,0},{8,14},{10,12},{12,10},{14,8},{16,22},{18,... | collective-permute-start | bytes 393224 | tf_op jit(solution)/shard_map/ppermute | solution.py:480
  28.3 0.9 %collective-permute-start.10 = (bf16[256,256]{1,0:T(8,128)(2,1)S(1)}, bf16[256,256]{1,0:T(8,128)(2,1)S(1)}, u32[]{:S(2)}, u32[]{:S(2)}) collective-permute-start(bf16[256,256]{1,0:T(8,128)(2,1)S(1)} %get-tuple-element.72), channel_id=1, source_target_pairs={{0,2},{2,0},{4,6},{6,4},{8,10},{10,8},{12,14},{14,12},{16,18},{18,... | collective-permute-start | bytes 393224 | tf_op jit(solution)/shard_map/ppermute | solution.py:480
  29.1 0.7 %collective-permute-start.11 = (bf16[256,256]{1,0:T(8,128)(2,1)S(1)}, bf16[256,256]{1,0:T(8,128)(2,1)S(1)}, u32[]{:S(2)}, u32[]{:S(2)}) collective-permute-start(bf16[256,256]{1,0:T(8,128)(2,1)S(1)} %get-tuple-element.73), channel_id=1, source_target_pairs={{0,4},{2,6},{4,0},{6,2},{8,12},{10,14},{12,8},{14,10},{16,20},{18,... | collective-permute-start | bytes 393224 | tf_op jit(solution)/shard_map/ppermute | solution.py:480
  29.9 1.5 %intra.1 = (f32[256,1024]{1,0:T(8,128)S(1)}, bf16[256,256]{1,0:T(8,128)(2,1)S(1)}, f32[256,1024]{1,0:T(8,128)S(1)}) custom-call(bf16[256,768]{1,0:T(8,128)(2,1)S(1)} %get-tuple-element.41.x_early, bf16[256,256]{1,0:T(8,128)(2,1)S(1)} %get-tuple-element.57.x_late, f32[24,768]{1,0:T(8,128)S(1)} %get-tuple-element.54.aux.aux_early, ...), custom_call_target="tpu_custom_call" | custom-call | flops 600000000 | bytes 4000000 | tf_op jit(solution)/shard_map/intra/pallas_call | solution.py:639
  31.3 1.8 %collective-permute-done.9.f3 = bf16[256,256]{1,0:T(8,128)(2,1)S(1)} collective-permute-done((bf16[256,256]{1,0:T(8,128)(2,1)S(1)}, bf16[256,256]{1,0:T(8,128)(2,1)S(1)}, u32[]{:S(2)}, u32[]{:S(2)}) %collective-permute-start.9) | collective-permute-done | bytes 131104 | tf_op jit(solution)/shard_map/ppermute | solution.py:480
  33.1 1.1 %collective-permute-done.10.f1 = bf16[256,256]{1,0:T(8,128)(2,1)S(1)} collective-permute-done((bf16[256,256]{1,0:T(8,128)(2,1)S(1)}, bf16[256,256]{1,0:T(8,128)(2,1)S(1)}, u32[]{:S(2)}, u32[]{:S(2)}) %collective-permute-start.10) | collective-permute-done | bytes 131104 | tf_op jit(solution)/shard_map/ppermute | solution.py:480
  34.2 0.3 collective-permute-done.11.f2
  34.5 1.1 %back.1 = bf16[256,1024]{1,0:T(8,128)(2,1)} custom-call(bf16[256,256]{1,0:T(8,128)(2,1)S(1)} %get-tuple-element.69.c, bf16[256,256]{1,0:T(8,128)(2,1)S(1)} %collective-permute-done.9.f3, bf16[256,256]{1,0:T(8,128)(2,1)S(1)} %collective-permute-done.10.f1, bf16[256,256]{1,0:T(8,128)(2,1)S(1)} %collective-permute-done.11.f2, ...), custom_call_target="tpu_custom_call" | custom-call | tf_op jit(solution)/shard_map/back/pallas_call | solution.py:664
  (1 shorter events, 0.0 us)
Async XLA Ops:
  0.0 2.5 %collective-permute-start = (bf16[256,256]{1,0:T(8,128)(2,1)}, bf16[256,256]{1,0:T(8,128)(2,1)S(1)}, u32[]{:S(2)}, u32[]{:S(2)}) collective-permute-start(bf16[256,256]{1,0:T(8,128)(2,1)} %own_hbm.1), channel_id=1, source_target_pairs={{0,1},{1,0},{2,3},{3,2},{4,5},{5,4},{6,7},{7,6},{8,9},{9,8},{10,11... | collective-permute-start | bytes 393224 | tf_op jit(solution)/shard_map/ppermute | solution.py:523
  0.0 2.5 %collective-permute-start.1 = (f32[4,256]{1,0:T(4,128)}, f32[4,256]{1,0:T(4,128)S(1)}, u32[]{:S(2)}, u32[]{:S(2)}) collective-permute-start(f32[4,256]{1,0:T(4,128)} %own_taps_hbm.1), channel_id=1, source_target_pairs={{0,1},{1,0},{2,3},{3,2},{4,5},{5,4},{6,7},{7,6},{8,9},{9,8},{10,11... | collective-permute-start | bytes 12296 | tf_op jit(solution)/shard_map/ppermute | solution.py:523
  0.5 2.0 %collective-permute-start.2 = (f32[256]{0:T(256)}, f32[256]{0:T(256)S(1)}, u32[]{:S(2)}, u32[]{:S(2)}) collective-permute-start(f32[256]{0:T(256)} %param.16), channel_id=1, source_target_pairs={{0,1},{1,0},{2,3},{3,2},{4,5},{5,4},{6,7},{7,6},{8,9},{9,8},{10,11... | collective-permute-start | bytes 3080 | tf_op jit(solution)/shard_map/ppermute | solution.py:523
  3.2 7.5 %collective-permute-start.3 = (bf16[272,256]{1,0:T(8,128)(2,1)S(1)}, bf16[272,256]{1,0:T(8,128)(2,1)S(1)}, u32[]{:S(2)}, u32[]{:S(2)}) collective-permute-start(bf16[272,256]{1,0:T(8,128)(2,1)S(1)} %get-tuple-element.59), channel_id=1, source_target_pairs={{0,6},{2,4},{4,2},{6,0},{8,14},{10,12},{12,10},{14,8},{16,22},{18,... | collective-permute-start | bytes 417800 | tf_op jit(solution)/shard_map/ppermute | solution.py:480
  5.7 8.0 %collective-permute-start.4 = (bf16[272,256]{1,0:T(8,128)(2,1)S(1)}, bf16[272,256]{1,0:T(8,128)(2,1)S(1)}, u32[]{:S(2)}, u32[]{:S(2)}) collective-permute-start(bf16[272,256]{1,0:T(8,128)(2,1)S(1)} %get-tuple-element.60), channel_id=1, source_target_pairs={{0,2},{2,0},{4,6},{6,4},{8,10},{10,8},{12,14},{14,12},{16,18},{18,... | collective-permute-start | bytes 417800 | tf_op jit(solution)/shard_map/ppermute | solution.py:480
  6.2 7.5 %collective-permute-start.5 = (bf16[272,256]{1,0:T(8,128)(2,1)S(1)}, bf16[272,256]{1,0:T(8,128)(2,1)S(1)}, u32[]{:S(2)}, u32[]{:S(2)}) collective-permute-start(bf16[272,256]{1,0:T(8,128)(2,1)S(1)} %get-tuple-element.61), channel_id=1, source_target_pairs={{0,4},{2,6},{4,0},{6,2},{8,12},{10,14},{12,8},{14,10},{16,20},{18,... | collective-permute-start | bytes 417800 | tf_op jit(solution)/shard_map/ppermute | solution.py:480
  6.7 7.8 %collective-permute-start.6 = (bf16[16,1536]{1,0:T(8,128)(2,1)S(1)}, bf16[16,1536]{1,0:T(8,128)(2,1)S(1)}, u32[]{:S(2)}, u32[]{:S(2)}) collective-permute-start(bf16[16,1536]{1,0:T(8,128)(2,1)S(1)} %get-tuple-element.64), channel_id=1, source_target_pairs={{0,2},{2,4},{4,6},{6,8},{8,10},{10,12},{12,14},{14,16},{16,18},{18... | collective-permute-start | bytes 147464 | tf_op jit(solution)/shard_map/ppermute | solution.py:490
  14.5 6.5 %collective-permute-start.8 = (bf16[272,256]{1,0:T(8,128)(2,1)S(1)}, bf16[272,256]{1,0:T(8,128)(2,1)S(1)}, u32[]{:S(2)}, u32[]{:S(2)}) collective-permute-start(bf16[272,256]{1,0:T(8,128)(2,1)S(1)} %group.1), channel_id=1, source_target_pairs={{0,8},{2,10},{4,12},{6,14},{8,16},{10,18},{12,20},{14,22},{16,24},... | collective-permute-start | bytes 417800 | tf_op jit(solution)/shard_map/ppermute | solution.py:485
  14.5 11.2 %collective-permute-start.7 = (bf16[272,256]{1,0:T(8,128)(2,1)S(1)}, bf16[272,256]{1,0:T(8,128)(2,1)S(1)}, u32[]{:S(2)}, u32[]{:S(2)}) collective-permute-start(bf16[272,256]{1,0:T(8,128)(2,1)S(1)} %group.1), channel_id=1, source_target_pairs={{0,16},{2,18},{4,20},{6,22},{8,24},{10,26},{12,28},{14,30},{1,17},... | collective-permute-start | bytes 417800 | tf_op jit(solution)/shard_map/ppermute | solution.py:490
  26.3 6.8 %collective-permute-start.9 = (bf16[256,256]{1,0:T(8,128)(2,1)S(1)}, bf16[256,256]{1,0:T(8,128)(2,1)S(1)}, u32[]{:S(2)}, u32[]{:S(2)}) collective-permute-start(bf16[256,256]{1,0:T(8,128)(2,1)S(1)} %get-tuple-element.71), channel_id=1, source_target_pairs={{0,6},{2,4},{4,2},{6,0},{8,14},{10,12},{12,10},{14,8},{16,22},{18,... | collective-permute-start | bytes 393224 | tf_op jit(solution)/shard_map/ppermute | solution.py:480
  28.3 5.9 %collective-permute-start.10 = (bf16[256,256]{1,0:T(8,128)(2,1)S(1)}, bf16[256,256]{1,0:T(8,128)(2,1)S(1)}, u32[]{:S(2)}, u32[]{:S(2)}) collective-permute-start(bf16[256,256]{1,0:T(8,128)(2,1)S(1)} %get-tuple-element.72), channel_id=1, source_target_pairs={{0,2},{2,0},{4,6},{6,4},{8,10},{10,8},{12,14},{14,12},{16,18},{18,... | collective-permute-start | bytes 393224 | tf_op jit(solution)/shard_map/ppermute | solution.py:480
  29.1 5.4 %collective-permute-start.11 = (bf16[256,256]{1,0:T(8,128)(2,1)S(1)}, bf16[256,256]{1,0:T(8,128)(2,1)S(1)}, u32[]{:S(2)}, u32[]{:S(2)}) collective-permute-start(bf16[256,256]{1,0:T(8,128)(2,1)S(1)} %get-tuple-element.73), channel_id=1, source_target_pairs={{0,4},{2,6},{4,0},{6,2},{8,12},{10,14},{12,8},{14,10},{16,20},{18,... | collective-permute-start | bytes 393224 | tf_op jit(solution)/shard_map/ppermute | solution.py:480

commit v7 on v6

--- a/solution.py
+++ b/solution.py
@@ -9,7 +9,7 @@
 GROUP = 4
 TAIL = 16
 GATE_AT, X_LAST_AT, X_FIRST_AT, B_LAST_AT, B_FIRST_AT = 1, 4, 7, 10, 13
-HALO = 16
+ENDS = 512
 LANES = 128
 NEG = -1e30
 F32 = jnp.float32
@@ -197,9 +197,12 @@
     block, state_size = own.shape
     count = own_taps.shape[0]
     channels = x.shape[1]
-    ends[:, 0:channels] = x[block - HALO : block, :]
-    ends[:, channels : channels + state_size] = own[block - HALO : block, :]
-    ends[:, channels + state_size :] = other[block - HALO : block, :]
+    last_rows = jnp.concatenate(
+        [part[block - TAIL : block, :].astype(F32)[TAIL - 3 :] for part in (x, own, other)], axis=1
+    )
+    packed = [last_rows[:, at : at + ENDS] for at in range(0, channels + 2 * state_size, ENDS)]
+    blank = jnp.zeros((TAIL - 3 * len(packed), ENDS), F32)
+    ends[...] = jnp.concatenate(packed + [blank], axis=0).astype(BF16)
     taps = jnp.where(first, own_taps[...], 0.5 * other_taps[...])
     bias = jnp.where(first, own_bias[...], 0.5 * other_bias[...])
     source = jnp.where(first, own[...].astype(F32), other[...].astype(F32))
@@ -312,7 +315,7 @@
             early_x.append(x * factors[k])
         b_rows = jnp.concatenate(early_b, axis=0).astype(BF16)
         added = dot(b_rows, jnp.concatenate(early_x, axis=0).astype(BF16), ((0,), (0,)))
-        step = 64
+        step = 32
         for top in range(0, rows, step):
             part = slice(top, top + step)
             value = added[part]
@@ -370,7 +373,7 @@
         for k in range(GROUP - 1):
             part = slice((k + 2) * TAIL, (k + 3) * TAIL)
             added.append(dot(b_rows[part], x_rows[part], ((0,), (0,))))
-        step = 32
+        step = 16
         for top in range(0, rows, step):
             part = slice(top, top + step)
             value = from_near * near[part, :].astype(F32) + far_factor * far[part, :].astype(F32) + added[0][part]
@@ -386,7 +389,7 @@
 def patched(before, halo, taps, offset_col):
     width = before.shape[1]
     count = taps.shape[0]
-    extended = jnp.concatenate([halo[HALO - 8 :].astype(F32), jnp.zeros((8, width), F32)], axis=0)
+    extended = jnp.concatenate([jnp.zeros((5, width), F32), halo, jnp.zeros((8, width), F32)], axis=0)
     total = before
     for lag in range(1, count):
         shifted_rows = extended[8 - lag : 16 - lag]
@@ -417,10 +420,14 @@
     columns[...] = rate_sum.T
     offset_col = offset_columns(offset[...])
 
-    early = patched(aux[0:8, :], halo[:, 0:channels], x_taps[...], offset_col)
+    packed = halo[...].astype(F32)
+    last_rows = jnp.concatenate(
+        [packed[3 * k : 3 * k + 3] for k in range((channels + 2 * state_size) // ENDS)], axis=1
+    )
+    early = patched(aux[0:8, :], last_rows[:, 0:channels], x_taps[...], offset_col)
     x_full[0:16, :] = jnp.concatenate([early, x_full[0:16, :].astype(F32)[8:16]], axis=0).astype(BF16)
-    own_halo = halo[:, channels : channels + state_size].astype(F32)
-    other_halo = halo[:, channels + state_size :].astype(F32)
+    own_halo = last_rows[:, channels : channels + state_size]
+    other_halo = last_rows[:, channels + state_size :]
     b_full[...] = b[...]
     early = patched(b_aux[8:16, :], jnp.where(first, own_halo, other_halo), b_aux[0:count, :], offset_col)
     b_full[0:16, :] = jnp.concatenate([early, b[0:16, :].astype(F32)[8:16]], axis=0).astype(BF16)
@@ -578,7 +585,7 @@
             jax.ShapeDtypeStruct((16, state_size), F32),
             jax.ShapeDtypeStruct((TAIL, state_size), F32),
             jax.ShapeDtypeStruct((state_size, block), BF16),
-            jax.ShapeDtypeStruct((HALO, channels + 2 * state_size), BF16),
+            jax.ShapeDtypeStruct((TAIL, ENDS), BF16),
         ],
         in_specs=[vmem] * 12,
         out_specs=[vmem] * 8,

time: 35.7 us -> 35.5 us (level)
  transfers between devices with their start and end apart: 12 -> 12, of which waited for: 7 -> 7; matrix products, arithmetic and copies ran while one was open for 0% -> 0% of each run, Pallas kernels for 12% -> 13%
where the time goes in v7:
time: 35.5 us; the launch traced here: 35.3 us
  waiting for transfers between devices  16.2 us (46%)
  starting transfers between devices  12.3 us (35%)
  Pallas kernels  6.74 us (19%)
    ppermute x6, starting transfers between devices, exchange(): lax.ppermute(array, 'seq', [(i, i ^ mask) for i in range(lax.axis_size('s...  7.11 us
    ppermute x6, waiting for transfers between devices, exchange(): lax.ppermute(array, 'seq', [(i, i ^ mask) for i in range(lax.axis_size('s...  6.04 us
    ppermute x1, waiting for transfers between devices, turned_on(): lax.ppermute(array, 'seq', [(i, (i + distance) % count) for i in range(co...  5.12 us
    ppermute x2, waiting for transfers between devices, shifted(): lax.ppermute(array, 'seq', [(i, i + distance) for i in range(count - dist...  5 us
    ppermute x2, starting transfers between devices, shifted(): lax.ppermute(array, 'seq', [(i, i + distance) for i in range(count - dist...  4.66 us
    pallas_call x1, Pallas kernels, on_device(): pl.pallas_call(channels_kernel, out_shape=[others, others, jax.ShapeDtype...  1.96 us
    pallas_call x1, Pallas kernels, on_device(): pl.pallas_call(intra_kernel, out_shape=[jax.ShapeDtypeStruct((block, chan...  1.5 us
    pallas_call x1, Pallas kernels, on_device(): pl.pallas_call(back_kernel, out_shape=out_shape, in_specs=[vmem] * (GROUP...  1.06 us
  transfers between devices with their start and end apart: 12, of which 7 were waited for; matrix products, arithmetic and copies ran while one was open for 0% of the time, Pallas kernels for 13%

profile of v7, /device:TPU:24, one launch (start us, length us, event | category | flops | bytes accessed | tf_op | source)
XLA Modules:
  0.0 35.3 jit_solution(17720973384193905493)
XLA Ops:
  0.0 0.0 collective-permute-start
  0.0 0.5 %collective-permute-start.1 = (f32[4,256]{1,0:T(4,128)}, f32[4,256]{1,0:T(4,128)S(1)}, u32[]{:S(2)}, u32[]{:S(2)}) collective-permute-start(f32[4,256]{1,0:T(4,128)} %own_taps_hbm.1), channel_id=1, source_target_pairs={{0,1},{1,0},{2,3},{3,2},{4,5},{5,4},{6,7},{7,6},{8,9},{9,8},{10,11... | collective-permute-start | bytes 12296 | tf_op jit(solution)/shard_map/ppermute | solution.py:530
  0.5 0.0 collective-permute-start.2
  0.5 2.0 %channels.1 = (bf16[256,768]{1,0:T(8,128)(2,1)S(1)}, bf16[256,768]{1,0:T(8,128)(2,1)S(1)}, f32[24,768]{1,0:T(8,128)S(1)}, f32[16,128]{1,0:T(8,128)S(1)}, f32[16,...) custom-call(bf16[256,1024]{1,0:T(8,128)(2,1)} %x_hbm.1, ...), custom_call_target="tpu_custom_call" | custom-call | tf_op jit(solution)/shard_map/channels/pallas_call | solution.py:538
  2.5 0.0 collective-permute-done.2
  2.5 0.0 collective-permute-done.1.other_taps
  2.5 0.0 collective-permute-done.other
  2.5 0.6 %states.1 = (bf16[272,256]{1,0:T(8,128)(2,1)S(1)}, bf16[272,256]{1,0:T(8,128)(2,1)S(1)}, bf16[272,256]{1,0:T(8,128)(2,1)S(1)}, bf16[256,256]{1,0:T(8,128)(2,1)S(...) custom-call(bf16[256,1024]{1,0:T(8,128)(2,1)S(1)} %get-tuple-element, ...), custom_call_target="tpu_custom_call" | custom-call | tf_op jit(solution)/shard_map/states/pallas_call | solution.py:578
  3.2 2.5 %collective-permute-start.3 = (bf16[272,256]{1,0:T(8,128)(2,1)S(1)}, bf16[272,256]{1,0:T(8,128)(2,1)S(1)}, u32[]{:S(2)}, u32[]{:S(2)}) collective-permute-start(bf16[272,256]{1,0:T(8,128)(2,1)S(1)} %get-tuple-element.59), channel_id=1, source_target_pairs={{0,6},{2,4},{4,2},{6,0},{8,14},{10,12},{12,10},{14,8},{16,22},{18,... | collective-permute-start | bytes 417800 | tf_op jit(solution)/shard_map/ppermute | solution.py:487
  5.7 0.5 %collective-permute-start.4 = (bf16[272,256]{1,0:T(8,128)(2,1)S(1)}, bf16[272,256]{1,0:T(8,128)(2,1)S(1)}, u32[]{:S(2)}, u32[]{:S(2)}) collective-permute-start(bf16[272,256]{1,0:T(8,128)(2,1)S(1)} %get-tuple-element.60), channel_id=1, source_target_pairs={{0,2},{2,0},{4,6},{6,4},{8,10},{10,8},{12,14},{14,12},{16,18},{18,... | collective-permute-start | bytes 417800 | tf_op jit(solution)/shard_map/ppermute | solution.py:487
  6.2 0.5 %collective-permute-start.5 = (bf16[272,256]{1,0:T(8,128)(2,1)S(1)}, bf16[272,256]{1,0:T(8,128)(2,1)S(1)}, u32[]{:S(2)}, u32[]{:S(2)}) collective-permute-start(bf16[272,256]{1,0:T(8,128)(2,1)S(1)} %get-tuple-element.61), channel_id=1, source_target_pairs={{0,4},{2,6},{4,0},{6,2},{8,12},{10,14},{12,8},{14,10},{16,20},{18,... | collective-permute-start | bytes 417800 | tf_op jit(solution)/shard_map/ppermute | solution.py:487
  6.7 3.4 %collective-permute-start.6 = (bf16[16,512]{1,0:T(8,128)(2,1)S(1)}, bf16[16,512]{1,0:T(8,128)(2,1)S(1)}, u32[]{:S(2)}, u32[]{:S(2)}) collective-permute-start(bf16[16,512]{1,0:T(8,128)(2,1)S(1)} %get-tuple-element.64), channel_id=1, source_target_pairs={{0,2},{2,4},{4,6},{6,8},{8,10},{10,12},{12,14},{14,16},{16,18},{18... | collective-permute-start | bytes 49160 | tf_op jit(solution)/shard_map/ppermute | solution.py:497
  10.1 0.6 %rest.1 = (bf16[272,256]{1,0:T(8,128)(2,1)S(1)}, bf16[256,256]{1,0:T(8,128)(2,1)S(1)}, f32[24,256]{1,0:T(8,128)S(1)}) custom-call(bf16[256,1024]{1,0:T(8,128)(2,1)S(1)} %get-tuple-element.42.x, f32[4,1024]{1,0:T(4,128)S(1)} %get-tuple-element.43.taps.refs_5_.x_taps, f32[1,1024]{1,0:T(1,128)S(1)} %get-tuple-element.44.bias.refs_6_.x_bias, ...), custom_call_target="tpu_custom_call" | custom-call | flops 400000000 | bytes 2000000 | tf_op jit(solution)/shard_map/rest/pallas_call | solution.py:597
  10.7 0.0 collective-permute-done.3.refs_0_.r3
  10.7 2.8 %collective-permute-done.4.refs_1_.r1 = bf16[272,256]{1,0:T(8,128)(2,1)S(1)} collective-permute-done((bf16[272,256]{1,0:T(8,128)(2,1)S(1)}, bf16[272,256]{1,0:T(8,128)(2,1)S(1)}, u32[]{:S(2)}, u32[]{:S(2)}) %collective-permute-start.4) | collective-permute-done | bytes 139296 | tf_op jit(solution)/shard_map/ppermute | solution.py:487
  13.5 0.0 collective-permute-done.5.refs_2_.r2
  13.5 0.4 %group.1 = bf16[272,256]{1,0:T(8,128)(2,1)S(1)} custom-call(bf16[272,256]{1,0:T(8,128)(2,1)S(1)} %collective-permute-done.3.refs_0_.r3, bf16[272,256]{1,0:T(8,128)(2,1)S(1)} %collective-permute-done.4.refs_1_.r1, bf16[272,256]{1,0:T(8,128)(2,1)S(1)} %collective-permute-done.5.refs_2_.r2, bf16[272,256]{1,0:T(8,128)(2,1)S(1)} %get-tuple-element.62.refs_3_.r0, ...), custom_call_target="tpu_custom_call" | custom-call | tf_op jit(solution)/shard_map/group/pallas_call | solution.py:621
  13.9 0.2 collective-permute-done.6.halo
  14.1 0.0 collective-permute-start.8
  14.2 1.3 %collective-permute-start.7 = (bf16[272,256]{1,0:T(8,128)(2,1)S(1)}, bf16[272,256]{1,0:T(8,128)(2,1)S(1)}, u32[]{:S(2)}, u32[]{:S(2)}) collective-permute-start(bf16[272,256]{1,0:T(8,128)(2,1)S(1)} %group.1), channel_id=1, source_target_pairs={{0,16},{2,18},{4,20},{6,22},{8,24},{10,26},{12,28},{14,30},{1,17},... | collective-permute-start | bytes 417800 | tf_op jit(solution)/shard_map/ppermute | solution.py:497
  15.5 5.1 %collective-permute-done.8.near = bf16[272,256]{1,0:T(8,128)(2,1)S(1)} collective-permute-done((bf16[272,256]{1,0:T(8,128)(2,1)S(1)}, bf16[272,256]{1,0:T(8,128)(2,1)S(1)}, u32[]{:S(2)}, u32[]{:S(2)}) %collective-permute-start.8) | collective-permute-done | bytes 139296 | tf_op jit(solution)/shard_map/ppermute | solution.py:492
  20.6 4.8 %collective-permute-done.7.far = bf16[272,256]{1,0:T(8,128)(2,1)S(1)} collective-permute-done((bf16[272,256]{1,0:T(8,128)(2,1)S(1)}, bf16[272,256]{1,0:T(8,128)(2,1)S(1)}, u32[]{:S(2)}, u32[]{:S(2)}) %collective-permute-start.7) | collective-permute-done | bytes 139296 | tf_op jit(solution)/shard_map/ppermute | solution.py:497
  25.3 0.6 %entering.1 = (bf16[256,256]{1,0:T(8,128)(2,1)S(1)}, bf16[256,256]{1,0:T(8,128)(2,1)S(1)}, bf16[256,256]{1,0:T(8,128)(2,1)S(1)}, bf16[256,256]{1,0:T(8,128)(2,1)S(1)}) custom-call(bf16[272,256]{1,0:T(8,128)(2,1)S(1)} %collective-permute-done.3.refs_0_.r3, bf16[272,256]{1,0:T(8,128)(2,1)S(1)} %collective-permute-done.4.refs_1_.r1, ...), custom_call_target="tpu_custom_call" | custom-call | tf_op jit(solution)/shard_map/entering/pallas_call | solution.py:636
  26.0 2.3 %collective-permute-start.9 = (bf16[256,256]{1,0:T(8,128)(2,1)S(1)}, bf16[256,256]{1,0:T(8,128)(2,1)S(1)}, u32[]{:S(2)}, u32[]{:S(2)}) collective-permute-start(bf16[256,256]{1,0:T(8,128)(2,1)S(1)} %get-tuple-element.71), channel_id=1, source_target_pairs={{0,6},{2,4},{4,2},{6,0},{8,14},{10,12},{12,10},{14,8},{16,22},{18,... | collective-permute-start | bytes 393224 | tf_op jit(solution)/shard_map/ppermute | solution.py:487
  28.3 0.7 %collective-permute-start.10 = (bf16[256,256]{1,0:T(8,128)(2,1)S(1)}, bf16[256,256]{1,0:T(8,128)(2,1)S(1)}, u32[]{:S(2)}, u32[]{:S(2)}) collective-permute-start(bf16[256,256]{1,0:T(8,128)(2,1)S(1)} %get-tuple-element.72), channel_id=1, source_target_pairs={{0,2},{2,0},{4,6},{6,4},{8,10},{10,8},{12,14},{14,12},{16,18},{18,... | collective-permute-start | bytes 393224 | tf_op jit(solution)/shard_map/ppermute | solution.py:487
  29.0 0.5 %collective-permute-start.11 = (bf16[256,256]{1,0:T(8,128)(2,1)S(1)}, bf16[256,256]{1,0:T(8,128)(2,1)S(1)}, u32[]{:S(2)}, u32[]{:S(2)}) collective-permute-start(bf16[256,256]{1,0:T(8,128)(2,1)S(1)} %get-tuple-element.73), channel_id=1, source_target_pairs={{0,4},{2,6},{4,0},{6,2},{8,12},{10,14},{12,8},{14,10},{16,20},{18,... | collective-permute-start | bytes 393224 | tf_op jit(solution)/shard_map/ppermute | solution.py:487
  29.5 1.5 %intra.1 = (f32[256,1024]{1,0:T(8,128)S(1)}, bf16[256,256]{1,0:T(8,128)(2,1)S(1)}, f32[256,1024]{1,0:T(8,128)S(1)}) custom-call(bf16[256,768]{1,0:T(8,128)(2,1)S(1)} %get-tuple-element.41.x_early, bf16[256,256]{1,0:T(8,128)(2,1)S(1)} %get-tuple-element.57.x_late, f32[24,768]{1,0:T(8,128)S(1)} %get-tuple-element.54.aux.aux_early, ...), custom_call_target="tpu_custom_call" | custom-call | flops 600000000 | bytes 4000000 | tf_op jit(solution)/shard_map/intra/pallas_call | solution.py:646
  31.0 1.8 %collective-permute-done.9.f3 = bf16[256,256]{1,0:T(8,128)(2,1)S(1)} collective-permute-done((bf16[256,256]{1,0:T(8,128)(2,1)S(1)}, bf16[256,256]{1,0:T(8,128)(2,1)S(1)}, u32[]{:S(2)}, u32[]{:S(2)}) %collective-permute-start.9) | collective-permute-done | bytes 131104 | tf_op jit(solution)/shard_map/ppermute | solution.py:487
  32.8 1.4 %collective-permute-done.10.f1 = bf16[256,256]{1,0:T(8,128)(2,1)S(1)} collective-permute-done((bf16[256,256]{1,0:T(8,128)(2,1)S(1)}, bf16[256,256]{1,0:T(8,128)(2,1)S(1)}, u32[]{:S(2)}, u32[]{:S(2)}) %collective-permute-start.10) | collective-permute-done | bytes 131104 | tf_op jit(solution)/shard_map/ppermute | solution.py:487
  34.2 0.1 collective-permute-done.11.f2
  34.3 1.1 %back.1 = bf16[256,1024]{1,0:T(8,128)(2,1)} custom-call(bf16[256,256]{1,0:T(8,128)(2,1)S(1)} %get-tuple-element.69.c, bf16[256,256]{1,0:T(8,128)(2,1)S(1)} %collective-permute-done.9.f3, bf16[256,256]{1,0:T(8,128)(2,1)S(1)} %collective-permute-done.10.f1, bf16[256,256]{1,0:T(8,128)(2,1)S(1)} %collective-permute-done.11.f2, ...), custom_call_target="tpu_custom_call" | custom-call | tf_op jit(solution)/shard_map/back/pallas_call | solution.py:671
  (1 shorter events, 0.0 us)
Async XLA Ops:
  0.0 2.5 %collective-permute-start = (bf16[256,256]{1,0:T(8,128)(2,1)}, bf16[256,256]{1,0:T(8,128)(2,1)S(1)}, u32[]{:S(2)}, u32[]{:S(2)}) collective-permute-start(bf16[256,256]{1,0:T(8,128)(2,1)} %own_hbm.1), channel_id=1, source_target_pairs={{0,1},{1,0},{2,3},{3,2},{4,5},{5,4},{6,7},{7,6},{8,9},{9,8},{10,11... | collective-permute-start | bytes 393224 | tf_op jit(solution)/shard_map/ppermute | solution.py:530
  0.0 2.5 %collective-permute-start.1 = (f32[4,256]{1,0:T(4,128)}, f32[4,256]{1,0:T(4,128)S(1)}, u32[]{:S(2)}, u32[]{:S(2)}) collective-permute-start(f32[4,256]{1,0:T(4,128)} %own_taps_hbm.1), channel_id=1, source_target_pairs={{0,1},{1,0},{2,3},{3,2},{4,5},{5,4},{6,7},{7,6},{8,9},{9,8},{10,11... | collective-permute-start | bytes 12296 | tf_op jit(solution)/shard_map/ppermute | solution.py:530
  0.5 2.0 %collective-permute-start.2 = (f32[256]{0:T(256)}, f32[256]{0:T(256)S(1)}, u32[]{:S(2)}, u32[]{:S(2)}) collective-permute-start(f32[256]{0:T(256)} %param.16), channel_id=1, source_target_pairs={{0,1},{1,0},{2,3},{3,2},{4,5},{5,4},{6,7},{7,6},{8,9},{9,8},{10,11... | collective-permute-start | bytes 3080 | tf_op jit(solution)/shard_map/ppermute | solution.py:530
  3.2 7.5 %collective-permute-start.3 = (bf16[272,256]{1,0:T(8,128)(2,1)S(1)}, bf16[272,256]{1,0:T(8,128)(2,1)S(1)}, u32[]{:S(2)}, u32[]{:S(2)}) collective-permute-start(bf16[272,256]{1,0:T(8,128)(2,1)S(1)} %get-tuple-element.59), channel_id=1, source_target_pairs={{0,6},{2,4},{4,2},{6,0},{8,14},{10,12},{12,10},{14,8},{16,22},{18,... | collective-permute-start | bytes 417800 | tf_op jit(solution)/shard_map/ppermute | solution.py:487
  5.7 7.8 %collective-permute-start.4 = (bf16[272,256]{1,0:T(8,128)(2,1)S(1)}, bf16[272,256]{1,0:T(8,128)(2,1)S(1)}, u32[]{:S(2)}, u32[]{:S(2)}) collective-permute-start(bf16[272,256]{1,0:T(8,128)(2,1)S(1)} %get-tuple-element.60), channel_id=1, source_target_pairs={{0,2},{2,0},{4,6},{6,4},{8,10},{10,8},{12,14},{14,12},{16,18},{18,... | collective-permute-start | bytes 417800 | tf_op jit(solution)/shard_map/ppermute | solution.py:487
  6.2 7.3 %collective-permute-start.5 = (bf16[272,256]{1,0:T(8,128)(2,1)S(1)}, bf16[272,256]{1,0:T(8,128)(2,1)S(1)}, u32[]{:S(2)}, u32[]{:S(2)}) collective-permute-start(bf16[272,256]{1,0:T(8,128)(2,1)S(1)} %get-tuple-element.61), channel_id=1, source_target_pairs={{0,4},{2,6},{4,0},{6,2},{8,12},{10,14},{12,8},{14,10},{16,20},{18,... | collective-permute-start | bytes 417800 | tf_op jit(solution)/shard_map/ppermute | solution.py:487
  6.7 7.4 %collective-permute-start.6 = (bf16[16,512]{1,0:T(8,128)(2,1)S(1)}, bf16[16,512]{1,0:T(8,128)(2,1)S(1)}, u32[]{:S(2)}, u32[]{:S(2)}) collective-permute-start(bf16[16,512]{1,0:T(8,128)(2,1)S(1)} %get-tuple-element.64), channel_id=1, source_target_pairs={{0,2},{2,4},{4,6},{6,8},{8,10},{10,12},{12,14},{14,16},{16,18},{18... | collective-permute-start | bytes 49160 | tf_op jit(solution)/shard_map/ppermute | solution.py:497
  14.1 6.5 %collective-permute-start.8 = (bf16[272,256]{1,0:T(8,128)(2,1)S(1)}, bf16[272,256]{1,0:T(8,128)(2,1)S(1)}, u32[]{:S(2)}, u32[]{:S(2)}) collective-permute-start(bf16[272,256]{1,0:T(8,128)(2,1)S(1)} %group.1), channel_id=1, source_target_pairs={{0,8},{2,10},{4,12},{6,14},{8,16},{10,18},{12,20},{14,22},{16,24},... | collective-permute-start | bytes 417800 | tf_op jit(solution)/shard_map/ppermute | solution.py:492
  14.2 11.2 %collective-permute-start.7 = (bf16[272,256]{1,0:T(8,128)(2,1)S(1)}, bf16[272,256]{1,0:T(8,128)(2,1)S(1)}, u32[]{:S(2)}, u32[]{:S(2)}) collective-permute-start(bf16[272,256]{1,0:T(8,128)(2,1)S(1)} %group.1), channel_id=1, source_target_pairs={{0,16},{2,18},{4,20},{6,22},{8,24},{10,26},{12,28},{14,30},{1,17},... | collective-permute-start | bytes 417800 | tf_op jit(solution)/shard_map/ppermute | solution.py:497
  26.0 6.8 %collective-permute-start.9 = (bf16[256,256]{1,0:T(8,128)(2,1)S(1)}, bf16[256,256]{1,0:T(8,128)(2,1)S(1)}, u32[]{:S(2)}, u32[]{:S(2)}) collective-permute-start(bf16[256,256]{1,0:T(8,128)(2,1)S(1)} %get-tuple-element.71), channel_id=1, source_target_pairs={{0,6},{2,4},{4,2},{6,0},{8,14},{10,12},{12,10},{14,8},{16,22},{18,... | collective-permute-start | bytes 393224 | tf_op jit(solution)/shard_map/ppermute | solution.py:487
  28.3 5.9 %collective-permute-start.10 = (bf16[256,256]{1,0:T(8,128)(2,1)S(1)}, bf16[256,256]{1,0:T(8,128)(2,1)S(1)}, u32[]{:S(2)}, u32[]{:S(2)}) collective-permute-start(bf16[256,256]{1,0:T(8,128)(2,1)S(1)} %get-tuple-element.72), channel_id=1, source_target_pairs={{0,2},{2,0},{4,6},{6,4},{8,10},{10,8},{12,14},{14,12},{16,18},{18,... | collective-permute-start | bytes 393224 | tf_op jit(solution)/shard_map/ppermute | solution.py:487
  29.0 5.3 %collective-permute-start.11 = (bf16[256,256]{1,0:T(8,128)(2,1)S(1)}, bf16[256,256]{1,0:T(8,128)(2,1)S(1)}, u32[]{:S(2)}, u32[]{:S(2)}) collective-permute-start(bf16[256,256]{1,0:T(8,128)(2,1)S(1)} %get-tuple-element.73), channel_id=1, source_target_pairs={{0,4},{2,6},{4,0},{6,2},{8,12},{10,14},{12,8},{14,10},{16,20},{18,... | collective-permute-start | bytes 393224 | tf_op jit(solution)/shard_map/ppermute | solution.py:487

commit v8 on v7

--- a/solution.py
+++ b/solution.py
@@ -337,53 +337,66 @@
         pl.when(member_here() == member)(lambda member=member: run(member))
 
 
-def entering_kernel(
-    r3, r1, r2, r0, far, near, x_taps, x_bias, b_taps, e0, e1, e2, e3
-):
-    group = group_here()
-    one = jnp.ones((1, r0.shape[1]), F32)
-    from_near = jnp.where(group >= 1, one, 0.0)
-    from_far = jnp.where(group >= 2, one, 0.0)
+def before_kernel(r3, r1, r2, r0, near, x_taps, x_bias, b_taps, partial, factors):
     rows = r0.shape[0] - TAIL
     width = r0.shape[1]
     count = x_taps.shape[0]
-    held, outs = (r0, r1, r2, r3), (e0, e1, e2, e3)
+    held = (r0, r1, r2, r3)
+    one = jnp.ones((1, width), F32)
+    from_near = jnp.where(group_here() >= 1, one, 0.0)
 
     def run(member):
         cols = slice(member * width, (member + 1) * width)
         taps, bias = tail_taps(x_taps[:, cols], x_bias[:, cols], b_taps[...], count)
         states = [held[member ^ k] for k in range(GROUP)]
-        targets = [outs[member ^ k] for k in range(GROUP)]
         tails = [tail_of(state) for state in states]
         near_tail = from_near * tail_of(near)
-        far_tail = from_far * tail_of(far)
         decays = [decay_of(tail) for tail in tails]
-        near_decay = decay_of(near_tail)
-        far_factor = near_decay * from_far
-        far_b, far_x = early_tokens(far_tail, jnp.zeros_like(far_tail), taps, bias)
-        near_b, near_x = early_tokens(near_tail, far_tail, taps, bias)
-        early_b, early_x = [far_b, near_b], [far_x * near_decay, near_x]
+        added = []
+        factor = one
+        for k in range(GROUP):
+            factors[member ^ k : (member ^ k) + 1, :] = factor
+            factor = factor * decays[k]
+        factors[GROUP : GROUP + 1, :] = decay_of(near_tail)
         for k in range(GROUP - 1):
             b, x = early_tokens(tails[k], tails[k - 1] if k else near_tail, taps, bias)
-            early_b.append(b)
-            early_x.append(x)
-        b_rows = jnp.concatenate(early_b, axis=0).astype(BF16)
-        x_rows = jnp.concatenate(early_x, axis=0).astype(BF16)
-        added = [dot(b_rows[: 2 * TAIL], x_rows[: 2 * TAIL], ((0,), (0,)))]
-        for k in range(GROUP - 1):
-            part = slice((k + 2) * TAIL, (k + 3) * TAIL)
-            added.append(dot(b_rows[part], x_rows[part], ((0,), (0,))))
-        step = 16
+            added.append(dot(b.astype(BF16), x.astype(BF16), ((0,), (0,))))
+        step = 32
         for top in range(0, rows, step):
             part = slice(top, top + step)
-            value = from_near * near[part, :].astype(F32) + far_factor * far[part, :].astype(F32) + added[0][part]
-            targets[0][part, :] = value.astype(BF16)
+            value = from_near * near[part, :].astype(F32)
+            partial[member, part, :] = value
             for k in range(GROUP - 1):
-                value = decays[k] * value + states[k][part, :].astype(F32) + added[k + 1][part]
-                targets[k + 1][part, :] = value.astype(BF16)
+                value = decays[k] * value + states[k][part, :].astype(F32) + added[k][part]
+                partial[member ^ (k + 1), part, :] = value
 
     for member in range(GROUP):
         pl.when(member_here() == member)(lambda member=member: run(member))
+
+
+def entering_kernel(far, near, partial, factors, x_taps, x_bias, b_taps, e0, e1, e2, e3):
+    group = group_here()
+    outs = (e0, e1, e2, e3)
+    rows, width = e0.shape
+    one = jnp.ones((1, width), F32)
+    from_far = jnp.where(group >= 2, one, 0.0)
+    near_tail = jnp.where(group >= 1, one, 0.0) * tail_of(near)
+    far_tail = from_far * tail_of(far)
+    cols = quarter(0, width)
+    taps, bias = tail_taps(x_taps[:, cols], x_bias[:, cols], b_taps[...], x_taps.shape[0])
+    near_decay = factors[GROUP : GROUP + 1, :]
+    far_factor = near_decay * from_far
+    far_b, far_x = early_tokens(far_tail, jnp.zeros_like(far_tail), taps, bias)
+    near_b, near_x = early_tokens(near_tail, far_tail, taps, bias)
+    b_rows = jnp.concatenate([far_b, near_b], axis=0).astype(BF16)
+    x_rows = jnp.concatenate([far_x * near_decay, near_x], axis=0).astype(BF16)
+    added = dot(b_rows, x_rows, ((0,), (0,)))
+    step = 32
+    for top in range(0, rows, step):
+        part = slice(top, top + step)
+        value = far_factor * far[part, :].astype(F32) + added[part]
+        for k, out in enumerate(outs):
+            out[part, :] = (partial[k, part, :] + factors[k : k + 1, :] * value).astype(BF16)
 
 
 def patched(before, halo, taps, offset_col):
@@ -633,14 +646,26 @@
     else:
         near, far = scan_groups(total, groups)
 
+    partial, factors = pl.pallas_call(
+        before_kernel,
+        out_shape=[
+            jax.ShapeDtypeStruct((GROUP, state_size, width), F32),
+            jax.ShapeDtypeStruct((8, width), F32),
+        ],
+        in_specs=[vmem] * (GROUP + 4),
+        out_specs=[vmem] * 2,
+        compiler_params=PARAMS,
+        cost_estimate=pl.CostEstimate(flops=100_000_000, bytes_accessed=2_000_000, transcendentals=10_000),
+        name="before",
+    )(r3, r1, r2, s0, near, x_taps, x_bias, b_aux)
     entering = pl.pallas_call(
         entering_kernel,
         out_shape=[jax.ShapeDtypeStruct((state_size, width), BF16)] * GROUP,
-        in_specs=[vmem] * (GROUP + 5),
+        in_specs=[vmem] * 7,
         out_specs=[vmem] * GROUP,
         compiler_params=PARAMS,
         name="entering",
-    )(r3, r1, r2, s0, far, near, x_taps, x_bias, b_aux)
+    )(far, near, partial, factors, x_taps, x_bias, b_aux)
     mine = [entering[0]] + [exchange(entering[k], k) for k in (1, 2, 3)]
 
     intra, c_conv, carry = pl.pallas_call(

time: 35.5 us -> 35.4 us (level)
  waiting for transfers between devices: 16.2 us -> 15.7 us
    ppermute x2, waiting for transfers between devices: 5 us -> 4.48 us  [shifted(): lax.ppermute(array, 'seq', [(i, i + distance) for i in range(count - dist...]
    pallas_call x0 -> x1, Pallas kernels: none -> 0.48 us  [on_device(): pl.pallas_call(before_kernel, out_shape=[jax.ShapeDtypeStruct((GROUP, sta...]
  transfers between devices with their start and end apart: 12 -> 12, of which waited for: 7 -> 7; matrix products, arithmetic and copies ran while one was open for 0% -> 0% of each run, Pallas kernels for 13% -> 14%
where the time goes in v8:
time: 35.4 us; the launch traced here: 35.2 us
  waiting for transfers between devices  15.7 us (44%)
  starting transfers between devices  12.3 us (35%)
  Pallas kernels  7.05 us (20%)
    ppermute x6, starting transfers between devices, exchange(): lax.ppermute(array, 'seq', [(i, i ^ mask) for i in range(lax.axis_size('s...  7.11 us
    ppermute x6, waiting for transfers between devices, exchange(): lax.ppermute(array, 'seq', [(i, i ^ mask) for i in range(lax.axis_size('s...  6.06 us
    ppermute x1, waiting for transfers between devices, turned_on(): lax.ppermute(array, 'seq', [(i, (i + distance) % count) for i in range(co...  5.13 us
    ppermute x2, starting transfers between devices, shifted(): lax.ppermute(array, 'seq', [(i, i + distance) for i in range(count - dist...  4.66 us
    ppermute x2, waiting for transfers between devices, shifted(): lax.ppermute(array, 'seq', [(i, i + distance) for i in range(count - dist...  4.48 us
    pallas_call x1, Pallas kernels, on_device(): pl.pallas_call(channels_kernel, out_shape=[others, others, jax.ShapeDtype...  1.96 us
    pallas_call x1, Pallas kernels, on_device(): pl.pallas_call(intra_kernel, out_shape=[jax.ShapeDtypeStruct((block, chan...  1.5 us
    pallas_call x1, Pallas kernels, on_device(): pl.pallas_call(back_kernel, out_shape=out_shape, in_specs=[vmem] * (GROUP...  1.06 us
  transfers between devices with their start and end apart: 12, of which 7 were waited for; matrix products, arithmetic and copies ran while one was open for 0% of the time, Pallas kernels for 14%

profile of v8, /device:TPU:24, one launch (start us, length us, event | category | flops | bytes accessed | tf_op | source)
XLA Modules:
  0.0 35.2 jit_solution(11668233965791233270)
XLA Ops:
  0.0 0.0 collective-permute-start
  0.0 0.5 %collective-permute-start.1 = (f32[4,256]{1,0:T(4,128)}, f32[4,256]{1,0:T(4,128)S(1)}, u32[]{:S(2)}, u32[]{:S(2)}) collective-permute-start(f32[4,256]{1,0:T(4,128)} %own_taps_hbm.1), channel_id=1, source_target_pairs={{0,1},{1,0},{2,3},{3,2},{4,5},{5,4},{6,7},{7,6},{8,9},{9,8},{10,11... | collective-permute-start | bytes 12296 | tf_op jit(solution)/shard_map/ppermute | solution.py:543
  0.5 0.0 collective-permute-start.2
  0.5 2.0 %channels.1 = (bf16[256,768]{1,0:T(8,128)(2,1)S(1)}, bf16[256,768]{1,0:T(8,128)(2,1)S(1)}, f32[24,768]{1,0:T(8,128)S(1)}, f32[16,128]{1,0:T(8,128)S(1)}, f32[16,...) custom-call(bf16[256,1024]{1,0:T(8,128)(2,1)} %x_hbm.1, ...), custom_call_target="tpu_custom_call" | custom-call | tf_op jit(solution)/shard_map/channels/pallas_call | solution.py:551
  2.5 0.0 collective-permute-done.2
  2.5 0.0 collective-permute-done.1.other_taps
  2.5 0.0 collective-permute-done.other
  2.5 0.6 %states.1 = (bf16[272,256]{1,0:T(8,128)(2,1)S(1)}, bf16[272,256]{1,0:T(8,128)(2,1)S(1)}, bf16[272,256]{1,0:T(8,128)(2,1)S(1)}, bf16[256,256]{1,0:T(8,128)(2,1)S(...) custom-call(bf16[256,1024]{1,0:T(8,128)(2,1)S(1)} %get-tuple-element, ...), custom_call_target="tpu_custom_call" | custom-call | tf_op jit(solution)/shard_map/states/pallas_call | solution.py:591
  3.2 2.5 %collective-permute-start.3 = (bf16[272,256]{1,0:T(8,128)(2,1)S(1)}, bf16[272,256]{1,0:T(8,128)(2,1)S(1)}, u32[]{:S(2)}, u32[]{:S(2)}) collective-permute-start(bf16[272,256]{1,0:T(8,128)(2,1)S(1)} %get-tuple-element.61), channel_id=1, source_target_pairs={{0,6},{2,4},{4,2},{6,0},{8,14},{10,12},{12,10},{14,8},{16,22},{18,... | collective-permute-start | bytes 417800 | tf_op jit(solution)/shard_map/ppermute | solution.py:500
  5.7 0.5 %collective-permute-start.4 = (bf16[272,256]{1,0:T(8,128)(2,1)S(1)}, bf16[272,256]{1,0:T(8,128)(2,1)S(1)}, u32[]{:S(2)}, u32[]{:S(2)}) collective-permute-start(bf16[272,256]{1,0:T(8,128)(2,1)S(1)} %get-tuple-element.62), channel_id=1, source_target_pairs={{0,2},{2,0},{4,6},{6,4},{8,10},{10,8},{12,14},{14,12},{16,18},{18,... | collective-permute-start | bytes 417800 | tf_op jit(solution)/shard_map/ppermute | solution.py:500
  6.2 0.5 %collective-permute-start.5 = (bf16[272,256]{1,0:T(8,128)(2,1)S(1)}, bf16[272,256]{1,0:T(8,128)(2,1)S(1)}, u32[]{:S(2)}, u32[]{:S(2)}) collective-permute-start(bf16[272,256]{1,0:T(8,128)(2,1)S(1)} %get-tuple-element.63), channel_id=1, source_target_pairs={{0,4},{2,6},{4,0},{6,2},{8,12},{10,14},{12,8},{14,10},{16,20},{18,... | collective-permute-start | bytes 417800 | tf_op jit(solution)/shard_map/ppermute | solution.py:500
  6.7 3.4 %collective-permute-start.6 = (bf16[16,512]{1,0:T(8,128)(2,1)S(1)}, bf16[16,512]{1,0:T(8,128)(2,1)S(1)}, u32[]{:S(2)}, u32[]{:S(2)}) collective-permute-start(bf16[16,512]{1,0:T(8,128)(2,1)S(1)} %get-tuple-element.66), channel_id=1, source_target_pairs={{0,2},{2,4},{4,6},{6,8},{8,10},{10,12},{12,14},{14,16},{16,18},{18... | collective-permute-start | bytes 49160 | tf_op jit(solution)/shard_map/ppermute | solution.py:510
  10.1 0.6 %rest.1 = (bf16[272,256]{1,0:T(8,128)(2,1)S(1)}, bf16[256,256]{1,0:T(8,128)(2,1)S(1)}, f32[24,256]{1,0:T(8,128)S(1)}) custom-call(bf16[256,1024]{1,0:T(8,128)(2,1)S(1)} %get-tuple-element.44.x, f32[4,1024]{1,0:T(4,128)S(1)} %get-tuple-element.45.taps.refs_5_.x_taps, f32[1,1024]{1,0:T(1,128)S(1)} %get-tuple-element.46.bias.refs_6_.x_bias, ...), custom_call_target="tpu_custom_call" | custom-call | flops 400000000 | bytes 2000000 | tf_op jit(solution)/shard_map/rest/pallas_call | solution.py:610
  10.7 0.0 collective-permute-done.3.refs_0_.r3
  10.7 2.8 %collective-permute-done.4.refs_1_.r1 = bf16[272,256]{1,0:T(8,128)(2,1)S(1)} collective-permute-done((bf16[272,256]{1,0:T(8,128)(2,1)S(1)}, bf16[272,256]{1,0:T(8,128)(2,1)S(1)}, u32[]{:S(2)}, u32[]{:S(2)}) %collective-permute-start.4) | collective-permute-done | bytes 139296 | tf_op jit(solution)/shard_map/ppermute | solution.py:500
  13.5 0.0 collective-permute-done.5.refs_2_.r2
  13.5 0.4 %group.1 = bf16[272,256]{1,0:T(8,128)(2,1)S(1)} custom-call(bf16[272,256]{1,0:T(8,128)(2,1)S(1)} %collective-permute-done.3.refs_0_.r3, bf16[272,256]{1,0:T(8,128)(2,1)S(1)} %collective-permute-done.4.refs_1_.r1, bf16[272,256]{1,0:T(8,128)(2,1)S(1)} %collective-permute-done.5.refs_2_.r2, bf16[272,256]{1,0:T(8,128)(2,1)S(1)} %get-tuple-element.64.refs_3_.r0, ...), custom_call_target="tpu_custom_call" | custom-call | tf_op jit(solution)/shard_map/group/pallas_call | solution.py:634
  13.9 0.2 collective-permute-done.6.halo
  14.1 0.1 collective-permute-start.8
  14.2 1.3 %collective-permute-start.7 = (bf16[272,256]{1,0:T(8,128)(2,1)S(1)}, bf16[272,256]{1,0:T(8,128)(2,1)S(1)}, u32[]{:S(2)}, u32[]{:S(2)}) collective-permute-start(bf16[272,256]{1,0:T(8,128)(2,1)S(1)} %group.1), channel_id=1, source_target_pairs={{0,16},{2,18},{4,20},{6,22},{8,24},{10,26},{12,28},{14,30},{1,17},... | collective-permute-start | bytes 417800 | tf_op jit(solution)/shard_map/ppermute | solution.py:510
  15.5 5.1 %collective-permute-done.8.near = bf16[272,256]{1,0:T(8,128)(2,1)S(1)} collective-permute-done((bf16[272,256]{1,0:T(8,128)(2,1)S(1)}, bf16[272,256]{1,0:T(8,128)(2,1)S(1)}, u32[]{:S(2)}, u32[]{:S(2)}) %collective-permute-start.8) | collective-permute-done | bytes 139296 | tf_op jit(solution)/shard_map/ppermute | solution.py:505
  20.6 0.5 %before.1 = (f32[4,256,256]{2,1,0:T(8,128)S(1)}, f32[8,256]{1,0:T(8,128)S(1)}) custom-call(bf16[272,256]{1,0:T(8,128)(2,1)S(1)} %collective-permute-done.3.refs_0_.r3, bf16[272,256]{1,0:T(8,128)(2,1)S(1)} %collective-permute-done.4.refs_1_.r1, bf16[272,256]{1,0:T(8,128)(2,1)S(1)} %collective-permute-done.5.refs_2_.r2, ...), custom_call_target="tpu_custom_call" | custom-call | flops 100000000 | bytes 2000000 | tf_op jit(solution)/shard_map/before/pallas_call | solution.py:649
  21.1 4.3 %collective-permute-done.7.far = bf16[272,256]{1,0:T(8,128)(2,1)S(1)} collective-permute-done((bf16[272,256]{1,0:T(8,128)(2,1)S(1)}, bf16[272,256]{1,0:T(8,128)(2,1)S(1)}, u32[]{:S(2)}, u32[]{:S(2)}) %collective-permute-start.7) | collective-permute-done | bytes 139296 | tf_op jit(solution)/shard_map/ppermute | solution.py:510
  25.3 0.4 %entering.1 = (bf16[256,256]{1,0:T(8,128)(2,1)S(1)}, bf16[256,256]{1,0:T(8,128)(2,1)S(1)}, bf16[256,256]{1,0:T(8,128)(2,1)S(1)}, bf16[256,256]{1,0:T(8,128)(2,1)S(1)}) custom-call(bf16[272,256]{1,0:T(8,128)(2,1)S(1)} %collective-permute-done.7.far, bf16[272,256]{1,0:T(8,128)(2,1)S(1)} %collective-permute-done.8.near, ...), custom_call_target="tpu_custom_call" | custom-call | tf_op jit(solution)/shard_map/entering/pallas_call | solution.py:661
  25.8 2.3 %collective-permute-start.9 = (bf16[256,256]{1,0:T(8,128)(2,1)S(1)}, bf16[256,256]{1,0:T(8,128)(2,1)S(1)}, u32[]{:S(2)}, u32[]{:S(2)}) collective-permute-start(bf16[256,256]{1,0:T(8,128)(2,1)S(1)} %get-tuple-element.75), channel_id=1, source_target_pairs={{0,6},{2,4},{4,2},{6,0},{8,14},{10,12},{12,10},{14,8},{16,22},{18,... | collective-permute-start | bytes 393224 | tf_op jit(solution)/shard_map/ppermute | solution.py:500
  28.1 0.7 %collective-permute-start.10 = (bf16[256,256]{1,0:T(8,128)(2,1)S(1)}, bf16[256,256]{1,0:T(8,128)(2,1)S(1)}, u32[]{:S(2)}, u32[]{:S(2)}) collective-permute-start(bf16[256,256]{1,0:T(8,128)(2,1)S(1)} %get-tuple-element.76), channel_id=1, source_target_pairs={{0,2},{2,0},{4,6},{6,4},{8,10},{10,8},{12,14},{14,12},{16,18},{18,... | collective-permute-start | bytes 393224 | tf_op jit(solution)/shard_map/ppermute | solution.py:500
  28.8 0.5 %collective-permute-start.11 = (bf16[256,256]{1,0:T(8,128)(2,1)S(1)}, bf16[256,256]{1,0:T(8,128)(2,1)S(1)}, u32[]{:S(2)}, u32[]{:S(2)}) collective-permute-start(bf16[256,256]{1,0:T(8,128)(2,1)S(1)} %get-tuple-element.77), channel_id=1, source_target_pairs={{0,4},{2,6},{4,0},{6,2},{8,12},{10,14},{12,8},{14,10},{16,20},{18,... | collective-permute-start | bytes 393224 | tf_op jit(solution)/shard_map/ppermute | solution.py:500
  29.3 1.5 %intra.1 = (f32[256,1024]{1,0:T(8,128)S(1)}, bf16[256,256]{1,0:T(8,128)(2,1)S(1)}, f32[256,1024]{1,0:T(8,128)S(1)}) custom-call(bf16[256,768]{1,0:T(8,128)(2,1)S(1)} %get-tuple-element.43.x_early, bf16[256,256]{1,0:T(8,128)(2,1)S(1)} %get-tuple-element.59.x_late, f32[24,768]{1,0:T(8,128)S(1)} %get-tuple-element.56.aux.aux_early, ...), custom_call_target="tpu_custom_call" | custom-call | flops 600000000 | bytes 4000000 | tf_op jit(solution)/shard_map/intra/pallas_call | solution.py:671
  30.9 1.7 %collective-permute-done.9.f3 = bf16[256,256]{1,0:T(8,128)(2,1)S(1)} collective-permute-done((bf16[256,256]{1,0:T(8,128)(2,1)S(1)}, bf16[256,256]{1,0:T(8,128)(2,1)S(1)}, u32[]{:S(2)}, u32[]{:S(2)}) %collective-permute-start.9) | collective-permute-done | bytes 131104 | tf_op jit(solution)/shard_map/ppermute | solution.py:500
  32.6 1.5 %collective-permute-done.10.f1 = bf16[256,256]{1,0:T(8,128)(2,1)S(1)} collective-permute-done((bf16[256,256]{1,0:T(8,128)(2,1)S(1)}, bf16[256,256]{1,0:T(8,128)(2,1)S(1)}, u32[]{:S(2)}, u32[]{:S(2)}) %collective-permute-start.10) | collective-permute-done | bytes 131104 | tf_op jit(solution)/shard_map/ppermute | solution.py:500
  34.1 0.1 collective-permute-done.11.f2
  34.1 1.1 %back.1 = bf16[256,1024]{1,0:T(8,128)(2,1)} custom-call(bf16[256,256]{1,0:T(8,128)(2,1)S(1)} %get-tuple-element.71.c, bf16[256,256]{1,0:T(8,128)(2,1)S(1)} %collective-permute-done.9.f3, bf16[256,256]{1,0:T(8,128)(2,1)S(1)} %collective-permute-done.10.f1, bf16[256,256]{1,0:T(8,128)(2,1)S(1)} %collective-permute-done.11.f2, ...), custom_call_target="tpu_custom_call" | custom-call | tf_op jit(solution)/shard_map/back/pallas_call | solution.py:696
  (1 shorter events, 0.0 us)
Async XLA Ops:
  0.0 2.5 %collective-permute-start = (bf16[256,256]{1,0:T(8,128)(2,1)}, bf16[256,256]{1,0:T(8,128)(2,1)S(1)}, u32[]{:S(2)}, u32[]{:S(2)}) collective-permute-start(bf16[256,256]{1,0:T(8,128)(2,1)} %own_hbm.1), channel_id=1, source_target_pairs={{0,1},{1,0},{2,3},{3,2},{4,5},{5,4},{6,7},{7,6},{8,9},{9,8},{10,11... | collective-permute-start | bytes 393224 | tf_op jit(solution)/shard_map/ppermute | solution.py:543
  0.0 2.5 %collective-permute-start.1 = (f32[4,256]{1,0:T(4,128)}, f32[4,256]{1,0:T(4,128)S(1)}, u32[]{:S(2)}, u32[]{:S(2)}) collective-permute-start(f32[4,256]{1,0:T(4,128)} %own_taps_hbm.1), channel_id=1, source_target_pairs={{0,1},{1,0},{2,3},{3,2},{4,5},{5,4},{6,7},{7,6},{8,9},{9,8},{10,11... | collective-permute-start | bytes 12296 | tf_op jit(solution)/shard_map/ppermute | solution.py:543
  0.5 2.0 %collective-permute-start.2 = (f32[256]{0:T(256)}, f32[256]{0:T(256)S(1)}, u32[]{:S(2)}, u32[]{:S(2)}) collective-permute-start(f32[256]{0:T(256)} %param.16), channel_id=1, source_target_pairs={{0,1},{1,0},{2,3},{3,2},{4,5},{5,4},{6,7},{7,6},{8,9},{9,8},{10,11... | collective-permute-start | bytes 3080 | tf_op jit(solution)/shard_map/ppermute | solution.py:543
  3.2 7.5 %collective-permute-start.3 = (bf16[272,256]{1,0:T(8,128)(2,1)S(1)}, bf16[272,256]{1,0:T(8,128)(2,1)S(1)}, u32[]{:S(2)}, u32[]{:S(2)}) collective-permute-start(bf16[272,256]{1,0:T(8,128)(2,1)S(1)} %get-tuple-element.61), channel_id=1, source_target_pairs={{0,6},{2,4},{4,2},{6,0},{8,14},{10,12},{12,10},{14,8},{16,22},{18,... | collective-permute-start | bytes 417800 | tf_op jit(solution)/shard_map/ppermute | solution.py:500
  5.7 7.8 %collective-permute-start.4 = (bf16[272,256]{1,0:T(8,128)(2,1)S(1)}, bf16[272,256]{1,0:T(8,128)(2,1)S(1)}, u32[]{:S(2)}, u32[]{:S(2)}) collective-permute-start(bf16[272,256]{1,0:T(8,128)(2,1)S(1)} %get-tuple-element.62), channel_id=1, source_target_pairs={{0,2},{2,0},{4,6},{6,4},{8,10},{10,8},{12,14},{14,12},{16,18},{18,... | collective-permute-start | bytes 417800 | tf_op jit(solution)/shard_map/ppermute | solution.py:500
  6.2 7.3 %collective-permute-start.5 = (bf16[272,256]{1,0:T(8,128)(2,1)S(1)}, bf16[272,256]{1,0:T(8,128)(2,1)S(1)}, u32[]{:S(2)}, u32[]{:S(2)}) collective-permute-start(bf16[272,256]{1,0:T(8,128)(2,1)S(1)} %get-tuple-element.63), channel_id=1, source_target_pairs={{0,4},{2,6},{4,0},{6,2},{8,12},{10,14},{12,8},{14,10},{16,20},{18,... | collective-permute-start | bytes 417800 | tf_op jit(solution)/shard_map/ppermute | solution.py:500
  6.7 7.4 %collective-permute-start.6 = (bf16[16,512]{1,0:T(8,128)(2,1)S(1)}, bf16[16,512]{1,0:T(8,128)(2,1)S(1)}, u32[]{:S(2)}, u32[]{:S(2)}) collective-permute-start(bf16[16,512]{1,0:T(8,128)(2,1)S(1)} %get-tuple-element.66), channel_id=1, source_target_pairs={{0,2},{2,4},{4,6},{6,8},{8,10},{10,12},{12,14},{14,16},{16,18},{18... | collective-permute-start | bytes 49160 | tf_op jit(solution)/shard_map/ppermute | solution.py:510
  14.1 6.5 %collective-permute-start.8 = (bf16[272,256]{1,0:T(8,128)(2,1)S(1)}, bf16[272,256]{1,0:T(8,128)(2,1)S(1)}, u32[]{:S(2)}, u32[]{:S(2)}) collective-permute-start(bf16[272,256]{1,0:T(8,128)(2,1)S(1)} %group.1), channel_id=1, source_target_pairs={{0,8},{2,10},{4,12},{6,14},{8,16},{10,18},{12,20},{14,22},{16,24},... | collective-permute-start | bytes 417800 | tf_op jit(solution)/shard_map/ppermute | solution.py:505
  14.2 11.2 %collective-permute-start.7 = (bf16[272,256]{1,0:T(8,128)(2,1)S(1)}, bf16[272,256]{1,0:T(8,128)(2,1)S(1)}, u32[]{:S(2)}, u32[]{:S(2)}) collective-permute-start(bf16[272,256]{1,0:T(8,128)(2,1)S(1)} %group.1), channel_id=1, source_target_pairs={{0,16},{2,18},{4,20},{6,22},{8,24},{10,26},{12,28},{14,30},{1,17},... | collective-permute-start | bytes 417800 | tf_op jit(solution)/shard_map/ppermute | solution.py:510
  25.8 6.8 %collective-permute-start.9 = (bf16[256,256]{1,0:T(8,128)(2,1)S(1)}, bf16[256,256]{1,0:T(8,128)(2,1)S(1)}, u32[]{:S(2)}, u32[]{:S(2)}) collective-permute-start(bf16[256,256]{1,0:T(8,128)(2,1)S(1)} %get-tuple-element.75), channel_id=1, source_target_pairs={{0,6},{2,4},{4,2},{6,0},{8,14},{10,12},{12,10},{14,8},{16,22},{18,... | collective-permute-start | bytes 393224 | tf_op jit(solution)/shard_map/ppermute | solution.py:500
  28.1 5.9 %collective-permute-start.10 = (bf16[256,256]{1,0:T(8,128)(2,1)S(1)}, bf16[256,256]{1,0:T(8,128)(2,1)S(1)}, u32[]{:S(2)}, u32[]{:S(2)}) collective-permute-start(bf16[256,256]{1,0:T(8,128)(2,1)S(1)} %get-tuple-element.76), channel_id=1, source_target_pairs={{0,2},{2,0},{4,6},{6,4},{8,10},{10,8},{12,14},{14,12},{16,18},{18,... | collective-permute-start | bytes 393224 | tf_op jit(solution)/shard_map/ppermute | solution.py:500
  28.8 5.3 %collective-permute-start.11 = (bf16[256,256]{1,0:T(8,128)(2,1)S(1)}, bf16[256,256]{1,0:T(8,128)(2,1)S(1)}, u32[]{:S(2)}, u32[]{:S(2)}) collective-permute-start(bf16[256,256]{1,0:T(8,128)(2,1)S(1)} %get-tuple-element.77), channel_id=1, source_target_pairs={{0,4},{2,6},{4,0},{6,2},{8,12},{10,14},{12,8},{14,10},{16,20},{18,... | collective-permute-start | bytes 393224 | tf_op jit(solution)/shard_map/ppermute | solution.py:500

commit v9 on v8

--- a/solution.py
+++ b/solution.py
@@ -482,15 +482,14 @@
             y[part, cols] = value
 
 
-def back_kernel(c, f3, f1, f2, f0, intra, carry, out, held, sems):
-    member = member_here()
+def back_kernel(c, *refs, members):
+    *parts, intra, carry, out, held, sems = refs
     width = out.shape[1] // GROUP
     copies = []
-    for k, state in enumerate((f0, f1, f2, f3)):
-        cols = pl.ds(pl.multiple_of((member ^ k) * width, width), width)
-        value = intra[:, cols] + carry[:, cols] * dot(c[...], state[...])
-        held[k] = value.astype(BF16)
-        copies.append(pltpu.make_async_copy(held.at[k], out.at[:, cols], sems.at[k]))
+    for slot, (k, state) in enumerate(zip(members, parts)):
+        cols = quarter(k, width)
+        held[slot] = (intra[:, cols] + carry[:, cols] * dot(c[...], state[...])).astype(BF16)
+        copies.append(pltpu.make_async_copy(held.at[slot], out.at[:, cols], sems.at[slot]))
         copies[-1].start()
     for copy in copies:
         copy.wait()
@@ -693,15 +692,30 @@
         b_main, b_aux, x_taps, time_step, rate_sum, offset, lags,
     )
     out_shape = jax.ShapeDtypeStruct((block, channels), BF16)
+    early, late = (0, 3), (1, 2)
+    begun = pl.pallas_call(
+        lambda *refs: back_kernel(*refs, members=early),
+        out_shape=out_shape,
+        in_specs=[vmem] * (len(early) + 3),
+        out_specs=hbm,
+        scratch_shapes=[pltpu.VMEM((len(early), block, width), BF16), pltpu.SemaphoreType.DMA((len(early),))],
+        compiler_params=PARAMS,
+        name="begin",
+    )(c_conv, *[mine[k] for k in early], intra, carry)
+
+    def last_kernel(c, f1, f2, intra, carry, begun, out, held, sems):
+        back_kernel(c, f1, f2, intra, carry, out, held, sems, members=late)
+
     return pl.pallas_call(
-        back_kernel,
+        last_kernel,
         out_shape=out_shape,
-        in_specs=[vmem] * (GROUP + 3),
+        in_specs=[vmem] * (len(late) + 3) + [hbm],
         out_specs=hbm,
-        scratch_shapes=[pltpu.VMEM((GROUP, block, width), BF16), pltpu.SemaphoreType.DMA((GROUP,))],
+        scratch_shapes=[pltpu.VMEM((len(late), block, width), BF16), pltpu.SemaphoreType.DMA((len(late),))],
+        input_output_aliases={len(late) + 3: 0},
         compiler_params=PARAMS,
         name="back",
-    )(c_conv, mine[3], mine[1], mine[2], mine[0], intra, carry)
+    )(c_conv, *[mine[k] for k in late], intra, carry, begun)
 
 
 def solution(mesh):

time: 35.4 us -> 35.3 us (level)
  waiting for transfers between devices: 15.7 us -> 14.7 us
  Pallas kernels: 7.05 us -> 7.88 us
    ppermute x6, waiting for transfers between devices: 6.06 us -> 5.11 us  [exchange(): lax.ppermute(array, 'seq', [(i, i ^ mask) for i in range(lax.axis_size('s...]
    pallas_call x1 -> x2, Pallas kernels: 1.06 us -> 1.89 us  [the longest x1 0.95 us: on_device(): pl.pallas_call(lambda *refs: back_kernel(*refs, members=early), out_shape...]
  transfers between devices with their start and end apart: 12 -> 12, of which waited for: 7 -> 7; matrix products, arithmetic and copies ran while one was open for 0% -> 0% of each run, Pallas kernels for 14% -> 17%
where the time goes in v9:
time: 35.3 us; the launch traced here: 35.1 us
  waiting for transfers between devices  14.7 us (42%)
  starting transfers between devices  12.3 us (35%)
  Pallas kernels  7.88 us (22%)
    ppermute x6, starting transfers between devices, exchange(): lax.ppermute(array, 'seq', [(i, i ^ mask) for i in range(lax.axis_size('s...  7.11 us
    ppermute x1, waiting for transfers between devices, turned_on(): lax.ppermute(array, 'seq', [(i, (i + distance) % count) for i in range(co...  5.13 us
    ppermute x6, waiting for transfers between devices, exchange(): lax.ppermute(array, 'seq', [(i, i ^ mask) for i in range(lax.axis_size('s...  5.11 us
    ppermute x2, starting transfers between devices, shifted(): lax.ppermute(array, 'seq', [(i, i + distance) for i in range(count - dist...  4.66 us
    ppermute x2, waiting for transfers between devices, shifted(): lax.ppermute(array, 'seq', [(i, i + distance) for i in range(count - dist...  4.48 us
    pallas_call x1, Pallas kernels, on_device(): pl.pallas_call(channels_kernel, out_shape=[others, others, jax.ShapeDtype...  1.96 us
    pallas_call x1, Pallas kernels, on_device(): pl.pallas_call(intra_kernel, out_shape=[jax.ShapeDtypeStruct((block, chan...  1.5 us
    pallas_call x1, Pallas kernels, on_device(): pl.pallas_call(lambda *refs: back_kernel(*refs, members=early), out_shape...  0.95 us
  transfers between devices with their start and end apart: 12, of which 7 were waited for; matrix products, arithmetic and copies ran while one was open for 0% of the time, Pallas kernels for 17%

profile of v9, /device:TPU:24, one launch (start us, length us, event | category | flops | bytes accessed | tf_op | source)
XLA Modules:
  0.0 35.1 jit_solution(4220399451050374928)
XLA Ops:
  0.0 0.0 collective-permute-start
  0.0 0.5 %collective-permute-start.1 = (f32[4,256]{1,0:T(4,128)}, f32[4,256]{1,0:T(4,128)S(1)}, u32[]{:S(2)}, u32[]{:S(2)}) collective-permute-start(f32[4,256]{1,0:T(4,128)} %own_taps_hbm.1), channel_id=1, source_target_pairs={{0,1},{1,0},{2,3},{3,2},{4,5},{5,4},{6,7},{7,6},{8,9},{9,8},{10,11... | collective-permute-start | bytes 12296 | tf_op jit(solution)/shard_map/ppermute | solution.py:542
  0.5 0.0 collective-permute-start.2
  0.5 2.0 %channels.1 = (bf16[256,768]{1,0:T(8,128)(2,1)S(1)}, bf16[256,768]{1,0:T(8,128)(2,1)S(1)}, f32[24,768]{1,0:T(8,128)S(1)}, f32[16,128]{1,0:T(8,128)S(1)}, f32[16,...) custom-call(bf16[256,1024]{1,0:T(8,128)(2,1)} %x_hbm.1, ...), custom_call_target="tpu_custom_call" | custom-call | tf_op jit(solution)/shard_map/channels/pallas_call | solution.py:550
  2.5 0.0 collective-permute-done.2
  2.5 0.0 collective-permute-done.other
  2.5 0.6 %states.1 = (bf16[272,256]{1,0:T(8,128)(2,1)S(1)}, bf16[272,256]{1,0:T(8,128)(2,1)S(1)}, bf16[272,256]{1,0:T(8,128)(2,1)S(1)}, bf16[256,256]{1,0:T(8,128)(2,1)S(...) custom-call(bf16[256,1024]{1,0:T(8,128)(2,1)S(1)} %get-tuple-element, ...), custom_call_target="tpu_custom_call" | custom-call | tf_op jit(solution)/shard_map/states/pallas_call | solution.py:590
  3.2 2.5 %collective-permute-start.3 = (bf16[272,256]{1,0:T(8,128)(2,1)S(1)}, bf16[272,256]{1,0:T(8,128)(2,1)S(1)}, u32[]{:S(2)}, u32[]{:S(2)}) collective-permute-start(bf16[272,256]{1,0:T(8,128)(2,1)S(1)} %get-tuple-element.61), channel_id=1, source_target_pairs={{0,6},{2,4},{4,2},{6,0},{8,14},{10,12},{12,10},{14,8},{16,22},{18,... | collective-permute-start | bytes 417800 | tf_op jit(solution)/shard_map/ppermute | solution.py:499
  5.7 0.5 %collective-permute-start.4 = (bf16[272,256]{1,0:T(8,128)(2,1)S(1)}, bf16[272,256]{1,0:T(8,128)(2,1)S(1)}, u32[]{:S(2)}, u32[]{:S(2)}) collective-permute-start(bf16[272,256]{1,0:T(8,128)(2,1)S(1)} %get-tuple-element.62), channel_id=1, source_target_pairs={{0,2},{2,0},{4,6},{6,4},{8,10},{10,8},{12,14},{14,12},{16,18},{18,... | collective-permute-start | bytes 417800 | tf_op jit(solution)/shard_map/ppermute | solution.py:499
  6.2 0.5 %collective-permute-start.5 = (bf16[272,256]{1,0:T(8,128)(2,1)S(1)}, bf16[272,256]{1,0:T(8,128)(2,1)S(1)}, u32[]{:S(2)}, u32[]{:S(2)}) collective-permute-start(bf16[272,256]{1,0:T(8,128)(2,1)S(1)} %get-tuple-element.63), channel_id=1, source_target_pairs={{0,4},{2,6},{4,0},{6,2},{8,12},{10,14},{12,8},{14,10},{16,20},{18,... | collective-permute-start | bytes 417800 | tf_op jit(solution)/shard_map/ppermute | solution.py:499
  6.7 3.4 %collective-permute-start.6 = (bf16[16,512]{1,0:T(8,128)(2,1)S(1)}, bf16[16,512]{1,0:T(8,128)(2,1)S(1)}, u32[]{:S(2)}, u32[]{:S(2)}) collective-permute-start(bf16[16,512]{1,0:T(8,128)(2,1)S(1)} %get-tuple-element.66), channel_id=1, source_target_pairs={{0,2},{2,4},{4,6},{6,8},{8,10},{10,12},{12,14},{14,16},{16,18},{18... | collective-permute-start | bytes 49160 | tf_op jit(solution)/shard_map/ppermute | solution.py:509
  10.1 0.6 %rest.1 = (bf16[272,256]{1,0:T(8,128)(2,1)S(1)}, bf16[256,256]{1,0:T(8,128)(2,1)S(1)}, f32[24,256]{1,0:T(8,128)S(1)}) custom-call(bf16[256,1024]{1,0:T(8,128)(2,1)S(1)} %get-tuple-element.44.x, f32[4,1024]{1,0:T(4,128)S(1)} %get-tuple-element.45.taps.refs_5_.x_taps, f32[1,1024]{1,0:T(1,128)S(1)} %get-tuple-element.46.bias.refs_6_.x_bias, ...), custom_call_target="tpu_custom_call" | custom-call | flops 400000000 | bytes 2000000 | tf_op jit(solution)/shard_map/rest/pallas_call | solution.py:609
  10.7 0.0 collective-permute-done.3.refs_0_.r3
  10.7 2.8 %collective-permute-done.4.refs_1_.r1 = bf16[272,256]{1,0:T(8,128)(2,1)S(1)} collective-permute-done((bf16[272,256]{1,0:T(8,128)(2,1)S(1)}, bf16[272,256]{1,0:T(8,128)(2,1)S(1)}, u32[]{:S(2)}, u32[]{:S(2)}) %collective-permute-start.4) | collective-permute-done | bytes 139296 | tf_op jit(solution)/shard_map/ppermute | solution.py:499
  13.5 0.0 collective-permute-done.5.refs_2_.r2
  13.5 0.4 %group.1 = bf16[272,256]{1,0:T(8,128)(2,1)S(1)} custom-call(bf16[272,256]{1,0:T(8,128)(2,1)S(1)} %collective-permute-done.3.refs_0_.r3, bf16[272,256]{1,0:T(8,128)(2,1)S(1)} %collective-permute-done.4.refs_1_.r1, bf16[272,256]{1,0:T(8,128)(2,1)S(1)} %collective-permute-done.5.refs_2_.r2, bf16[272,256]{1,0:T(8,128)(2,1)S(1)} %get-tuple-element.64.refs_3_.r0, ...), custom_call_target="tpu_custom_call" | custom-call | tf_op jit(solution)/shard_map/group/pallas_call | solution.py:633
  13.9 0.2 collective-permute-done.6.halo
  14.1 0.1 collective-permute-start.8
  14.2 1.3 %collective-permute-start.7 = (bf16[272,256]{1,0:T(8,128)(2,1)S(1)}, bf16[272,256]{1,0:T(8,128)(2,1)S(1)}, u32[]{:S(2)}, u32[]{:S(2)}) collective-permute-start(bf16[272,256]{1,0:T(8,128)(2,1)S(1)} %group.1), channel_id=1, source_target_pairs={{0,16},{2,18},{4,20},{6,22},{8,24},{10,26},{12,28},{14,30},{1,17},... | collective-permute-start | bytes 417800 | tf_op jit(solution)/shard_map/ppermute | solution.py:509
  15.5 5.1 %collective-permute-done.8.near = bf16[272,256]{1,0:T(8,128)(2,1)S(1)} collective-permute-done((bf16[272,256]{1,0:T(8,128)(2,1)S(1)}, bf16[272,256]{1,0:T(8,128)(2,1)S(1)}, u32[]{:S(2)}, u32[]{:S(2)}) %collective-permute-start.8) | collective-permute-done | bytes 139296 | tf_op jit(solution)/shard_map/ppermute | solution.py:504
  20.6 0.5 %before.1 = (f32[4,256,256]{2,1,0:T(8,128)S(1)}, f32[8,256]{1,0:T(8,128)S(1)}) custom-call(bf16[272,256]{1,0:T(8,128)(2,1)S(1)} %collective-permute-done.3.refs_0_.r3, bf16[272,256]{1,0:T(8,128)(2,1)S(1)} %collective-permute-done.4.refs_1_.r1, bf16[272,256]{1,0:T(8,128)(2,1)S(1)} %collective-permute-done.5.refs_2_.r2, ...), custom_call_target="tpu_custom_call" | custom-call | flops 100000000 | bytes 2000000 | tf_op jit(solution)/shard_map/before/pallas_call | solution.py:648
  21.1 4.3 %collective-permute-done.7.far = bf16[272,256]{1,0:T(8,128)(2,1)S(1)} collective-permute-done((bf16[272,256]{1,0:T(8,128)(2,1)S(1)}, bf16[272,256]{1,0:T(8,128)(2,1)S(1)}, u32[]{:S(2)}, u32[]{:S(2)}) %collective-permute-start.7) | collective-permute-done | bytes 139296 | tf_op jit(solution)/shard_map/ppermute | solution.py:509
  25.3 0.4 %entering.1 = (bf16[256,256]{1,0:T(8,128)(2,1)S(1)}, bf16[256,256]{1,0:T(8,128)(2,1)S(1)}, bf16[256,256]{1,0:T(8,128)(2,1)S(1)}, bf16[256,256]{1,0:T(8,128)(2,1)S(1)}) custom-call(bf16[272,256]{1,0:T(8,128)(2,1)S(1)} %collective-permute-done.7.far, bf16[272,256]{1,0:T(8,128)(2,1)S(1)} %collective-permute-done.8.near, ...), custom_call_target="tpu_custom_call" | custom-call | tf_op jit(solution)/shard_map/entering/pallas_call | solution.py:660
  25.8 2.3 %collective-permute-start.11 = (bf16[256,256]{1,0:T(8,128)(2,1)S(1)}, bf16[256,256]{1,0:T(8,128)(2,1)S(1)}, u32[]{:S(2)}, u32[]{:S(2)}) collective-permute-start(bf16[256,256]{1,0:T(8,128)(2,1)S(1)} %get-tuple-element.80), channel_id=1, source_target_pairs={{0,6},{2,4},{4,2},{6,0},{8,14},{10,12},{12,10},{14,8},{16,22},{18,... | collective-permute-start | bytes 393224 | tf_op jit(solution)/shard_map/ppermute | solution.py:499
  28.1 0.7 %collective-permute-start.9 = (bf16[256,256]{1,0:T(8,128)(2,1)S(1)}, bf16[256,256]{1,0:T(8,128)(2,1)S(1)}, u32[]{:S(2)}, u32[]{:S(2)}) collective-permute-start(bf16[256,256]{1,0:T(8,128)(2,1)S(1)} %get-tuple-element.75), channel_id=1, source_target_pairs={{0,2},{2,0},{4,6},{6,4},{8,10},{10,8},{12,14},{14,12},{16,18},{18,... | collective-permute-start | bytes 393224 | tf_op jit(solution)/shard_map/ppermute | solution.py:499
  28.8 0.5 %collective-permute-start.10 = (bf16[256,256]{1,0:T(8,128)(2,1)S(1)}, bf16[256,256]{1,0:T(8,128)(2,1)S(1)}, u32[]{:S(2)}, u32[]{:S(2)}) collective-permute-start(bf16[256,256]{1,0:T(8,128)(2,1)S(1)} %get-tuple-element.76), channel_id=1, source_target_pairs={{0,4},{2,6},{4,0},{6,2},{8,12},{10,14},{12,8},{14,10},{16,20},{18,... | collective-permute-start | bytes 393224 | tf_op jit(solution)/shard_map/ppermute | solution.py:499
  29.3 1.5 %intra.1 = (f32[256,1024]{1,0:T(8,128)S(1)}, bf16[256,256]{1,0:T(8,128)(2,1)S(1)}, f32[256,1024]{1,0:T(8,128)S(1)}) custom-call(bf16[256,768]{1,0:T(8,128)(2,1)S(1)} %get-tuple-element.43.x_early, bf16[256,256]{1,0:T(8,128)(2,1)S(1)} %get-tuple-element.59.x_late, f32[24,768]{1,0:T(8,128)S(1)} %get-tuple-element.56.aux.aux_early, ...), custom_call_target="tpu_custom_call" | custom-call | flops 600000000 | bytes 4000000 | tf_op jit(solution)/shard_map/intra/pallas_call | solution.py:670
  30.8 1.8 %collective-permute-done.11.refs_2_ = bf16[256,256]{1,0:T(8,128)(2,1)S(1)} collective-permute-done((bf16[256,256]{1,0:T(8,128)(2,1)S(1)}, bf16[256,256]{1,0:T(8,128)(2,1)S(1)}, u32[]{:S(2)}, u32[]{:S(2)}) %collective-permute-start.11) | collective-permute-done | bytes 131104 | tf_op jit(solution)/shard_map/ppermute | solution.py:499
  32.6 1.0 %begin.1.begun = bf16[256,1024]{1,0:T(8,128)(2,1)} custom-call(bf16[256,256]{1,0:T(8,128)(2,1)S(1)} %get-tuple-element.71.refs_0_.c, bf16[256,256]{1,0:T(8,128)(2,1)S(1)} %get-tuple-element.79.refs_1_, bf16[256,256]{1,0:T(8,128)(2,1)S(1)} %collective-permute-done.11.refs_2_, f32[256,1024]{1,0:T(8,128)S(1)} %get-tuple-element.77.refs_3_.intra, ...), custom_call_target="tpu_custom_call" | custom-call | tf_op jit(solution)/shard_map/begin/pallas_call | solution.py:696
  33.6 0.5 %collective-permute-done.9.f1 = bf16[256,256]{1,0:T(8,128)(2,1)S(1)} collective-permute-done((bf16[256,256]{1,0:T(8,128)(2,1)S(1)}, bf16[256,256]{1,0:T(8,128)(2,1)S(1)}, u32[]{:S(2)}, u32[]{:S(2)}) %collective-permute-start.9) | collective-permute-done | bytes 131104 | tf_op jit(solution)/shard_map/ppermute | solution.py:499
  34.1 0.1 collective-permute-done.10.f2
  34.1 0.9 %back.1 = bf16[256,1024]{1,0:T(8,128)(2,1)} custom-call(bf16[256,256]{1,0:T(8,128)(2,1)S(1)} %get-tuple-element.71.refs_0_.c, bf16[256,256]{1,0:T(8,128)(2,1)S(1)} %collective-permute-done.9.f1, bf16[256,256]{1,0:T(8,128)(2,1)S(1)} %collective-permute-done.10.f2, f32[256,1024]{1,0:T(8,128)S(1)} %get-tuple-element.77.refs_3_.intra, ...), custom_call_target="tpu_custom_call", output_to_operand_aliasing={{}: (5, {})} | custom-call | tf_op jit(solution)/shard_map/back/pallas_call | solution.py:709
  (2 shorter events, 0.0 us)
Async XLA Ops:
  0.0 2.5 %collective-permute-start = (bf16[256,256]{1,0:T(8,128)(2,1)}, bf16[256,256]{1,0:T(8,128)(2,1)S(1)}, u32[]{:S(2)}, u32[]{:S(2)}) collective-permute-start(bf16[256,256]{1,0:T(8,128)(2,1)} %own_hbm.1), channel_id=1, source_target_pairs={{0,1},{1,0},{2,3},{3,2},{4,5},{5,4},{6,7},{7,6},{8,9},{9,8},{10,11... | collective-permute-start | bytes 393224 | tf_op jit(solution)/shard_map/ppermute | solution.py:542
  0.0 2.5 %collective-permute-start.1 = (f32[4,256]{1,0:T(4,128)}, f32[4,256]{1,0:T(4,128)S(1)}, u32[]{:S(2)}, u32[]{:S(2)}) collective-permute-start(f32[4,256]{1,0:T(4,128)} %own_taps_hbm.1), channel_id=1, source_target_pairs={{0,1},{1,0},{2,3},{3,2},{4,5},{5,4},{6,7},{7,6},{8,9},{9,8},{10,11... | collective-permute-start | bytes 12296 | tf_op jit(solution)/shard_map/ppermute | solution.py:542
  0.5 2.0 %collective-permute-start.2 = (f32[256]{0:T(256)}, f32[256]{0:T(256)S(1)}, u32[]{:S(2)}, u32[]{:S(2)}) collective-permute-start(f32[256]{0:T(256)} %param.16), channel_id=1, source_target_pairs={{0,1},{1,0},{2,3},{3,2},{4,5},{5,4},{6,7},{7,6},{8,9},{9,8},{10,11... | collective-permute-start | bytes 3080 | tf_op jit(solution)/shard_map/ppermute | solution.py:542
  3.2 7.5 %collective-permute-start.3 = (bf16[272,256]{1,0:T(8,128)(2,1)S(1)}, bf16[272,256]{1,0:T(8,128)(2,1)S(1)}, u32[]{:S(2)}, u32[]{:S(2)}) collective-permute-start(bf16[272,256]{1,0:T(8,128)(2,1)S(1)} %get-tuple-element.61), channel_id=1, source_target_pairs={{0,6},{2,4},{4,2},{6,0},{8,14},{10,12},{12,10},{14,8},{16,22},{18,... | collective-permute-start | bytes 417800 | tf_op jit(solution)/shard_map/ppermute | solution.py:499
  5.7 7.8 %collective-permute-start.4 = (bf16[272,256]{1,0:T(8,128)(2,1)S(1)}, bf16[272,256]{1,0:T(8,128)(2,1)S(1)}, u32[]{:S(2)}, u32[]{:S(2)}) collective-permute-start(bf16[272,256]{1,0:T(8,128)(2,1)S(1)} %get-tuple-element.62), channel_id=1, source_target_pairs={{0,2},{2,0},{4,6},{6,4},{8,10},{10,8},{12,14},{14,12},{16,18},{18,... | collective-permute-start | bytes 417800 | tf_op jit(solution)/shard_map/ppermute | solution.py:499
  6.2 7.3 %collective-permute-start.5 = (bf16[272,256]{1,0:T(8,128)(2,1)S(1)}, bf16[272,256]{1,0:T(8,128)(2,1)S(1)}, u32[]{:S(2)}, u32[]{:S(2)}) collective-permute-start(bf16[272,256]{1,0:T(8,128)(2,1)S(1)} %get-tuple-element.63), channel_id=1, source_target_pairs={{0,4},{2,6},{4,0},{6,2},{8,12},{10,14},{12,8},{14,10},{16,20},{18,... | collective-permute-start | bytes 417800 | tf_op jit(solution)/shard_map/ppermute | solution.py:499
  6.7 7.4 %collective-permute-start.6 = (bf16[16,512]{1,0:T(8,128)(2,1)S(1)}, bf16[16,512]{1,0:T(8,128)(2,1)S(1)}, u32[]{:S(2)}, u32[]{:S(2)}) collective-permute-start(bf16[16,512]{1,0:T(8,128)(2,1)S(1)} %get-tuple-element.66), channel_id=1, source_target_pairs={{0,2},{2,4},{4,6},{6,8},{8,10},{10,12},{12,14},{14,16},{16,18},{18... | collective-permute-start | bytes 49160 | tf_op jit(solution)/shard_map/ppermute | solution.py:509
  14.1 6.5 %collective-permute-start.8 = (bf16[272,256]{1,0:T(8,128)(2,1)S(1)}, bf16[272,256]{1,0:T(8,128)(2,1)S(1)}, u32[]{:S(2)}, u32[]{:S(2)}) collective-permute-start(bf16[272,256]{1,0:T(8,128)(2,1)S(1)} %group.1), channel_id=1, source_target_pairs={{0,8},{2,10},{4,12},{6,14},{8,16},{10,18},{12,20},{14,22},{16,24},... | collective-permute-start | bytes 417800 | tf_op jit(solution)/shard_map/ppermute | solution.py:504
  14.2 11.2 %collective-permute-start.7 = (bf16[272,256]{1,0:T(8,128)(2,1)S(1)}, bf16[272,256]{1,0:T(8,128)(2,1)S(1)}, u32[]{:S(2)}, u32[]{:S(2)}) collective-permute-start(bf16[272,256]{1,0:T(8,128)(2,1)S(1)} %group.1), channel_id=1, source_target_pairs={{0,16},{2,18},{4,20},{6,22},{8,24},{10,26},{12,28},{14,30},{1,17},... | collective-permute-start | bytes 417800 | tf_op jit(solution)/shard_map/ppermute | solution.py:509
  25.8 6.8 %collective-permute-start.11 = (bf16[256,256]{1,0:T(8,128)(2,1)S(1)}, bf16[256,256]{1,0:T(8,128)(2,1)S(1)}, u32[]{:S(2)}, u32[]{:S(2)}) collective-permute-start(bf16[256,256]{1,0:T(8,128)(2,1)S(1)} %get-tuple-element.80), channel_id=1, source_target_pairs={{0,6},{2,4},{4,2},{6,0},{8,14},{10,12},{12,10},{14,8},{16,22},{18,... | collective-permute-start | bytes 393224 | tf_op jit(solution)/shard_map/ppermute | solution.py:499
  28.1 5.9 %collective-permute-start.9 = (bf16[256,256]{1,0:T(8,128)(2,1)S(1)}, bf16[256,256]{1,0:T(8,128)(2,1)S(1)}, u32[]{:S(2)}, u32[]{:S(2)}) collective-permute-start(bf16[256,256]{1,0:T(8,128)(2,1)S(1)} %get-tuple-element.75), channel_id=1, source_target_pairs={{0,2},{2,0},{4,6},{6,4},{8,10},{10,8},{12,14},{14,12},{16,18},{18,... | collective-permute-start | bytes 393224 | tf_op jit(solution)/shard_map/ppermute | solution.py:499
  28.8 5.3 %collective-permute-start.10 = (bf16[256,256]{1,0:T(8,128)(2,1)S(1)}, bf16[256,256]{1,0:T(8,128)(2,1)S(1)}, u32[]{:S(2)}, u32[]{:S(2)}) collective-permute-start(bf16[256,256]{1,0:T(8,128)(2,1)S(1)} %get-tuple-element.76), channel_id=1, source_target_pairs={{0,4},{2,6},{4,0},{6,2},{8,12},{10,14},{12,8},{14,10},{16,20},{18,... | collective-permute-start | bytes 393224 | tf_op jit(solution)/shard_map/ppermute | solution.py:499

commit v10 on v9

--- a/solution.py
+++ b/solution.py
@@ -692,7 +692,7 @@
         b_main, b_aux, x_taps, time_step, rate_sum, offset, lags,
     )
     out_shape = jax.ShapeDtypeStruct((block, channels), BF16)
-    early, late = (0, 3), (1, 2)
+    early, late = (0, 3), (2, 1)
     begun = pl.pallas_call(
         lambda *refs: back_kernel(*refs, members=early),
         out_shape=out_shape,

time: 35.3 us -> 35.2 us (level)
  no operation moved by 1% of the time
where the time goes in v10:
time: 35.2 us; the launch traced here: 35.1 us
  waiting for transfers between devices  14.7 us (42%)
  starting transfers between devices  12.3 us (35%)
  Pallas kernels  7.89 us (22%)
    ppermute x6, starting transfers between devices, exchange(): lax.ppermute(array, 'seq', [(i, i ^ mask) for i in range(lax.axis_size('s...  7.11 us
    ppermute x1, waiting for transfers between devices, turned_on(): lax.ppermute(array, 'seq', [(i, (i + distance) % count) for i in range(co...  5.13 us
    ppermute x6, waiting for transfers between devices, exchange(): lax.ppermute(array, 'seq', [(i, i ^ mask) for i in range(lax.axis_size('s...  5.09 us
    ppermute x2, starting transfers between devices, shifted(): lax.ppermute(array, 'seq', [(i, i + distance) for i in range(count - dist...  4.66 us
    ppermute x2, waiting for transfers between devices, shifted(): lax.ppermute(array, 'seq', [(i, i + distance) for i in range(count - dist...  4.48 us
    pallas_call x1, Pallas kernels, on_device(): pl.pallas_call(channels_kernel, out_shape=[others, others, jax.ShapeDtype...  1.96 us
    pallas_call x1, Pallas kernels, on_device(): pl.pallas_call(intra_kernel, out_shape=[jax.ShapeDtypeStruct((block, chan...  1.5 us
    pallas_call x1, Pallas kernels, on_device(): pl.pallas_call(lambda *refs: back_kernel(*refs, members=early), out_shape...  0.95 us
  transfers between devices with their start and end apart: 12, of which 7 were waited for; matrix products, arithmetic and copies ran while one was open for 0% of the time, Pallas kernels for 17%

profile of v10, /device:TPU:24, one launch (start us, length us, event | category | flops | bytes accessed | tf_op | source)
XLA Modules:
  0.0 35.1 jit_solution(6905452525281241372)
XLA Ops:
  0.0 0.0 collective-permute-start
  0.0 0.5 %collective-permute-start.1 = (f32[4,256]{1,0:T(4,128)}, f32[4,256]{1,0:T(4,128)S(1)}, u32[]{:S(2)}, u32[]{:S(2)}) collective-permute-start(f32[4,256]{1,0:T(4,128)} %own_taps_hbm.1), channel_id=1, source_target_pairs={{0,1},{1,0},{2,3},{3,2},{4,5},{5,4},{6,7},{7,6},{8,9},{9,8},{10,11... | collective-permute-start | bytes 12296 | tf_op jit(solution)/shard_map/ppermute | solution.py:542
  0.5 0.0 collective-permute-start.2
  0.5 2.0 %channels.1 = (bf16[256,768]{1,0:T(8,128)(2,1)S(1)}, bf16[256,768]{1,0:T(8,128)(2,1)S(1)}, f32[24,768]{1,0:T(8,128)S(1)}, f32[16,128]{1,0:T(8,128)S(1)}, f32[16,...) custom-call(bf16[256,1024]{1,0:T(8,128)(2,1)} %x_hbm.1, ...), custom_call_target="tpu_custom_call" | custom-call | tf_op jit(solution)/shard_map/channels/pallas_call | solution.py:550
  2.5 0.0 collective-permute-done.2
  2.5 0.0 collective-permute-done.1.other_taps
  2.5 0.0 collective-permute-done.other
  2.5 0.6 %states.1 = (bf16[272,256]{1,0:T(8,128)(2,1)S(1)}, bf16[272,256]{1,0:T(8,128)(2,1)S(1)}, bf16[272,256]{1,0:T(8,128)(2,1)S(1)}, bf16[256,256]{1,0:T(8,128)(2,1)S(...) custom-call(bf16[256,1024]{1,0:T(8,128)(2,1)S(1)} %get-tuple-element, ...), custom_call_target="tpu_custom_call" | custom-call | tf_op jit(solution)/shard_map/states/pallas_call | solution.py:590
  3.2 2.5 %collective-permute-start.3 = (bf16[272,256]{1,0:T(8,128)(2,1)S(1)}, bf16[272,256]{1,0:T(8,128)(2,1)S(1)}, u32[]{:S(2)}, u32[]{:S(2)}) collective-permute-start(bf16[272,256]{1,0:T(8,128)(2,1)S(1)} %get-tuple-element.61), channel_id=1, source_target_pairs={{0,6},{2,4},{4,2},{6,0},{8,14},{10,12},{12,10},{14,8},{16,22},{18,... | collective-permute-start | bytes 417800 | tf_op jit(solution)/shard_map/ppermute | solution.py:499
  5.7 0.5 %collective-permute-start.4 = (bf16[272,256]{1,0:T(8,128)(2,1)S(1)}, bf16[272,256]{1,0:T(8,128)(2,1)S(1)}, u32[]{:S(2)}, u32[]{:S(2)}) collective-permute-start(bf16[272,256]{1,0:T(8,128)(2,1)S(1)} %get-tuple-element.62), channel_id=1, source_target_pairs={{0,2},{2,0},{4,6},{6,4},{8,10},{10,8},{12,14},{14,12},{16,18},{18,... | collective-permute-start | bytes 417800 | tf_op jit(solution)/shard_map/ppermute | solution.py:499
  6.2 0.5 %collective-permute-start.5 = (bf16[272,256]{1,0:T(8,128)(2,1)S(1)}, bf16[272,256]{1,0:T(8,128)(2,1)S(1)}, u32[]{:S(2)}, u32[]{:S(2)}) collective-permute-start(bf16[272,256]{1,0:T(8,128)(2,1)S(1)} %get-tuple-element.63), channel_id=1, source_target_pairs={{0,4},{2,6},{4,0},{6,2},{8,12},{10,14},{12,8},{14,10},{16,20},{18,... | collective-permute-start | bytes 417800 | tf_op jit(solution)/shard_map/ppermute | solution.py:499
  6.7 3.4 %collective-permute-start.6 = (bf16[16,512]{1,0:T(8,128)(2,1)S(1)}, bf16[16,512]{1,0:T(8,128)(2,1)S(1)}, u32[]{:S(2)}, u32[]{:S(2)}) collective-permute-start(bf16[16,512]{1,0:T(8,128)(2,1)S(1)} %get-tuple-element.66), channel_id=1, source_target_pairs={{0,2},{2,4},{4,6},{6,8},{8,10},{10,12},{12,14},{14,16},{16,18},{18... | collective-permute-start | bytes 49160 | tf_op jit(solution)/shard_map/ppermute | solution.py:509
  10.1 0.6 %rest.1 = (bf16[272,256]{1,0:T(8,128)(2,1)S(1)}, bf16[256,256]{1,0:T(8,128)(2,1)S(1)}, f32[24,256]{1,0:T(8,128)S(1)}) custom-call(bf16[256,1024]{1,0:T(8,128)(2,1)S(1)} %get-tuple-element.44.x, f32[4,1024]{1,0:T(4,128)S(1)} %get-tuple-element.45.taps.refs_5_.x_taps, f32[1,1024]{1,0:T(1,128)S(1)} %get-tuple-element.46.bias.refs_6_.x_bias, ...), custom_call_target="tpu_custom_call" | custom-call | flops 400000000 | bytes 2000000 | tf_op jit(solution)/shard_map/rest/pallas_call | solution.py:609
  10.7 2.8 %collective-permute-done.4.refs_1_.r1 = bf16[272,256]{1,0:T(8,128)(2,1)S(1)} collective-permute-done((bf16[272,256]{1,0:T(8,128)(2,1)S(1)}, bf16[272,256]{1,0:T(8,128)(2,1)S(1)}, u32[]{:S(2)}, u32[]{:S(2)}) %collective-permute-start.4) | collective-permute-done | bytes 139296 | tf_op jit(solution)/shard_map/ppermute | solution.py:499
  13.5 0.0 collective-permute-done.5.refs_2_.r2
  13.5 0.4 %group.1 = bf16[272,256]{1,0:T(8,128)(2,1)S(1)} custom-call(bf16[272,256]{1,0:T(8,128)(2,1)S(1)} %collective-permute-done.3.refs_0_.r3, bf16[272,256]{1,0:T(8,128)(2,1)S(1)} %collective-permute-done.4.refs_1_.r1, bf16[272,256]{1,0:T(8,128)(2,1)S(1)} %collective-permute-done.5.refs_2_.r2, bf16[272,256]{1,0:T(8,128)(2,1)S(1)} %get-tuple-element.64.refs_3_.r0, ...), custom_call_target="tpu_custom_call" | custom-call | tf_op jit(solution)/shard_map/group/pallas_call | solution.py:633
  13.9 0.2 collective-permute-done.6.halo
  14.1 0.1 collective-permute-start.8
  14.2 1.3 %collective-permute-start.7 = (bf16[272,256]{1,0:T(8,128)(2,1)S(1)}, bf16[272,256]{1,0:T(8,128)(2,1)S(1)}, u32[]{:S(2)}, u32[]{:S(2)}) collective-permute-start(bf16[272,256]{1,0:T(8,128)(2,1)S(1)} %group.1), channel_id=1, source_target_pairs={{0,16},{2,18},{4,20},{6,22},{8,24},{10,26},{12,28},{14,30},{1,17},... | collective-permute-start | bytes 417800 | tf_op jit(solution)/shard_map/ppermute | solution.py:509
  15.5 5.1 %collective-permute-done.8.near = bf16[272,256]{1,0:T(8,128)(2,1)S(1)} collective-permute-done((bf16[272,256]{1,0:T(8,128)(2,1)S(1)}, bf16[272,256]{1,0:T(8,128)(2,1)S(1)}, u32[]{:S(2)}, u32[]{:S(2)}) %collective-permute-start.8) | collective-permute-done | bytes 139296 | tf_op jit(solution)/shard_map/ppermute | solution.py:504
  20.6 0.5 %before.1 = (f32[4,256,256]{2,1,0:T(8,128)S(1)}, f32[8,256]{1,0:T(8,128)S(1)}) custom-call(bf16[272,256]{1,0:T(8,128)(2,1)S(1)} %collective-permute-done.3.refs_0_.r3, bf16[272,256]{1,0:T(8,128)(2,1)S(1)} %collective-permute-done.4.refs_1_.r1, bf16[272,256]{1,0:T(8,128)(2,1)S(1)} %collective-permute-done.5.refs_2_.r2, ...), custom_call_target="tpu_custom_call" | custom-call | flops 100000000 | bytes 2000000 | tf_op jit(solution)/shard_map/before/pallas_call | solution.py:648
  21.1 4.3 %collective-permute-done.7.far = bf16[272,256]{1,0:T(8,128)(2,1)S(1)} collective-permute-done((bf16[272,256]{1,0:T(8,128)(2,1)S(1)}, bf16[272,256]{1,0:T(8,128)(2,1)S(1)}, u32[]{:S(2)}, u32[]{:S(2)}) %collective-permute-start.7) | collective-permute-done | bytes 139296 | tf_op jit(solution)/shard_map/ppermute | solution.py:509
  25.3 0.4 %entering.1 = (bf16[256,256]{1,0:T(8,128)(2,1)S(1)}, bf16[256,256]{1,0:T(8,128)(2,1)S(1)}, bf16[256,256]{1,0:T(8,128)(2,1)S(1)}, bf16[256,256]{1,0:T(8,128)(2,1)S(1)}) custom-call(bf16[272,256]{1,0:T(8,128)(2,1)S(1)} %collective-permute-done.7.far, bf16[272,256]{1,0:T(8,128)(2,1)S(1)} %collective-permute-done.8.near, ...), custom_call_target="tpu_custom_call" | custom-call | tf_op jit(solution)/shard_map/entering/pallas_call | solution.py:660
  25.8 2.3 %collective-permute-start.11 = (bf16[256,256]{1,0:T(8,128)(2,1)S(1)}, bf16[256,256]{1,0:T(8,128)(2,1)S(1)}, u32[]{:S(2)}, u32[]{:S(2)}) collective-permute-start(bf16[256,256]{1,0:T(8,128)(2,1)S(1)} %get-tuple-element.80), channel_id=1, source_target_pairs={{0,6},{2,4},{4,2},{6,0},{8,14},{10,12},{12,10},{14,8},{16,22},{18,... | collective-permute-start | bytes 393224 | tf_op jit(solution)/shard_map/ppermute | solution.py:499
  28.1 0.5 %collective-permute-start.9 = (bf16[256,256]{1,0:T(8,128)(2,1)S(1)}, bf16[256,256]{1,0:T(8,128)(2,1)S(1)}, u32[]{:S(2)}, u32[]{:S(2)}) collective-permute-start(bf16[256,256]{1,0:T(8,128)(2,1)S(1)} %get-tuple-element.75), channel_id=1, source_target_pairs={{0,4},{2,6},{4,0},{6,2},{8,12},{10,14},{12,8},{14,10},{16,20},{18,... | collective-permute-start | bytes 393224 | tf_op jit(solution)/shard_map/ppermute | solution.py:499
  28.6 0.7 %collective-permute-start.10 = (bf16[256,256]{1,0:T(8,128)(2,1)S(1)}, bf16[256,256]{1,0:T(8,128)(2,1)S(1)}, u32[]{:S(2)}, u32[]{:S(2)}) collective-permute-start(bf16[256,256]{1,0:T(8,128)(2,1)S(1)} %get-tuple-element.76), channel_id=1, source_target_pairs={{0,2},{2,0},{4,6},{6,4},{8,10},{10,8},{12,14},{14,12},{16,18},{18,... | collective-permute-start | bytes 393224 | tf_op jit(solution)/shard_map/ppermute | solution.py:499
  29.3 1.5 %intra.1 = (f32[256,1024]{1,0:T(8,128)S(1)}, bf16[256,256]{1,0:T(8,128)(2,1)S(1)}, f32[256,1024]{1,0:T(8,128)S(1)}) custom-call(bf16[256,768]{1,0:T(8,128)(2,1)S(1)} %get-tuple-element.43.x_early, bf16[256,256]{1,0:T(8,128)(2,1)S(1)} %get-tuple-element.59.x_late, f32[24,768]{1,0:T(8,128)S(1)} %get-tuple-element.56.aux.aux_early, ...), custom_call_target="tpu_custom_call" | custom-call | flops 600000000 | bytes 4000000 | tf_op jit(solution)/shard_map/intra/pallas_call | solution.py:670
  30.8 2.0 %collective-permute-done.11.refs_2_ = bf16[256,256]{1,0:T(8,128)(2,1)S(1)} collective-permute-done((bf16[256,256]{1,0:T(8,128)(2,1)S(1)}, bf16[256,256]{1,0:T(8,128)(2,1)S(1)}, u32[]{:S(2)}, u32[]{:S(2)}) %collective-permute-start.11) | collective-permute-done | bytes 131104 | tf_op jit(solution)/shard_map/ppermute | solution.py:499
  32.9 0.9 %begin.1.begun = bf16[256,1024]{1,0:T(8,128)(2,1)} custom-call(bf16[256,256]{1,0:T(8,128)(2,1)S(1)} %get-tuple-element.71.refs_0_.c, bf16[256,256]{1,0:T(8,128)(2,1)S(1)} %get-tuple-element.79.refs_1_, bf16[256,256]{1,0:T(8,128)(2,1)S(1)} %collective-permute-done.11.refs_2_, f32[256,1024]{1,0:T(8,128)S(1)} %get-tuple-element.77.refs_3_.intra, ...), custom_call_target="tpu_custom_call" | custom-call | tf_op jit(solution)/shard_map/begin/pallas_call | solution.py:696
  33.8 0.1 collective-permute-done.9.f1
  33.9 0.2 collective-permute-done.10.f2
  34.1 0.9 %back.1 = bf16[256,1024]{1,0:T(8,128)(2,1)} custom-call(bf16[256,256]{1,0:T(8,128)(2,1)S(1)} %get-tuple-element.71.refs_0_.c, bf16[256,256]{1,0:T(8,128)(2,1)S(1)} %collective-permute-done.9.f1, bf16[256,256]{1,0:T(8,128)(2,1)S(1)} %collective-permute-done.10.f2, f32[256,1024]{1,0:T(8,128)S(1)} %get-tuple-element.77.refs_3_.intra, ...), custom_call_target="tpu_custom_call", output_to_operand_aliasing={{}: (5, {})} | custom-call | tf_op jit(solution)/shard_map/back/pallas_call | solution.py:709
  (2 shorter events, 0.0 us)
Async XLA Ops:
  0.0 2.5 %collective-permute-start = (bf16[256,256]{1,0:T(8,128)(2,1)}, bf16[256,256]{1,0:T(8,128)(2,1)S(1)}, u32[]{:S(2)}, u32[]{:S(2)}) collective-permute-start(bf16[256,256]{1,0:T(8,128)(2,1)} %own_hbm.1), channel_id=1, source_target_pairs={{0,1},{1,0},{2,3},{3,2},{4,5},{5,4},{6,7},{7,6},{8,9},{9,8},{10,11... | collective-permute-start | bytes 393224 | tf_op jit(solution)/shard_map/ppermute | solution.py:542
  0.0 2.5 %collective-permute-start.1 = (f32[4,256]{1,0:T(4,128)}, f32[4,256]{1,0:T(4,128)S(1)}, u32[]{:S(2)}, u32[]{:S(2)}) collective-permute-start(f32[4,256]{1,0:T(4,128)} %own_taps_hbm.1), channel_id=1, source_target_pairs={{0,1},{1,0},{2,3},{3,2},{4,5},{5,4},{6,7},{7,6},{8,9},{9,8},{10,11... | collective-permute-start | bytes 12296 | tf_op jit(solution)/shard_map/ppermute | solution.py:542
  0.5 2.0 %collective-permute-start.2 = (f32[256]{0:T(256)}, f32[256]{0:T(256)S(1)}, u32[]{:S(2)}, u32[]{:S(2)}) collective-permute-start(f32[256]{0:T(256)} %param.16), channel_id=1, source_target_pairs={{0,1},{1,0},{2,3},{3,2},{4,5},{5,4},{6,7},{7,6},{8,9},{9,8},{10,11... | collective-permute-start | bytes 3080 | tf_op jit(solution)/shard_map/ppermute | solution.py:542
  3.2 7.5 %collective-permute-start.3 = (bf16[272,256]{1,0:T(8,128)(2,1)S(1)}, bf16[272,256]{1,0:T(8,128)(2,1)S(1)}, u32[]{:S(2)}, u32[]{:S(2)}) collective-permute-start(bf16[272,256]{1,0:T(8,128)(2,1)S(1)} %get-tuple-element.61), channel_id=1, source_target_pairs={{0,6},{2,4},{4,2},{6,0},{8,14},{10,12},{12,10},{14,8},{16,22},{18,... | collective-permute-start | bytes 417800 | tf_op jit(solution)/shard_map/ppermute | solution.py:499
  5.7 7.8 %collective-permute-start.4 = (bf16[272,256]{1,0:T(8,128)(2,1)S(1)}, bf16[272,256]{1,0:T(8,128)(2,1)S(1)}, u32[]{:S(2)}, u32[]{:S(2)}) collective-permute-start(bf16[272,256]{1,0:T(8,128)(2,1)S(1)} %get-tuple-element.62), channel_id=1, source_target_pairs={{0,2},{2,0},{4,6},{6,4},{8,10},{10,8},{12,14},{14,12},{16,18},{18,... | collective-permute-start | bytes 417800 | tf_op jit(solution)/shard_map/ppermute | solution.py:499
  6.2 7.3 %collective-permute-start.5 = (bf16[272,256]{1,0:T(8,128)(2,1)S(1)}, bf16[272,256]{1,0:T(8,128)(2,1)S(1)}, u32[]{:S(2)}, u32[]{:S(2)}) collective-permute-start(bf16[272,256]{1,0:T(8,128)(2,1)S(1)} %get-tuple-element.63), channel_id=1, source_target_pairs={{0,4},{2,6},{4,0},{6,2},{8,12},{10,14},{12,8},{14,10},{16,20},{18,... | collective-permute-start | bytes 417800 | tf_op jit(solution)/shard_map/ppermute | solution.py:499
  6.7 7.4 %collective-permute-start.6 = (bf16[16,512]{1,0:T(8,128)(2,1)S(1)}, bf16[16,512]{1,0:T(8,128)(2,1)S(1)}, u32[]{:S(2)}, u32[]{:S(2)}) collective-permute-start(bf16[16,512]{1,0:T(8,128)(2,1)S(1)} %get-tuple-element.66), channel_id=1, source_target_pairs={{0,2},{2,4},{4,6},{6,8},{8,10},{10,12},{12,14},{14,16},{16,18},{18... | collective-permute-start | bytes 49160 | tf_op jit(solution)/shard_map/ppermute | solution.py:509
  14.1 6.5 %collective-permute-start.8 = (bf16[272,256]{1,0:T(8,128)(2,1)S(1)}, bf16[272,256]{1,0:T(8,128)(2,1)S(1)}, u32[]{:S(2)}, u32[]{:S(2)}) collective-permute-start(bf16[272,256]{1,0:T(8,128)(2,1)S(1)} %group.1), channel_id=1, source_target_pairs={{0,8},{2,10},{4,12},{6,14},{8,16},{10,18},{12,20},{14,22},{16,24},... | collective-permute-start | bytes 417800 | tf_op jit(solution)/shard_map/ppermute | solution.py:504
  14.2 11.2 %collective-permute-start.7 = (bf16[272,256]{1,0:T(8,128)(2,1)S(1)}, bf16[272,256]{1,0:T(8,128)(2,1)S(1)}, u32[]{:S(2)}, u32[]{:S(2)}) collective-permute-start(bf16[272,256]{1,0:T(8,128)(2,1)S(1)} %group.1), channel_id=1, source_target_pairs={{0,16},{2,18},{4,20},{6,22},{8,24},{10,26},{12,28},{14,30},{1,17},... | collective-permute-start | bytes 417800 | tf_op jit(solution)/shard_map/ppermute | solution.py:509
  25.8 7.1 %collective-permute-start.11 = (bf16[256,256]{1,0:T(8,128)(2,1)S(1)}, bf16[256,256]{1,0:T(8,128)(2,1)S(1)}, u32[]{:S(2)}, u32[]{:S(2)}) collective-permute-start(bf16[256,256]{1,0:T(8,128)(2,1)S(1)} %get-tuple-element.80), channel_id=1, source_target_pairs={{0,6},{2,4},{4,2},{6,0},{8,14},{10,12},{12,10},{14,8},{16,22},{18,... | collective-permute-start | bytes 393224 | tf_op jit(solution)/shard_map/ppermute | solution.py:499
  28.1 5.8 %collective-permute-start.9 = (bf16[256,256]{1,0:T(8,128)(2,1)S(1)}, bf16[256,256]{1,0:T(8,128)(2,1)S(1)}, u32[]{:S(2)}, u32[]{:S(2)}) collective-permute-start(bf16[256,256]{1,0:T(8,128)(2,1)S(1)} %get-tuple-element.75), channel_id=1, source_target_pairs={{0,4},{2,6},{4,0},{6,2},{8,12},{10,14},{12,8},{14,10},{16,20},{18,... | collective-permute-start | bytes 393224 | tf_op jit(solution)/shard_map/ppermute | solution.py:499
  28.6 5.5 %collective-permute-start.10 = (bf16[256,256]{1,0:T(8,128)(2,1)S(1)}, bf16[256,256]{1,0:T(8,128)(2,1)S(1)}, u32[]{:S(2)}, u32[]{:S(2)}) collective-permute-start(bf16[256,256]{1,0:T(8,128)(2,1)S(1)} %get-tuple-element.76), channel_id=1, source_target_pairs={{0,2},{2,0},{4,6},{6,4},{8,10},{10,8},{12,14},{14,12},{16,18},{18,... | collective-permute-start | bytes 393224 | tf_op jit(solution)/shard_map/ppermute | solution.py:499
